TPU v7x, 256 devices: a whole 4x4x8 slice. The times are simulated.
256 devices in a mesh: dp: 64 (over x, z, core), mp: 4 (over y).
Axes of the slice: x: 4, y: 4, z: 8, core: 2. Of those that a mesh axis runs over, the one named last changes fastest.
Arguments:
- activations: bfloat16 [32768, 2560], P('dp'), may hold values from -6 to 6
- cotangent: bfloat16 [32768, 6912], P('dp', 'mp'), may hold values from -6 to 6
- frozen_weight: bfloat16 [2560, 6912], P(None, 'mp'), may hold values from -0.078125 to 0.078125
- skew_params: bfloat16 [10, 256, 256], replicated, may hold values from -0.125 to 0.125
- tile_order: int32 [20], replicated, may hold values from 0 to 19, each once
- block_owner: int32 [10], replicated, may hold values from 0 to 63, as said below
Outputs:
- input_grad: bfloat16 [32768, 2560], P('dp', 'mp')
- skew_grads: float32 [192, 256, 256], P('dp')
Inputs may be any that keep to these rules, and one draw needn't show every extreme that they name: `tile_order`: a permutation of the 20 tiles. `block_owner`: no index of dp owns more than 3 blocks, and some index owns exactly 3; indices 0 and 64 - 1 own blocks in every draw.
All inputs are finite; a program needn't handle non-finite values.
Results may differ from a plain program's by a relative error of at most 0.001.
Values sent between devices are 32-bit elements; how exact they have to be, the bound alone decides.
No kernel may reach another device: no remote copies, remote signals or barrier semaphores. Data moves between devices by JAX's collectives and lax.ppermute only.
A program may use at most 128 MiB of HBM per device.

v0:
```python
import math

import jax
import jax.numpy as jnp
from jax import lax
from jax.sharding import PartitionSpec as P

SLOTS = 3


highest = lax.Precision.HIGHEST


def product(first, second):
    return jnp.einsum("bij,bjk->bik", first, second, precision=highest)


def cayley_parts(params):
    plain = params.astype(jnp.float32)
    skew = plain - jnp.swapaxes(plain, 1, 2)
    square = product(skew, skew)
    cube = product(square, skew)
    identity = jnp.eye(skew.shape[1], dtype=jnp.float32)
    return (skew, identity[None] + 2.0 * skew + 2.0 * square + cube)


def to_blocks(matrix, order, tile_count, block_count):
    tiled = matrix.reshape(matrix.shape[0], tile_count, -1)
    return jnp.take(tiled, order, axis=1).reshape(matrix.shape[0], block_count, -1)


def inverse_order(order, tile_count):
    positions = jnp.arange(tile_count, dtype=jnp.int32)
    matches = (order[:, None] == positions[None, :]).astype(jnp.int32)
    return jnp.sum(positions[:, None] * matches, axis=0)


def adjoint(gram, skew):
    transposed = jnp.swapaxes(skew, 1, 2)
    left = product(gram, transposed)
    right = product(transposed, gram)
    total = (
        2.0 * gram
        + 2.0 * (left + right)
        + product(left, transposed)
        + product(transposed, left)
        + product(transposed, right)
    )
    return total - jnp.swapaxes(total, 1, 2)


def local(activations, cotangent, frozen_weight, skew_params, tile_order, block_owner):
    token_rows = activations.shape[0]
    tile_count = tile_order.shape[0]
    block_count = block_owner.shape[0]
    skew, rotation = cayley_parts(skew_params)
    partial_grad = lax.dot_general(
        cotangent, frozen_weight, (((1,), (1,)), ((), ())), preferred_element_type=jnp.float32
    )
    feature_grad = lax.psum(partial_grad, "mp")
    grad_blocks = to_blocks(feature_grad, tile_order, tile_count, block_count)
    own_tiles = tile_count // lax.axis_size("mp")
    inverse = inverse_order(tile_order, tile_count)
    own_places = lax.dynamic_slice_in_dim(inverse, lax.axis_index("mp") * own_tiles, own_tiles, 0)
    half_rows = rotation.reshape(block_count * 2, rotation.shape[1] // 2, rotation.shape[2])
    own_rotation = jnp.take(half_rows, own_places, axis=0)
    own_blocks = jnp.take(grad_blocks, own_places // 2, axis=1)
    own_rotated = jnp.einsum("tkj,kij->tki", own_blocks, own_rotation, precision=highest)
    input_grad = own_rotated.reshape(token_rows, -1).astype(jnp.bfloat16)
    quarter = token_rows // lax.axis_size("mp")
    row_start = lax.axis_index("mp") * quarter
    some_inputs = lax.dynamic_slice_in_dim(activations, row_start, quarter, 0)
    input_blocks = to_blocks(some_inputs, tile_order, tile_count, block_count).astype(jnp.float32)
    some_grads = lax.dynamic_slice_in_dim(grad_blocks, row_start, quarter, 0)
    local_gram = jnp.einsum("tbi,tbj->bij", input_blocks, some_grads, precision=highest)
    gram = lax.psum(local_gram, ("dp", "mp"))
    owned = (block_owner == lax.axis_index("dp")).astype(jnp.int32)
    ranking = jnp.cumsum(owned) - 1
    slot_ids = jnp.arange(SLOTS, dtype=jnp.int32)
    selector = ((owned[None, :] == 1) & (ranking[None, :] == slot_ids[:, None])).astype(jnp.float32)
    gram_slots = jnp.einsum("sb,bij->sij", selector, gram, precision=highest)
    skew_slots = jnp.einsum("sb,bij->sij", selector, skew, precision=highest)
    scaling = 1.0 / math.sqrt(token_rows * lax.axis_size("dp"))
    skew_grads = adjoint(gram_slots, skew_slots) * scaling
    return (input_grad, skew_grads)


def solution(mesh):
    placed = (P("dp", None), P("dp", "mp"), P(None, "mp"), P(), P(), P())
    return jax.shard_map(
        local,
        mesh=mesh,
        in_specs=placed,
        out_specs=(P("dp", "mp"), P("dp", None, None)),
        check_vma=False,
    )
```

profile of v0, /device:TPU:32, one launch (start us, length us, event | category | flops | bytes accessed | tf_op | source)
XLA Modules:
  0.0 451.0 jit_solution(274264501818761207)
XLA Ops:
  7.2 0.0 copy-start
  7.2 0.0 all-reduce.3.cloned.1.call-start
  7.2 11.5 %fusion.34 = f32[512,2560]{0,1:T(8,128)} fusion(bf16[512,1728]{0,1:T(8,128)(2,1)} %param.7, bf16[2560,1728]{0,1:T(8,128)(2,1)} %param.8), kind=kOutput, calls=%fused_computation.62 | convolution fusion | flops 4529848320 | bytes 15859712 | tf_op jit(solution)/shard_map/dot_general | solution.py:57
  18.7 5.9 %copy.80 = f32[512,20,128]{2,0,1:T(8,128)} copy(f32[512,20,128]{0,2,1:T(8,128)} %bitcast.49) | data formatting | bytes 10485760 | tf_op jit(solution)/shard_map/reshape | solution.py:28
  24.6 0.0 copy-start.5
  24.6 0.0 copy-start.6
  24.6 0.0 all-reduce.3.cloned.1.call-update
  24.6 0.0 all-reduce.5.cloned.1.call-start
  24.7 0.6 copy-done.5
  25.3 0.2 reduce-window.8
  25.4 0.0 copy-done.6
  25.5 0.1 broadcast_in_dim.63
  25.5 0.1 broadcast_in_dim.64
  25.7 0.0 copy-done
  25.7 0.1 constant_dynamic-slice_fusion
  25.7 0.3 copy.100
  26.1 0.3 copy.84
  26.4 0.7 gather_fusion.3
  27.1 0.3 copy.85
  27.4 1.6 copy.77
  29.0 0.0 copy-start.4
  29.1 1.9 copy.78
  31.0 0.1 select_reduce_fusion
  31.1 0.1 compare_and_fusion.2
  31.2 0.0 copy-done.4
  31.2 0.5 bitcast_select_fusion
  31.7 2.4 bitcast_subtract_fusion
  34.1 3.9 fusion
  38.0 104.4 %all-reduce.3.cloned.1.call-done = f32[512,20,128]{2,0,1:T(8,128)} async-done(((f32[512,20,128]{2,0,1:T(8,128)}), f32[512,20,128]{2,0,1:T(8,128)}) %all-reduce.3.cloned.1.call-update) | async-done | bytes 5242896 | tf_op jit(solution)/shard_map/psum | solution.py:60
  142.4 5.7 %gather_fusion.1 = f32[20,512,128]{2,1,0:T(8,128)} fusion(f32[512,20,128]{2,0,1:T(8,128)} %all-reduce.3.cloned.1.call-done, s32[1024]{0:T(1024)S(1)} %pad_clamp_fusion.1), kind=kCustom, calls=%fused_computation.1 | custom fusion | bytes 10485840 | tf_op jit(solution)/shard_map/jit(_take)/gather | solution.py:29
  148.1 5.9 %copy.81 = f32[512,20,128]{0,2,1:T(8,128)} copy(f32[512,20,128]{2,0,1:T(8,128)} %bitcast.47) | data formatting | bytes 10485760 | tf_op jit(solution)/shard_map/jit(_take)/gather | solution.py:29
  154.0 5.9 %copy.82 = f32[512,10,256]{2,0,1:T(8,128)} copy(f32[512,10,256]{0,2,1:T(8,128)} %bitcast.48) | data formatting | bytes 10485760 | tf_op jit(solution)/shard_map/jit(_take)/gather | solution.py:29
  159.9 2.9 broadcast_select_fusion
  162.8 0.0 copy-start.2
  162.8 2.3 copy-done.2
  165.1 2.8 fusion.11
  167.9 0.0 all-reduce.5.cloned.1.call-update
  167.9 1.5 copy.90
  169.4 2.9 fusion.33
  172.3 4.8 %add_add_fusion = f32[10,256,256]{2,1,0:T(8,128)} fusion(f32[10,256,256]{2,1,0:T(8,128)S(1)} %fusion.33, f32[10,256,256]{2,1,0:T(8,128)S(1)} %bitcast_subtract_fusion, f32[256,256]{1,0:T(8,128)S(1)} %fusion.24), kind=kOutput, calls=%fused_computation.13 | convolution fusion | flops 2016542720 | bytes 8126464 | tf_op jit(solution)/shard_map/bij,bjk->bik/dot_general | solution.py:15
  177.1 3.2 gather_fusion
  180.3 3.2 gather_fusion.2
  183.5 4.7 %fusion.7 = bf16[5,128,512]{2,1,0:T(8,128)(2,1)} fusion(f32[5,512,256]{2,1,0:T(8,128)S(1)} %gather_fusion.2, pred[5]{0:T(512)(128)(4,1)S(1)} %get-tuple-element.16, f32[5,128,256]{2,1,0:T(8,128)} %gather_fusion, pred[5]{0:T(512)(128)(4,1)S(1)} %get-tuple-element.10), kind=kOutput, calls=%fused_computation.14 | convolution fusion | flops 1007779840 | bytes 3932170 | tf_op jit(solution)/shard_map/tkj,kij->tki/dot_general | solution.py:68
  188.2 2.2 copy.97
  190.4 0.0 copy-start.3
  190.4 238.1 %all-reduce.5.cloned.1.call-done = f32[10,256,256]{2,1,0:T(8,128)} async-done(((f32[10,256,256]{2,1,0:T(8,128)}), f32[10,256,256]{2,1,0:T(8,128)}) %all-reduce.5.cloned.1.call-update) | async-done | bytes 2621456 | tf_op jit(solution)/shard_map/psum | solution.py:76
  428.5 4.8 %fusion.2 = f32[3,256,256]{2,0,1:T(4,128)S(1)} fusion(f32[10,256,256]{2,1,0:T(8,128)} %all-reduce.5.cloned.1.call-done, s32[10]{0:T(128)S(1)} %add_bitcast_fusion, pred[10]{0:T(512)(128)(4,1)S(1)} %get-tuple-element.14), kind=kOutput, calls=%fused_computation.6 | convolution fusion | flops 23593020 | bytes 3407922 | tf_op jit(solution)/shard_map/sb,bij->sij/dot_general | solution.py:81
  433.3 0.0 copy-done.3
  433.3 1.0 fusion.17
  434.4 1.0 fusion.19
  435.4 1.1 convolution_add_fusion.2
  436.5 0.9 convolution_add_fusion.1
  437.4 0.0 copy-start.1
  437.5 1.8 convolution_add_fusion
  439.2 2.3 copy.96
  441.5 1.5 fusion.14
  443.0 1.1 copy.98
  444.2 0.0 copy-done.1
  (9 shorter events, 0.1 us)
Async XLA Ops:
  7.2 18.5 %copy-start = (bf16[512,2560]{1,0:T(8,128)(2,1)S(1)}, bf16[512,2560]{1,0:T(8,128)(2,1)}, u32[]{:S(2)}) copy-start(bf16[512,2560]{1,0:T(8,128)(2,1)} %param.6) | copy-start | bytes 7864324
  7.2 135.2 %all-reduce.3.cloned.1.call-start = ((), (), s32[]{:S(2)}) async-start(), calls=%async_computation | async-start | bytes 10485760 | tf_op jit(solution)/shard_map/psum | solution.py:60
  24.6 0.7 copy-start.5
  24.6 0.8 copy-start.6
  24.6 403.9 %all-reduce.5.cloned.1.call-start = ((), (), s32[]{:S(2)}) async-start(), calls=%async_computation.1 | async-start | bytes 5242880 | tf_op jit(solution)/shard_map/psum | solution.py:76
  29.0 2.1 copy-start.4
  162.8 2.3 copy-start.2
  190.4 243.0 %copy-start.3 = (f32[3,256,256]{2,0,1:T(4,128)S(1)}, f32[3,256,256]{2,0,1:T(4,128)}, u32[]{:S(2)}) copy-start(f32[3,256,256]{2,0,1:T(4,128)} %fusion) | copy-start | bytes 2359300
  437.4 6.7 %copy-start.1 = (bf16[512,2560]{1,0:T(8,128)(2,1)S(1)}, bf16[512,2560]{1,0:T(8,128)(2,1)}, u32[]{:S(2)}) copy-start(bf16[512,2560]{1,0:T(8,128)(2,1)} %param.6) | copy-start | bytes 7864324
Sparse Core Ops, SparseCore 0:
  24.8 117.6 all-reduce.2
  168.0 260.4 all-reduce.4
where the time goes:
time: 454 us; the launch traced here: 451 us
  waiting for transfers between devices  343 us (76%)
  local copies, waits for them, and re-layouts  45.2 us (10%)
  matrix products  41.2 us (9%)
  between operations  14.3 us (3%)
  other arithmetic  7.66 us (2%)
    psum x1, waiting for transfers between devices, local(): gram = lax.psum(local_gram, ('dp', 'mp'))  238 us
    psum x1, waiting for transfers between devices, local(): feature_grad = lax.psum(partial_grad, 'mp')  104 us
    gather x5, local copies, waits for them, and re-layouts, to_blocks(): jnp.take(tiled, order, axis=1).reshape(matrix.shape[0], block_count, -1)  18.5 us
    dot_general x7, matrix products, product(): return jnp.einsum('bij,bjk->bik', first, second, precision=highest)  13.5 us
    dot_general x1, matrix products, local(): lax.dot_general(cotangent, frozen_weight, (((1,), (1,)), ((), ())), prefe...  11.5 us
  transfers between devices with their start and end apart: 2, of which 2 were waited for; matrix products, arithmetic and copies ran while one was open for 8% of the time, Pallas kernels for 0%

commit v1 on v0

v1 whole, which is shorter than its diff:
```python
import math

import jax
import jax.numpy as jnp
from jax import lax
from jax.experimental import pallas as pl
from jax.experimental.pallas import tpu as pltpu
from jax.sharding import Mesh
from jax.sharding import PartitionSpec as P

SLOTS = 3
X, Z, CORES, Y = 4, 8, 2, 4
TILE = 128
BLOCK = 256
f32 = jnp.float32
bf16 = jnp.bfloat16
NN = (((1,), (0,)), ((), ()))
NT = (((1,), (1,)), ((), ()))
TN = (((0,), (0,)), ((), ()))


def dot(a, b, dims=NN):
    return lax.dot_general(a, b, dims, preferred_element_type=f32)


def split(a):
    high = a.astype(bf16)
    return high, (a - high.astype(f32)).astype(bf16)


def product(a, b):
    return dot(a[0], b[0]) + (dot(a[0], b[1]) + dot(a[1], b[0]))


def main_kernel(order, place, w0, w1, cot, a0, a1, skew_ref, *outs):
    sums, packs = outs[:8], outs[8:]
    b = pl.program_id(0)
    y, core = place[0], place[1]
    plain = skew_ref[0].astype(f32)
    turned = plain.T - plain
    turned_pair = split(turned)
    square = product(turned_pair, turned_pair)
    cube = product(split(square), turned_pair)
    rows = lax.broadcasted_iota(jnp.int32, (BLOCK, BLOCK), 0)
    cols = lax.broadcasted_iota(jnp.int32, (BLOCK, BLOCK), 1)
    rotation_t = jnp.where(rows == cols, 1.0, 0.0) + 2.0 * turned + 2.0 * square + cube
    weight = jnp.concatenate([w0[...], w1[...]], axis=0)
    grad = dot(cot[...], weight, NT)
    grad_pair = split(grad)
    inputs = jnp.concatenate([a0[...], a1[...]], axis=1)
    gram = dot(inputs, grad_pair[0], TN) + dot(inputs, grad_pair[1], TN)
    rotated = product(grad_pair, split(rotation_t))
    half = rotated.shape[0] // 2
    for side in range(2):
        tile = order[2 * b + side]
        owner = lax.div(tile, 5)
        place_in = lax.rem(tile, 5)
        relative = lax.rem(owner - y + Y, Y)
        columns = rotated[:, side * TILE : (side + 1) * TILE]
        for r in range(Y):

            @pl.when(relative == r)
            def _(r=r, place_in=place_in, columns=columns):
                sums[2 * r][place_in] = columns[:half]
                sums[2 * r + 1][place_in] = columns[half:]

    gram_t = gram.T
    odd = gram - gram_t
    first = product(split(odd), turned_pair)
    second = product(split(2.0 * (gram + gram_t) + first), turned_pair)
    third = product(turned_pair, split(first))
    total = odd + second + 0.5 * third
    grads = total - total.T
    near = rows[:TILE, :TILE] < cols[:TILE, :TILE]
    pack = jnp.concatenate(
        [jnp.where(near, grads[:TILE, :TILE], grads[TILE:, TILE:]), grads[:TILE, TILE:]], axis=0
    ).reshape(32, 8, TILE)
    mine = lax.div(b, 5) == core
    where = lax.rem(b, 5)

    @pl.when(mine)
    def _():
        packs[0][:, pl.ds(where, 1)] = pack[:, None]

    @pl.when(jnp.logical_not(mine))
    def _():
        packs[1][:, pl.ds(where, 1)] = pack[:, None]


def main_call(tile_order, place, frozen_weight, cotangent, activations, skew_params):
    tokens = cotangent.shape[0]
    wide = cotangent.shape[1]
    sums = [jax.ShapeDtypeStruct((5, tokens // 2, TILE), f32)] * 8
    packs = [jax.ShapeDtypeStruct((32, 5, 8, TILE), f32)] * 2
    whole3 = pl.BlockSpec((5, tokens // 2, TILE), lambda b, o, p: (0, 0, 0))
    whole4 = pl.BlockSpec((32, 5, 8, TILE), lambda b, o, p: (0, 0, 0, 0))
    return pl.pallas_call(
        main_kernel,
        out_shape=sums + packs,
        grid_spec=pltpu.PrefetchScalarGridSpec(
            num_scalar_prefetch=2,
            grid=(10,),
            in_specs=[
                pl.BlockSpec((TILE, wide), lambda b, o, p: (o[2 * b], 0)),
                pl.BlockSpec((TILE, wide), lambda b, o, p: (o[2 * b + 1], 0)),
                pl.BlockSpec((tokens, wide), lambda b, o, p: (0, 0)),
                pl.BlockSpec((tokens, TILE), lambda b, o, p: (0, o[2 * b])),
                pl.BlockSpec((tokens, TILE), lambda b, o, p: (0, o[2 * b + 1])),
                pl.BlockSpec((1, BLOCK, BLOCK), lambda b, o, p: (b, 0, 0)),
            ],
            out_specs=[whole3] * 8 + [whole4] * 2,
        ),
        compiler_params=pltpu.CompilerParams(vmem_limit_bytes=44 * 2**20),
        cost_estimate=pl.CostEstimate(flops=12 * 10**9, bytes_accessed=22 * 10**6, transcendentals=0),
        name="main",
    )(tile_order, place, frozen_weight, frozen_weight, cotangent, activations, activations, skew_params)


def sum_kernel(parts, out):
    total = parts[0]
    for i in range(1, 32):
        total = total + parts[i]
    out[...] = total


def sum_call(parts):
    return pl.pallas_call(
        sum_kernel,
        out_shape=jax.ShapeDtypeStruct(parts.shape[1:], f32),
        cost_estimate=pl.CostEstimate(flops=10**6, bytes_accessed=10**6, transcendentals=0),
        name="slice_sum",
    )(parts)


def route_kernel(owner, place, own, other, out):
    core = place[1]
    out[...] = jnp.zeros_like(out)
    for b in range(10):
        target = owner[b]
        rank = jnp.int32(0)
        for e in range(b):
            rank = rank + jnp.where(owner[e] == target, 1, 0)
        side, j = b // 5, b % 5

        @pl.when(lax.rem(target, CORES) == core)
        def _(target=target, rank=rank, side=side, j=j):
            value = jnp.where(core == side, own[j], other[j])
            out[lax.div(target, CORES), rank] = value


def route_call(block_owner, place, own, other):
    smem = pl.BlockSpec(memory_space=pltpu.SMEM)
    vmem = pl.BlockSpec(memory_space=pltpu.VMEM)
    return pl.pallas_call(
        route_kernel,
        out_shape=jax.ShapeDtypeStruct((32, SLOTS, 8, TILE), f32),
        in_specs=[smem, smem, vmem, vmem],
        out_specs=vmem,
        cost_estimate=pl.CostEstimate(flops=10**5, bytes_accessed=10**6, transcendentals=0),
        name="route",
    )(block_owner, place, own, other)


def unpack_kernel(scale, parts, out):
    rows = lax.broadcasted_iota(jnp.int32, (TILE, TILE), 0)
    cols = lax.broadcasted_iota(jnp.int32, (TILE, TILE), 1)
    for s in range(SLOTS):
        pack = parts[:, s].reshape(2 * TILE, TILE) * scale
        upper = jnp.where(rows < cols, pack[:TILE], 0.0)
        lower = jnp.where(rows > cols, pack[:TILE], 0.0)
        across = pack[TILE:]
        out[s, :TILE, :TILE] = upper - upper.T
        out[s, TILE:, TILE:] = lower - lower.T
        out[s, :TILE, TILE:] = across
        out[s, TILE:, :TILE] = -across.T


def unpack_call(parts, scale):
    return pl.pallas_call(
        lambda parts, out: unpack_kernel(scale, parts, out),
        out_shape=jax.ShapeDtypeStruct((SLOTS, BLOCK, BLOCK), f32),
        cost_estimate=pl.CostEstimate(flops=10**6, bytes_accessed=10**6, transcendentals=0),
        name="unpack",
    )(parts)


def finish_kernel(a0, a1, a2, b0, b1, b2, out):
    half = a0.shape[1]
    for k in range(5):
        columns = slice(k * TILE, (k + 1) * TILE)
        out[:half, columns] = (a0[k] + a1[k] + a2[k]).astype(bf16)
        out[half:, columns] = (b0[k] + b1[k] + b2[k]).astype(bf16)


def finish_call(*parts):
    tokens = 2 * parts[0].shape[1]
    return pl.pallas_call(
        finish_kernel,
        out_shape=jax.ShapeDtypeStruct((tokens, 5 * TILE), bf16),
        compiler_params=pltpu.CompilerParams(vmem_limit_bytes=16 * 2**20),
        cost_estimate=pl.CostEstimate(flops=10**6, bytes_accessed=5 * 10**6, transcendentals=0),
        name="finish",
    )(*parts)


def turn(size, by):
    return [(i, (i + by) % size) for i in range(size)]


def local(activations, cotangent, frozen_weight, skew_params, tile_order, block_owner):
    place = jnp.stack([lax.axis_index("y"), lax.axis_index("core")]).astype(jnp.int32)
    outs = main_call(tile_order, place, frozen_weight, cotangent, activations, skew_params)
    (own_a, own_b, next_a, next_b, far_a, far_b, last_a, last_b, pack_own, pack_other) = outs
    far_a = lax.ppermute(far_a, "y", turn(Y, 1))
    last_a = lax.ppermute(last_a, "y", turn(Y, -1))
    far_b = lax.ppermute(far_b, "y", turn(Y, -1))
    next_b = lax.ppermute(next_b, "y", turn(Y, 1))
    pack = pack_own + lax.ppermute(pack_other, "core", turn(CORES, 1))
    slices = sum_call(lax.all_to_all(pack, ("x", "z"), 0, 0, tiled=True))
    next_a = lax.ppermute(next_a + far_a, "y", turn(Y, 1))
    last_b = lax.ppermute(last_b + far_b, "y", turn(Y, -1))
    others = [lax.ppermute(slices, "y", turn(Y, s)) for s in (1, 2, 3)]
    slices = (slices + others[1]) + (others[0] + others[2])
    routed = route_call(block_owner, place, slices, lax.ppermute(slices, "core", turn(CORES, 1)))
    owned = lax.all_to_all(routed, ("x", "z"), 0, 0, tiled=True)
    scale = 1.0 / math.sqrt(cotangent.shape[0] * X * Z * CORES)
    skew_grads = unpack_call(owned, scale)
    input_grad = finish_call(own_a, next_a, last_a, own_b, next_b, last_b)
    return (input_grad, skew_grads)


def solution(mesh):
    grid = Mesh(mesh.devices.reshape(X, Z, CORES, Y), ("x", "z", "core", "y"))
    dp = ("x", "z", "core")
    placed = (P(dp, None), P(dp, "y"), P(None, "y"), P(), P(), P())
    return jax.shard_map(
        local,
        mesh=grid,
        in_specs=placed,
        out_specs=(P(dp, "y"), P(dp, None, None)),
        check_vma=False,
    )
```

time: 454 us -> 146 us (0.32)
  waiting for transfers between devices: 343 us -> 49.3 us
  matrix products: 41.2 us -> 0 us
  Pallas kernels: 0 us -> 38.8 us
  starting transfers between devices: 0.08 us -> 31.7 us
  local copies, waits for them, and re-layouts: 45.2 us -> 20 us
  between operations: 14.3 us -> 0.79 us
    psum x2 -> x0, waiting for transfers between devices: 343 us -> none  [the longest x1 238 us: local(): gram = lax.psum(local_gram, ('dp', 'mp'))]
    dot_general x12 -> x0, matrix products: 41.2 us -> none  [the longest x7 13.5 us: product(): return jnp.einsum('bij,bjk->bik', first, second, precision=highest)]
    pallas_call x0 -> x5, Pallas kernels: none -> 38.8 us  [the longest x1 32.3 us: main_call(): pl.pallas_call(main_kernel, out_shape=sums + packs, grid_spec=pltpu.Prefe...]
    ppermute x0 -> x11, waiting for transfers between devices: none -> 32 us  [the longest x1 12.3 us: local(): next_a = lax.ppermute(next_a + far_a, 'y', turn(Y, 1))]
    gather x7 -> x0, local copies, waits for them, and re-layouts: 24.9 us -> none  [the longest x5 18.5 us: to_blocks(): jnp.take(tiled, order, axis=1).reshape(matrix.shape[0], block_count, -1)]
    all_to_all x0 -> x2, waiting for transfers between devices: none -> 17.3 us  [the longest x1 17.3 us: local(): slices = sum_call(lax.all_to_all(pack, ('x', 'z'), 0, 0, tiled=True))]
    all_to_all x0 -> x2, starting transfers between devices: none -> 16.4 us  [the longest x1 11.4 us: local(): slices = sum_call(lax.all_to_all(pack, ('x', 'z'), 0, 0, tiled=True))]
    ppermute x0 -> x11, starting transfers between devices: none -> 15.4 us  [the longest x3 5.25 us: local(): others = [lax.ppermute(slices, 'y', turn(Y, s)) for s in (1, 2, 3)]]
  transfers between devices with their start and end apart: 2 -> 13, of which waited for: 2 -> 8; matrix products, arithmetic and copies ran while one was open for 8% -> 2% of each run, Pallas kernels for 0% -> 3%
where the time goes in v1:
time: 146 us; the launch traced here: 145 us
  waiting for transfers between devices  49.3 us (34%)
  Pallas kernels  38.8 us (27%)
  starting transfers between devices  31.7 us (22%)
  local copies, waits for them, and re-layouts  20 us (14%)
  other arithmetic  4.04 us (3%)
    pallas_call x1, Pallas kernels, main_call(): pl.pallas_call(main_kernel, out_shape=sums + packs, grid_spec=pltpu.Prefe...  32.3 us
    unnamed x30, local copies, waits for them, and re-layouts  20 us
    all_to_all x1, waiting for transfers between devices, local(): slices = sum_call(lax.all_to_all(pack, ('x', 'z'), 0, 0, tiled=True))  17.3 us
    ppermute x1, waiting for transfers between devices, local(): next_a = lax.ppermute(next_a + far_a, 'y', turn(Y, 1))  12.3 us
    all_to_all x1, starting transfers between devices, local(): slices = sum_call(lax.all_to_all(pack, ('x', 'z'), 0, 0, tiled=True))  11.4 us
    ppermute x1, waiting for transfers between devices, local(): last_a = lax.ppermute(last_a, 'y', turn(Y, -1))  9.74 us
    ppermute x3, starting transfers between devices, local(): others = [lax.ppermute(slices, 'y', turn(Y, s)) for s in (1, 2, 3)]  5.25 us
    all_to_all x1, starting transfers between devices, local(): owned = lax.all_to_all(routed, ('x', 'z'), 0, 0, tiled=True)  5.04 us
  transfers between devices with their start and end apart: 13, of which 8 were waited for; matrix products, arithmetic and copies ran while one was open for 2% of the time, Pallas kernels for 3%

profile of v1, /device:TPU:32, one launch (start us, length us, event | category | flops | bytes accessed | tf_op | source)
XLA Modules:
  0.0 144.7 jit_solution(501151143287249416)
XLA Ops:
  0.6 2.8 %copy.10.cot = bf16[512,1728]{1,0:T(8,128)(2,1)S(1)} copy(bf16[512,1728]{0,1:T(8,128)(2,1)} %param.7) | data formatting | bytes 3538944 | tf_op args[1]
  3.4 0.0 copy-start.11
  3.4 12.7 %copy.8.w0.w1 = bf16[2560,1728]{1,0:T(8,128)(2,1)} copy(bf16[2560,1728]{0,1:T(8,128)(2,1)} %param.8) | data formatting | bytes 17694720 | tf_op args[2]
  16.1 0.1 pad_add_fusion.place
  16.2 0.0 copy-done.11
  16.2 1.3 copy-done.5
  17.5 0.0 copy-start.4
  17.5 32.3 %main.1 = (f32[5,256,128]{2,1,0:T(8,128)S(1)}, f32[5,256,128]{2,1,0:T(8,128)S(1)}, f32[5,256,128]{2,1,0:T(8,128)S(1)}, f32[5,256,128]{2,1,0:T(8,128)S(1)}, f32[5...) custom-call(s32[20]{0:T(128)S(1)} %copy-done.11, ...), custom_call_target="tpu_custom_call" | custom-call | flops 12000000000 | bytes 22000000 | tf_op jit(solution)/shard_map/main/pallas_call | solution.py:97
  49.8 0.0 copy-done.4
  49.8 0.0 copy-start
  49.8 0.9 copy-done
  50.7 0.0 copy-start.2
  50.7 0.8 copy-done.2
  51.5 0.0 copy-start.6
  51.5 0.9 copy-done.6
  52.4 0.0 copy-start.8
  52.4 0.0 copy-start.9
  52.4 0.0 copy-start.10
  52.4 0.0 collective-permute-start.6
  52.4 2.1 %collective-permute-done.6 = f32[32,5,8,128]{3,2,1,0:T(8,128)S(1)} collective-permute-done((f32[32,5,8,128]{3,2,1,0:T(8,128)S(1)}, f32[32,5,8,128]{3,2,1,0:T(8,128)S(1)}, u32[]{:S(2)}, u32[]{:S(2)}) %collective-permute-start.6) | collective-permute-done | bytes 655392 | tf_op jit(solution)/shard_map/ppermute | solution.py:218
  54.5 0.0 copy-done.8
  54.5 0.0 copy-done.9
  54.5 0.0 copy-done.10
  54.5 0.0 copy-start.7
  54.5 0.0 copy-start.3
  54.5 0.9 add.20
  55.4 0.0 copy-start.1
  55.4 11.4 %all-to-all-start = ((f32[32,5,8,128]{3,2,1,0:T(8,128)}), f32[32,5,8,128]{3,2,1,0:T(8,128)}, u32[]{:S(2)}, u32[]{:S(2)}) async-start(f32[32,5,8,128]{3,2,1,0:T(8,128)} %add.20), calls=%async_computation | async-start | bytes 1310720 | tf_op jit(solution)/shard_map/all_to_all | solution.py:219
  66.8 1.7 %collective-permute-start = (f32[5,256,128]{2,1,0:T(8,128)}, f32[5,256,128]{2,1,0:T(8,128)}, u32[]{:S(2)}, u32[]{:S(2)}) collective-permute-start(f32[5,256,128]{2,1,0:T(8,128)} %copy-done.10), channel_id=1, source_target_pairs={{0,1},{1,2},{2,3},{3,0},{4,5},{5,6},{6,7},{7,4},{8,9},{9,10},{10,1... | collective-permute-start | bytes 1966088 | tf_op jit(solution)/shard_map/ppermute | solution.py:214
  68.5 1.6 %collective-permute-start.4 = (f32[5,256,128]{2,1,0:T(8,128)}, f32[5,256,128]{2,1,0:T(8,128)}, u32[]{:S(2)}, u32[]{:S(2)}) collective-permute-start(f32[5,256,128]{2,1,0:T(8,128)} %copy-done.9), channel_id=1, source_target_pairs={{0,3},{1,0},{2,1},{3,2},{4,7},{5,4},{6,5},{7,6},{8,11},{9,8},{10,9... | collective-permute-start | bytes 1966088 | tf_op jit(solution)/shard_map/ppermute | solution.py:216
  70.1 17.3 %all-to-all-done.parts = f32[32,5,8,128]{3,2,1,0:T(8,128)} async-done(((f32[32,5,8,128]{3,2,1,0:T(8,128)}), f32[32,5,8,128]{3,2,1,0:T(8,128)}, u32[]{:S(2)}, u32[]{:S(2)}) %all-to-all-start) | async-done | bytes 655392 | tf_op jit(solution)/shard_map/all_to_all | solution.py:219
  87.5 1.7 %slice_sum.1 = f32[5,8,128]{2,1,0:T(8,128)} custom-call(f32[32,5,8,128]{3,2,1,0:T(8,128)} %all-to-all-done.parts), custom_call_target="tpu_custom_call" | custom-call | flops 1000000 | bytes 1000000 | tf_op jit(solution)/shard_map/slice_sum/pallas_call | solution.py:127
  89.2 3.0 %collective-permute-start.9 = (f32[5,8,128]{2,1,0:T(8,128)}, f32[5,8,128]{2,1,0:T(8,128)S(1)}, u32[]{:S(2)}, u32[]{:S(2)}) collective-permute-start(f32[5,8,128]{2,1,0:T(8,128)} %slice_sum.1), channel_id=1, source_target_pairs={{0,3},{1,0},{2,1},{3,2},{4,7},{5,4},{6,5},{7,6},{8,11},{9,8},{10,9... | collective-permute-start | bytes 61448 | tf_op jit(solution)/shard_map/ppermute | solution.py:222
  92.2 0.0 collective-permute-start.8
  92.2 2.2 %collective-permute-start.7 = (f32[5,8,128]{2,1,0:T(8,128)}, f32[5,8,128]{2,1,0:T(8,128)S(1)}, u32[]{:S(2)}, u32[]{:S(2)}) collective-permute-start(f32[5,8,128]{2,1,0:T(8,128)} %slice_sum.1), channel_id=1, source_target_pairs={{0,2},{1,3},{2,0},{3,1},{4,6},{5,7},{6,4},{7,5},{8,10},{9,11},{10,... | collective-permute-start | bytes 61448 | tf_op jit(solution)/shard_map/ppermute | solution.py:222
  94.5 0.0 collective-permute-done.9
  94.5 3.0 %collective-permute-done.8 = f32[5,8,128]{2,1,0:T(8,128)S(1)} collective-permute-done((f32[5,8,128]{2,1,0:T(8,128)}, f32[5,8,128]{2,1,0:T(8,128)S(1)}, u32[]{:S(2)}, u32[]{:S(2)}) %collective-permute-start.8) | collective-permute-done | bytes 20512 | tf_op jit(solution)/shard_map/ppermute | solution.py:222
  97.4 0.3 collective-permute-done.7
  97.7 0.7 add_add_fusion.own
  98.4 0.0 copy-start.12
  98.4 0.1 collective-permute-start.10
  98.5 1.2 collective-permute-done.10.other
  99.7 0.0 copy-done.12
  99.7 0.6 copy-done.13
  100.3 1.7 %route.1 = f32[32,3,8,128]{3,2,1,0:T(8,128)} custom-call(s32[10]{0:T(128)} %owner.1, s32[2]{0:T(128)} %copy-done.4, f32[5,8,128]{2,1,0:T(8,128)} %copy-done.12, f32[5,8,128]{2,1,0:T(8,128)} %copy-done.13), custom_call_target="tpu_custom_call" | custom-call | flops 100000 | bytes 1000000 | tf_op jit(solution)/shard_map/route/pallas_call | solution.py:154
  102.0 5.0 %all-to-all-start.1 = ((f32[32,3,8,128]{3,2,1,0:T(8,128)}), f32[32,3,8,128]{3,2,1,0:T(8,128)}, u32[]{:S(2)}, u32[]{:S(2)}) async-start(f32[32,3,8,128]{3,2,1,0:T(8,128)} %route.1), calls=%async_computation.1 | async-start | bytes 786432 | tf_op jit(solution)/shard_map/all_to_all | solution.py:225
  107.1 3.3 %collective-permute-start.2 = (f32[5,256,128]{2,1,0:T(8,128)}, f32[5,256,128]{2,1,0:T(8,128)S(1)}, u32[]{:S(2)}, u32[]{:S(2)}) collective-permute-start(f32[5,256,128]{2,1,0:T(8,128)} %copy-done.8), channel_id=1, source_target_pairs={{0,3},{1,0},{2,1},{3,2},{4,7},{5,4},{6,5},{7,6},{8,11},{9,8},{10,9... | collective-permute-start | bytes 1966088 | tf_op jit(solution)/shard_map/ppermute | solution.py:215
  110.4 0.0 copy-done.7
  110.4 0.0 collective-permute-start.3
  110.4 0.0 collective-permute-done
  110.4 0.0 copy-done.3
  110.4 1.2 add.18
  111.6 0.1 collective-permute-start.1
  111.6 0.0 collective-permute-done.4
  111.7 0.0 copy-done.1
  111.7 1.2 add.19
  112.8 3.3 %collective-permute-start.5 = (f32[5,256,128]{2,1,0:T(8,128)S(1)}, f32[5,256,128]{2,1,0:T(8,128)S(1)}, u32[]{:S(2)}, u32[]{:S(2)}) collective-permute-start(f32[5,256,128]{2,1,0:T(8,128)S(1)} %add.19), channel_id=1, source_target_pairs={{0,3},{1,0},{2,1},{3,2},{4,7},{5,4},{6,5},{7,6},{8,11},{9,8},{10,9... | collective-permute-start | bytes 1966088 | tf_op jit(solution)/shard_map/ppermute | solution.py:221
  116.1 9.7 %collective-permute-done.2.a2 = f32[5,256,128]{2,1,0:T(8,128)S(1)} collective-permute-done((f32[5,256,128]{2,1,0:T(8,128)}, f32[5,256,128]{2,1,0:T(8,128)S(1)}, u32[]{:S(2)}, u32[]{:S(2)}) %collective-permute-start.2) | collective-permute-done | bytes 655392 | tf_op jit(solution)/shard_map/ppermute | solution.py:215
  125.9 3.4 %collective-permute-done.3.b1 = f32[5,256,128]{2,1,0:T(8,128)S(1)} collective-permute-done((f32[5,256,128]{2,1,0:T(8,128)S(1)}, f32[5,256,128]{2,1,0:T(8,128)S(1)}, u32[]{:S(2)}, u32[]{:S(2)}) %collective-permute-start.3) | collective-permute-done | bytes 655392 | tf_op jit(solution)/shard_map/ppermute | solution.py:217
  129.3 12.3 %collective-permute-done.1.a1 = f32[5,256,128]{2,1,0:T(8,128)S(1)} collective-permute-done((f32[5,256,128]{2,1,0:T(8,128)S(1)}, f32[5,256,128]{2,1,0:T(8,128)S(1)}, u32[]{:S(2)}, u32[]{:S(2)}) %collective-permute-start.1) | collective-permute-done | bytes 655392 | tf_op jit(solution)/shard_map/ppermute | solution.py:220
  141.6 0.0 collective-permute-done.5.b2
  141.6 1.0 finish.1
  142.6 0.0 all-to-all-done.1.parts
  142.6 2.1 %unpack.1 = f32[3,256,256]{2,1,0:T(8,128)} custom-call(f32[32,3,8,128]{3,2,1,0:T(8,128)} %all-to-all-done.1.parts), custom_call_target="tpu_custom_call" | custom-call | flops 1000000 | bytes 1000000 | tf_op jit(solution)/shard_map/unpack/pallas_call | solution.py:179
  (2 shorter events, 0.0 us)
Async XLA Ops:
  3.4 12.8 %copy-start.11 = (s32[20]{0:T(128)S(1)}, s32[20]{0:T(128)}, u32[]{:S(2)}) copy-start(s32[20]{0:T(128)} %order.1) | copy-start | bytes 244
  16.2 1.3 copy-start.5
  17.5 32.3 %copy-start.4 = (s32[2]{0:T(128)}, s32[2]{0:T(128)S(1)}, u32[]{:S(2)}) copy-start(s32[2]{0:T(128)S(1)} %pad_add_fusion.place) | copy-start | bytes 28
  49.8 0.9 copy-start
  50.7 0.8 copy-start.2
  51.5 0.9 copy-start.6
  52.4 2.1 %copy-start.8 = (f32[5,256,128]{2,1,0:T(8,128)}, f32[5,256,128]{2,1,0:T(8,128)S(1)}, u32[]{:S(2)}) copy-start(f32[5,256,128]{2,1,0:T(8,128)S(1)} %get-tuple-element.15) | copy-start | bytes 1966084
  52.4 2.1 %copy-start.9 = (f32[5,256,128]{2,1,0:T(8,128)}, f32[5,256,128]{2,1,0:T(8,128)S(1)}, u32[]{:S(2)}) copy-start(f32[5,256,128]{2,1,0:T(8,128)S(1)} %get-tuple-element.19) | copy-start | bytes 1966084
  52.4 2.1 %copy-start.10 = (f32[5,256,128]{2,1,0:T(8,128)}, f32[5,256,128]{2,1,0:T(8,128)S(1)}, u32[]{:S(2)}) copy-start(f32[5,256,128]{2,1,0:T(8,128)S(1)} %get-tuple-element.14) | copy-start | bytes 1966084
  52.4 2.1 %collective-permute-start.6 = (f32[32,5,8,128]{3,2,1,0:T(8,128)S(1)}, f32[32,5,8,128]{3,2,1,0:T(8,128)S(1)}, u32[]{:S(2)}, u32[]{:S(2)}) collective-permute-start(f32[32,5,8,128]{3,2,1,0:T(8,128)S(1)} %get-tuple-element.21), channel_id=1, source_target_pairs={{0,4},{4,0},{1,5},{5,1},{2,6},{6,2},{3,7},{7,3},{8,12},{12,8},{9,1... | collective-permute-start | bytes 1966088 | tf_op jit(solution)/shard_map/ppermute | solution.py:218
  54.5 55.9 %copy-start.7 = (f32[5,256,128]{2,1,0:T(8,128)S(1)}, f32[5,256,128]{2,1,0:T(8,128)}, u32[]{:S(2)}) copy-start(f32[5,256,128]{2,1,0:T(8,128)} %copy-done.6) | copy-start | bytes 1966084
  54.5 55.9 %copy-start.3 = (f32[5,256,128]{2,1,0:T(8,128)S(1)}, f32[5,256,128]{2,1,0:T(8,128)}, u32[]{:S(2)}) copy-start(f32[5,256,128]{2,1,0:T(8,128)} %copy-done.2) | copy-start | bytes 1966084
  55.4 56.2 %copy-start.1 = (f32[5,256,128]{2,1,0:T(8,128)S(1)}, f32[5,256,128]{2,1,0:T(8,128)}, u32[]{:S(2)}) copy-start(f32[5,256,128]{2,1,0:T(8,128)} %copy-done) | copy-start | bytes 1966084
  55.4 32.0 %all-to-all-start = ((f32[32,5,8,128]{3,2,1,0:T(8,128)}), f32[32,5,8,128]{3,2,1,0:T(8,128)}, u32[]{:S(2)}, u32[]{:S(2)}) async-start(f32[32,5,8,128]{3,2,1,0:T(8,128)} %add.20), calls=%async_computation | async-start | bytes 1310720 | tf_op jit(solution)/shard_map/all_to_all | solution.py:219
  66.8 43.6 %collective-permute-start = (f32[5,256,128]{2,1,0:T(8,128)}, f32[5,256,128]{2,1,0:T(8,128)}, u32[]{:S(2)}, u32[]{:S(2)}) collective-permute-start(f32[5,256,128]{2,1,0:T(8,128)} %copy-done.10), channel_id=1, source_target_pairs={{0,1},{1,2},{2,3},{3,0},{4,5},{5,6},{6,7},{7,4},{8,9},{9,10},{10,1... | collective-permute-start | bytes 1966088 | tf_op jit(solution)/shard_map/ppermute | solution.py:214
  68.5 43.2 %collective-permute-start.4 = (f32[5,256,128]{2,1,0:T(8,128)}, f32[5,256,128]{2,1,0:T(8,128)}, u32[]{:S(2)}, u32[]{:S(2)}) collective-permute-start(f32[5,256,128]{2,1,0:T(8,128)} %copy-done.9), channel_id=1, source_target_pairs={{0,3},{1,0},{2,1},{3,2},{4,7},{5,4},{6,5},{7,6},{8,11},{9,8},{10,9... | collective-permute-start | bytes 1966088 | tf_op jit(solution)/shard_map/ppermute | solution.py:216
  89.2 5.3 %collective-permute-start.9 = (f32[5,8,128]{2,1,0:T(8,128)}, f32[5,8,128]{2,1,0:T(8,128)S(1)}, u32[]{:S(2)}, u32[]{:S(2)}) collective-permute-start(f32[5,8,128]{2,1,0:T(8,128)} %slice_sum.1), channel_id=1, source_target_pairs={{0,3},{1,0},{2,1},{3,2},{4,7},{5,4},{6,5},{7,6},{8,11},{9,8},{10,9... | collective-permute-start | bytes 61448 | tf_op jit(solution)/shard_map/ppermute | solution.py:222
  92.2 5.2 %collective-permute-start.8 = (f32[5,8,128]{2,1,0:T(8,128)}, f32[5,8,128]{2,1,0:T(8,128)S(1)}, u32[]{:S(2)}, u32[]{:S(2)}) collective-permute-start(f32[5,8,128]{2,1,0:T(8,128)} %slice_sum.1), channel_id=1, source_target_pairs={{0,1},{1,2},{2,3},{3,0},{4,5},{5,6},{6,7},{7,4},{8,9},{9,10},{10,1... | collective-permute-start | bytes 61448 | tf_op jit(solution)/shard_map/ppermute | solution.py:222
  92.2 5.5 %collective-permute-start.7 = (f32[5,8,128]{2,1,0:T(8,128)}, f32[5,8,128]{2,1,0:T(8,128)S(1)}, u32[]{:S(2)}, u32[]{:S(2)}) collective-permute-start(f32[5,8,128]{2,1,0:T(8,128)} %slice_sum.1), channel_id=1, source_target_pairs={{0,2},{1,3},{2,0},{3,1},{4,6},{5,7},{6,4},{7,5},{8,10},{9,11},{10,... | collective-permute-start | bytes 61448 | tf_op jit(solution)/shard_map/ppermute | solution.py:222
  98.4 1.3 copy-start.12
  98.4 1.3 collective-permute-start.10
  99.7 0.6 copy-start.13
  102.0 40.6 %all-to-all-start.1 = ((f32[32,3,8,128]{3,2,1,0:T(8,128)}), f32[32,3,8,128]{3,2,1,0:T(8,128)}, u32[]{:S(2)}, u32[]{:S(2)}) async-start(f32[32,3,8,128]{3,2,1,0:T(8,128)} %route.1), calls=%async_computation.1 | async-start | bytes 786432 | tf_op jit(solution)/shard_map/all_to_all | solution.py:225
  107.1 18.8 %collective-permute-start.2 = (f32[5,256,128]{2,1,0:T(8,128)}, f32[5,256,128]{2,1,0:T(8,128)S(1)}, u32[]{:S(2)}, u32[]{:S(2)}) collective-permute-start(f32[5,256,128]{2,1,0:T(8,128)} %copy-done.8), channel_id=1, source_target_pairs={{0,3},{1,0},{2,1},{3,2},{4,7},{5,4},{6,5},{7,6},{8,11},{9,8},{10,9... | collective-permute-start | bytes 1966088 | tf_op jit(solution)/shard_map/ppermute | solution.py:215
  110.4 18.9 %collective-permute-start.3 = (f32[5,256,128]{2,1,0:T(8,128)S(1)}, f32[5,256,128]{2,1,0:T(8,128)S(1)}, u32[]{:S(2)}, u32[]{:S(2)}) collective-permute-start(f32[5,256,128]{2,1,0:T(8,128)S(1)} %copy-done.7), channel_id=1, source_target_pairs={{0,1},{1,2},{2,3},{3,0},{4,5},{5,6},{6,7},{7,4},{8,9},{9,10},{10,1... | collective-permute-start | bytes 1966088 | tf_op jit(solution)/shard_map/ppermute | solution.py:217
  111.6 30.0 %collective-permute-start.1 = (f32[5,256,128]{2,1,0:T(8,128)S(1)}, f32[5,256,128]{2,1,0:T(8,128)S(1)}, u32[]{:S(2)}, u32[]{:S(2)}) collective-permute-start(f32[5,256,128]{2,1,0:T(8,128)S(1)} %add.18), channel_id=1, source_target_pairs={{0,1},{1,2},{2,3},{3,0},{4,5},{5,6},{6,7},{7,4},{8,9},{9,10},{10,1... | collective-permute-start | bytes 1966088 | tf_op jit(solution)/shard_map/ppermute | solution.py:220
  112.8 28.8 %collective-permute-start.5 = (f32[5,256,128]{2,1,0:T(8,128)S(1)}, f32[5,256,128]{2,1,0:T(8,128)S(1)}, u32[]{:S(2)}, u32[]{:S(2)}) collective-permute-start(f32[5,256,128]{2,1,0:T(8,128)S(1)} %add.19), channel_id=1, source_target_pairs={{0,3},{1,0},{2,1},{3,2},{4,7},{5,4},{6,5},{7,6},{8,11},{9,8},{10,9... | collective-permute-start | bytes 1966088 | tf_op jit(solution)/shard_map/ppermute | solution.py:221

commit v2 on v1

v2 whole, which is shorter than its diff:
```python
import math

import jax
import jax.numpy as jnp
from jax import lax
from jax.experimental import pallas as pl
from jax.experimental.pallas import tpu as pltpu
from jax.sharding import Mesh
from jax.sharding import PartitionSpec as P

SLOTS = 3
FINISH = 10**10
MERGE = int(2e10)
X, Z, CORES, Y = 4, 8, 2, 4
TILE = 128
BLOCK = 256
f32 = jnp.float32
bf16 = jnp.bfloat16
NN = (((1,), (0,)), ((), ()))
NT = (((1,), (1,)), ((), ()))
TN = (((0,), (0,)), ((), ()))


def dot(a, b, dims=NN):
    return lax.dot_general(a, b, dims, preferred_element_type=f32)


def split(a):
    high = a.astype(bf16)
    return high, (a - high.astype(f32)).astype(bf16)


def stack(a, axis):
    return jnp.concatenate([a[0], a[0], a[1]] if axis else [a[0], a[1], a[0]], axis=axis)


def product(a, b):
    return dot(stack(a, 1), stack(b, 0))


def turned_skew(ref, b):
    plain = ref[b].astype(f32)
    return plain.T - plain


def grad_kernel(
    order, place, weight, cot_t, inputs, skew, turn_high, turn_low, high, low, mine, other,
    skews, tiles, cots, cot, ins, weight_sems, input_sems, sems,
):
    core = place[1]

    def column(t):
        return pl.ds(pl.multiple_of(order[t] * TILE, TILE), TILE)

    def fetch(t):
        return pltpu.make_async_copy(
            weight.at[:, column(t)], tiles.at[t // 2, :, pl.ds(TILE * (t % 2), TILE)], weight_sems.at[t]
        )

    def fetch_inputs(t):
        return pltpu.make_async_copy(
            inputs.at[:, column(t)], ins.at[t // 2, :, pl.ds(TILE * (t % 2), TILE)], input_sems.at[t]
        )

    get_skew = pltpu.make_async_copy(skew, skews, sems.at[0])
    get_cot = pltpu.make_async_copy(cot_t, cots, sems.at[1])
    get_skew.start()
    get_cot.start()
    for t in range(20):
        fetch(t).start()
    for t in range(20):
        fetch_inputs(t).start()
    get_skew.wait()
    rows = lax.broadcasted_iota(jnp.int32, (BLOCK, BLOCK), 0)
    cols = lax.broadcasted_iota(jnp.int32, (BLOCK, BLOCK), 1)
    identity = jnp.where(rows == cols, 1.0, 0.0)
    for b0 in range(0, 10, 5):
        group = range(b0, b0 + 5)
        turned = [turned_skew(skews, b) for b in group]
        pairs = [split(a) for a in turned]
        squares = [product(a, a) for a in pairs]
        cubes = [product(split(a), p) for a, p in zip(squares, pairs)]
        for b, a, square, cube in zip(group, turned, squares, cubes):
            turn_high[b], turn_low[b] = split(identity + 2.0 * a + 2.0 * square + cube)
    get_cot.wait()
    cot[...] = cots[...].T
    for t in range(20):
        fetch(t).wait()
    for b in range(10):
        high[b], low[b] = split(dot(cot[...], tiles[b]))
    for t in range(20):
        fetch_inputs(t).wait()
    for out, first in ((mine, 5 * core), (other, 5 * (1 - core))):
        for j in range(5):
            b = first + j
            tile = ins[b]
            out[j] = dot(tile, high[b], TN) + dot(tile, low[b], TN)


def vmem():
    return pl.BlockSpec(memory_space=pltpu.VMEM)


def smem():
    return pl.BlockSpec(memory_space=pltpu.SMEM)


def anywhere():
    return pl.BlockSpec(memory_space=pltpu.HBM)


def grad_call(tile_order, place, weight_t, cot_t, activations, skew_params):
    wide, tokens = cot_t.shape
    turns = jax.ShapeDtypeStruct((10, BLOCK, BLOCK), bf16)
    part = jax.ShapeDtypeStruct((10, tokens, BLOCK), bf16)
    gram = jax.ShapeDtypeStruct((5, BLOCK, BLOCK), f32)
    return pl.pallas_call(
        grad_kernel,
        out_shape=[turns, turns, part, part, gram, gram],
        in_specs=[smem(), smem()] + [anywhere() for _ in range(4)],
        out_specs=[vmem() for _ in range(6)],
        scratch_shapes=[
            pltpu.VMEM((10, BLOCK, BLOCK), bf16),
            pltpu.VMEM((10, wide, BLOCK), bf16),
            pltpu.VMEM((wide, tokens), bf16),
            pltpu.VMEM((tokens, wide), bf16),
            pltpu.VMEM((10, tokens, BLOCK), bf16),
            pltpu.SemaphoreType.DMA((20,)),
            pltpu.SemaphoreType.DMA((20,)),
            pltpu.SemaphoreType.DMA((2,)),
        ],
        compiler_params=pltpu.CompilerParams(vmem_limit_bytes=40 * 2**20),
        cost_estimate=pl.CostEstimate(flops=8 * 10**9, bytes_accessed=14 * 10**6, transcendentals=0),
        name="grad",
    )(tile_order, place, weight_t, cot_t, activations, skew_params)


def rotate_kernel(order, place, turn_high, turn_low, high, low, far_a, far_b, next_a, next_b, last_a, last_b, own, rotated):
    y = place[0]
    for b in range(10):
        product_b = product((high[b], low[b]), (turn_high[b], turn_low[b]))
        rotated[order[2 * b]] = product_b[:, :TILE]
        rotated[order[2 * b + 1]] = product_b[:, TILE:]
    half = rotated.shape[1] // 2
    for k in range(5):
        own[k] = rotated[5 * y + k]
        for r, (a, b) in enumerate(((next_a, next_b), (far_a, far_b), (last_a, last_b))):
            tile = 5 * lax.rem(y + r + 1, Y) + k
            a[k] = rotated[tile, :half]
            b[k] = rotated[tile, half:]


def rotate_call(tile_order, place, turn_high, turn_low, high, low):
    tokens = high.shape[1]
    half = jax.ShapeDtypeStruct((5, tokens // 2, TILE), f32)
    return pl.pallas_call(
        rotate_kernel,
        out_shape=[half] * 6 + [jax.ShapeDtypeStruct((5, tokens, TILE), f32)],
        in_specs=[smem(), smem()] + [vmem() for _ in range(4)],
        out_specs=[vmem() for _ in range(6)] + [vmem()],
        scratch_shapes=[pltpu.VMEM((20, tokens, TILE), f32)],
        compiler_params=pltpu.CompilerParams(vmem_limit_bytes=24 * 2**20),
        cost_estimate=pl.CostEstimate(flops=2 * 10**9, bytes_accessed=10 * 10**6, transcendentals=0),
        name="rotate",
    )(tile_order, place, turn_high, turn_low, high, low)


def adjoint_kernel(place, mine, came, skew, out):
    core = place[1]
    rows = lax.broadcasted_iota(jnp.int32, (TILE, TILE), 0)
    cols = lax.broadcasted_iota(jnp.int32, (TILE, TILE), 1)
    group = range(5)
    turned = [split(turned_skew(skew, 5 * core + j)) for j in group]
    grams = [mine[j] + came[j] for j in group]
    odd = [a - a.T for a in grams]
    even = [2.0 * (a + a.T) for a in grams]
    first = [product(split(a), t) for a, t in zip(odd, turned)]
    second = [product(split(e + a), t) for e, a, t in zip(even, first, turned)]
    third = [product(t, split(a)) for a, t in zip(first, turned)]
    for j in group:
        total = odd[j] + second[j] + 0.5 * third[j]
        grads = total - total.T
        out[:, j] = jnp.concatenate(
            [jnp.where(rows < cols, grads[:TILE, :TILE], grads[TILE:, TILE:]), grads[:TILE, TILE:]], axis=0
        ).reshape(32, 8, TILE)


def adjoint_call(place, mine, came, skew_params):
    return pl.pallas_call(
        adjoint_kernel,
        out_shape=jax.ShapeDtypeStruct((32, 5, 8, TILE), f32),
        in_specs=[smem()] + [vmem() for _ in range(3)],
        out_specs=vmem(),
        compiler_params=pltpu.CompilerParams(vmem_limit_bytes=20 * 2**20),
        cost_estimate=pl.CostEstimate(flops=2 * 10**9, bytes_accessed=4 * 10**6, transcendentals=0),
        name="adjoint",
    )(place, mine, came, skew_params)


def merge_kernel(next_a, far_a, last_b, far_b, out_a, out_b):
    out_a[...] = next_a[...] + far_a[...]
    out_b[...] = last_b[...] + far_b[...]


def merge_call(*parts):
    return pl.pallas_call(
        merge_kernel,
        out_shape=[jax.ShapeDtypeStruct(parts[0].shape, f32)] * 2,
        in_specs=[vmem() for _ in range(4)],
        out_specs=[vmem() for _ in range(2)],
        compiler_params=pltpu.CompilerParams(vmem_limit_bytes=4 * 2**20),
        cost_estimate=pl.CostEstimate(flops=MERGE, bytes_accessed=4 * 10**6, transcendentals=0),
        name="merge",
    )(*parts)


def sum_kernel(parts, out):
    total = parts[0]
    for i in range(1, 32):
        total = total + parts[i]
    out[...] = total


def sum_call(parts):
    return pl.pallas_call(
        sum_kernel,
        out_shape=jax.ShapeDtypeStruct(parts.shape[1:], f32),
        cost_estimate=pl.CostEstimate(flops=10**6, bytes_accessed=10**6, transcendentals=0),
        name="slice_sum",
    )(parts)


def route_kernel(owner, place, own, other, out):
    core = place[1]
    out[...] = jnp.zeros_like(out)
    for b in range(10):
        target = owner[b]
        rank = jnp.int32(0)
        for e in range(b):
            rank = rank + jnp.where(owner[e] == target, 1, 0)
        side, j = b // 5, b % 5

        @pl.when(lax.rem(target, CORES) == core)
        def _(target=target, rank=rank, side=side, j=j):
            value = jnp.where(core == side, own[j], other[j])
            out[lax.div(target, CORES), rank] = value


def route_call(block_owner, place, own, other):
    return pl.pallas_call(
        route_kernel,
        out_shape=jax.ShapeDtypeStruct((32, SLOTS, 8, TILE), f32),
        in_specs=[smem(), smem(), vmem(), vmem()],
        out_specs=vmem(),
        cost_estimate=pl.CostEstimate(flops=10**5, bytes_accessed=10**6, transcendentals=0),
        name="route",
    )(block_owner, place, own, other)


def unpack_kernel(scale, parts, out):
    rows = lax.broadcasted_iota(jnp.int32, (TILE, TILE), 0)
    cols = lax.broadcasted_iota(jnp.int32, (TILE, TILE), 1)
    for s in range(SLOTS):
        pack = parts[:, s].reshape(2 * TILE, TILE) * scale
        upper = jnp.where(rows < cols, pack[:TILE], 0.0)
        lower = jnp.where(rows > cols, pack[:TILE], 0.0)
        across = pack[TILE:]
        out[s, :TILE, :TILE] = upper - upper.T
        out[s, TILE:, TILE:] = lower - lower.T
        out[s, :TILE, TILE:] = across
        out[s, TILE:, :TILE] = -across.T


def unpack_call(parts, scale):
    return pl.pallas_call(
        lambda parts, out: unpack_kernel(scale, parts, out),
        out_shape=jax.ShapeDtypeStruct((SLOTS, BLOCK, BLOCK), f32),
        in_specs=[vmem()],
        cost_estimate=pl.CostEstimate(flops=10**6, bytes_accessed=10**6, transcendentals=0),
        name="unpack",
    )(parts)


def finish_kernel(own, a1, a2, b1, b2, out):
    half = own.shape[1] // 2
    for k in range(5):
        columns = slice(k * TILE, (k + 1) * TILE)
        out[:half, columns] = (own[k, :half] + a1[k] + a2[k]).astype(bf16)
        out[half:, columns] = (own[k, half:] + b1[k] + b2[k]).astype(bf16)


def finish_call(*parts):
    return pl.pallas_call(
        finish_kernel,
        out_shape=jax.ShapeDtypeStruct((parts[0].shape[1], 5 * TILE), bf16),
        in_specs=[vmem() for _ in range(5)],
        compiler_params=pltpu.CompilerParams(vmem_limit_bytes=16 * 2**20),
        cost_estimate=pl.CostEstimate(flops=FINISH, bytes_accessed=5 * 10**6, transcendentals=0),
        name="finish",
    )(*parts)


def turn(size, by):
    return [(i, (i + by) % size) for i in range(size)]


def exchange(parts):
    rows = parts.reshape(parts.shape[0], -1, parts.shape[-1])
    return lax.all_to_all(rows, ("x", "z"), 0, 0, tiled=True).reshape(parts.shape)


def local(activations, cotangent, frozen_weight, skew_params, tile_order, block_owner):
    place = jnp.stack([lax.axis_index("y"), lax.axis_index("core")]).astype(jnp.int32)
    turn_high, turn_low, high, low, mine, other = grad_call(
        tile_order, place, frozen_weight.T, cotangent.T, activations, skew_params
    )
    came = lax.ppermute(other, "core", turn(CORES, 1))
    far_a, far_b, next_a, next_b, last_a, last_b, own = rotate_call(
        tile_order, place, turn_high, turn_low, high, low
    )
    far_a = lax.ppermute(far_a, "y", turn(Y, 1))
    far_b = lax.ppermute(far_b, "y", turn(Y, -1))
    last_a = lax.ppermute(last_a, "y", turn(Y, -1))
    next_b = lax.ppermute(next_b, "y", turn(Y, 1))
    pack = adjoint_call(place, mine, came, skew_params)
    parts = exchange(pack)
    next_a, last_b = merge_call(next_a, far_a, last_b, far_b)
    parts, next_a, last_b = lax.optimization_barrier((parts, next_a, last_b))
    slices = sum_call(parts)
    slices, last_a, next_b = lax.optimization_barrier((slices, last_a, next_b))
    next_a = lax.ppermute(next_a, "y", turn(Y, 1))
    last_b = lax.ppermute(last_b, "y", turn(Y, -1))
    others = [lax.ppermute(slices, "y", turn(Y, s)) for s in (1, 2, 3)]
    slices = (slices + others[1]) + (others[0] + others[2])
    routed = route_call(block_owner, place, slices, lax.ppermute(slices, "core", turn(CORES, 1)))
    owned = exchange(routed)
    scale = 1.0 / math.sqrt(cotangent.shape[0] * X * Z * CORES)
    skew_grads = unpack_call(owned, scale)
    input_grad = finish_call(own, next_a, last_a, next_b, last_b)
    return (input_grad, skew_grads)


def solution(mesh):
    grid = Mesh(mesh.devices.reshape(X, Z, CORES, Y), ("x", "z", "core", "y"))
    dp = ("x", "z", "core")
    placed = (P(dp, None), P(dp, "y"), P(None, "y"), P(), P(), P())
    return jax.shard_map(
        local,
        mesh=grid,
        in_specs=placed,
        out_specs=(P(dp, "y"), P(dp, None, None)),
        check_vma=False,
    )
```

time: 146 us -> 108 us (0.74)
  local copies, waits for them, and re-layouts: 20 us -> 7.07 us
  waiting for transfers between devices: 49.3 us -> 38.9 us
  Pallas kernels: 38.8 us -> 30 us
  other arithmetic: 4.04 us -> 0.81 us
  starting transfers between devices: 31.7 us -> 29.9 us
    ppermute x3, waiting for transfers between devices: 14.4 us -> 0.01 us  [the longest x1 0.01 us: local(): next_a = lax.ppermute(next_a, 'y', turn(Y, 1))]
    unnamed x30 -> x22, local copies, waits for them, and re-layouts: 20 us -> 7.07 us
    all_to_all x2, waiting for transfers between devices: 17.3 us -> 28.6 us  [exchange(): lax.all_to_all(rows, ('x', 'z'), 0, 0, tiled=True).reshape(parts.shape)]
    ppermute x1, waiting for transfers between devices: 9.74 us -> 0.01 us  [local(): last_a = lax.ppermute(last_a, 'y', turn(Y, -1))]
    pallas_call x2 -> x5, Pallas kernels: 33.3 us -> 24.5 us  [the longest x1 12.5 us: grad_call(): pl.pallas_call(grad_kernel, out_shape=[turns, turns, part, part, gram, gr...]
    ppermute x3, waiting for transfers between devices: 3.25 us -> 9.07 us  [local(): others = [lax.ppermute(slices, 'y', turn(Y, s)) for s in (1, 2, 3)]]
    ppermute x1, waiting for transfers between devices: 3.39 us -> 0.01 us  [local(): next_b = lax.ppermute(next_b, 'y', turn(Y, 1))]
    add x3 -> x0, other arithmetic: 3.23 us -> none  [the longest x1 1.16 us: local(): next_a = lax.ppermute(next_a + far_a, 'y', turn(Y, 1))]
  transfers between devices with their start and end apart: 13 -> 13, of which waited for: 8 -> 6; matrix products, arithmetic and copies ran while one was open for 2% -> 1% of each run, Pallas kernels for 3% -> 14%
where the time goes in v2:
time: 108 us; the launch traced here: 107 us
  waiting for transfers between devices  38.9 us (36%)
  Pallas kernels  30 us (28%)
  starting transfers between devices  29.9 us (28%)
  local copies, waits for them, and re-layouts  7.07 us (7%)
    all_to_all x2, waiting for transfers between devices, exchange(): lax.all_to_all(rows, ('x', 'z'), 0, 0, tiled=True).reshape(parts.shape)  28.6 us
    all_to_all x2, starting transfers between devices, exchange(): lax.all_to_all(rows, ('x', 'z'), 0, 0, tiled=True).reshape(parts.shape)  18 us
    pallas_call x1, Pallas kernels, grad_call(): pl.pallas_call(grad_kernel, out_shape=[turns, turns, part, part, gram, gr...  12.5 us
    ppermute x3, waiting for transfers between devices, local(): others = [lax.ppermute(slices, 'y', turn(Y, s)) for s in (1, 2, 3)]  9.07 us
    unnamed x22, local copies, waits for them, and re-layouts  7.07 us
    pallas_call x1, Pallas kernels, rotate_call(): pl.pallas_call(rotate_kernel, out_shape=[half] * 6 + [jax.ShapeDtypeStruc...  4.65 us
    pallas_call x1, Pallas kernels, adjoint_call(): pl.pallas_call(adjoint_kernel, out_shape=jax.ShapeDtypeStruct((32, 5, 8,...  3.68 us
    ppermute x3, starting transfers between devices, local(): others = [lax.ppermute(slices, 'y', turn(Y, s)) for s in (1, 2, 3)]  3.21 us
  transfers between devices with their start and end apart: 13, of which 6 were waited for; matrix products, arithmetic and copies ran while one was open for 1% of the time, Pallas kernels for 14%

profile of v2, /device:TPU:32, one launch (start us, length us, event | category | flops | bytes accessed | tf_op | source)
XLA Modules:
  0.0 107.5 jit_solution(10158838244350215282)
XLA Ops:
  0.6 0.1 pad_add_fusion.place
  0.7 0.0 copy-start
  0.7 0.0 copy-start.1
  0.7 0.7 copy-done.1
  1.4 0.0 copy-start.2
  1.4 1.5 %copy-done.2 = bf16[512,1728]{0,1:T(8,128)(2,1)S(1)} copy-done((bf16[512,1728]{0,1:T(8,128)(2,1)S(1)}, bf16[512,1728]{0,1:T(8,128)(2,1)}, u32[]{:S(2)}) %copy-start.2) | copy-done | bytes 1769496
  2.8 0.0 copy-start.3
  2.8 1.3 %copy-done.3 = bf16[10,256,256]{2,1,0:T(8,128)(2,1)S(1)} copy-done((bf16[10,256,256]{2,1,0:T(8,128)(2,1)S(1)}, bf16[10,256,256]{2,1,0:T(8,128)(2,1)}, u32[]{:S(2)}) %copy-start.3) | copy-done | bytes 1310744
  4.2 12.5 %grad.1 = (bf16[10,256,256]{2,1,0:T(8,128)(2,1)S(1)}, bf16[10,256,256]{2,1,0:T(8,128)(2,1)S(1)}, bf16[10,512,256]{2,1,0:T(8,128)(2,1)S(1)}, bf16[10,512,256]{2,1...) custom-call(s32[20]{0:T(128)S(1)} %copy-done.1, s32[2]{0:T(128)S(1)} %pad_add_fusion.place, ...), custom_call_target="tpu_custom_call" | custom-call | flops 8000000000 | bytes 14000000 | tf_op jit(solution)/shard_map/grad/pallas_call | solution.py:117
  16.6 0.1 collective-permute-start
  16.7 4.6 %rotate.1 = (f32[5,256,128]{2,1,0:T(8,128)}, f32[5,256,128]{2,1,0:T(8,128)}, f32[5,256,128]{2,1,0:T(8,128)S(1)}, f32[5,256,128]{2,1,0:T(8,128)}, f32[5,256,128]{...) custom-call(s32[20]{0:T(128)S(1)} %copy-done.1, s32[2]{0:T(128)S(1)} %pad_add_fusion.place, ...), custom_call_target="tpu_custom_call" | custom-call | flops 2000000000 | bytes 10000000 | tf_op jit(solution)/shard_map/rotate/pallas_call | solution.py:156
  21.4 0.0 copy-start.5
  21.4 0.0 copy-start.7
  21.4 1.6 %collective-permute-start.1 = (f32[5,256,128]{2,1,0:T(8,128)}, f32[5,256,128]{2,1,0:T(8,128)}, u32[]{:S(2)}, u32[]{:S(2)}) collective-permute-start(f32[5,256,128]{2,1,0:T(8,128)} %get-tuple-element.31), channel_id=1, source_target_pairs={{0,1},{1,2},{2,3},{3,0},{4,5},{5,6},{6,7},{7,4},{8,9},{9,10},{10,1... | collective-permute-start | bytes 1966088 | tf_op jit(solution)/shard_map/ppermute | solution.py:321
  23.0 1.7 %collective-permute-start.2 = (f32[5,256,128]{2,1,0:T(8,128)}, f32[5,256,128]{2,1,0:T(8,128)}, u32[]{:S(2)}, u32[]{:S(2)}) collective-permute-start(f32[5,256,128]{2,1,0:T(8,128)} %get-tuple-element.33), channel_id=1, source_target_pairs={{0,3},{1,0},{2,1},{3,2},{4,7},{5,4},{6,5},{7,6},{8,11},{9,8},{10,9... | collective-permute-start | bytes 1966088 | tf_op jit(solution)/shard_map/ppermute | solution.py:322
  24.6 1.8 %collective-permute-start.4 = (f32[5,256,128]{2,1,0:T(8,128)}, f32[5,256,128]{2,1,0:T(8,128)S(1)}, u32[]{:S(2)}, u32[]{:S(2)}) collective-permute-start(f32[5,256,128]{2,1,0:T(8,128)} %get-tuple-element.38), channel_id=1, source_target_pairs={{0,3},{1,0},{2,1},{3,2},{4,7},{5,4},{6,5},{7,6},{8,11},{9,8},{10,9... | collective-permute-start | bytes 1966088 | tf_op jit(solution)/shard_map/ppermute | solution.py:323
  26.4 0.2 collective-permute-start.5
  26.7 0.0 collective-permute-done.came
  26.7 0.0 copy-done
  26.7 3.7 %adjoint.1 = f32[32,5,8,128]{3,2,1,0:T(8,128)} custom-call(s32[2]{0:T(128)S(1)} %pad_add_fusion.place, f32[5,256,256]{2,1,0:T(8,128)S(1)} %get-tuple-element.28.mine, f32[5,256,256]{2,1,0:T(8,128)S(1)} %collective-permute-done.came, bf16[10,256,256]{2,1,0:T(8,128)(2,1)S(1)} %copy-done.3), custom_call_target="tpu_custom_call" | custom-call | flops 2000000000 | bytes 4000000 | tf_op jit(solution)/shard_map/adjoint/pallas_call | solution.py:189
  30.3 0.0 copy-done.5
  30.3 0.0 copy-done.7
  30.3 11.2 %all-to-all-start = ((f32[32,40,128]{2,1,0:T(8,128)}), f32[32,40,128]{2,1,0:T(8,128)}, u32[]{:S(2)}, u32[]{:S(2)}) async-start(f32[32,40,128]{2,1,0:T(8,128)} %bitcast.4), calls=%async_computation | async-start | bytes 1310720 | tf_op jit(solution)/shard_map/all_to_all | solution.py:309
  41.6 0.0 collective-permute-done.1.far_a
  41.6 0.0 collective-permute-done.2.far_b
  41.6 0.0 copy-start.6
  41.6 1.1 %copy-done.6 = f32[5,256,128]{2,1,0:T(8,128)S(1)} copy-done((f32[5,256,128]{2,1,0:T(8,128)S(1)}, f32[5,256,128]{2,1,0:T(8,128)}, u32[]{:S(2)}) %copy-start.6) | copy-done | bytes 655384
  42.7 0.0 copy-start.8
  42.7 1.1 %copy-done.8 = f32[5,256,128]{2,1,0:T(8,128)S(1)} copy-done((f32[5,256,128]{2,1,0:T(8,128)S(1)}, f32[5,256,128]{2,1,0:T(8,128)}, u32[]{:S(2)}) %copy-start.8) | copy-done | bytes 655384
  43.8 1.4 %merge.1 = (f32[5,256,128]{2,1,0:T(8,128)S(1)}, f32[5,256,128]{2,1,0:T(8,128)S(1)}) custom-call(f32[5,256,128]{2,1,0:T(8,128)S(1)} %copy-done.6, f32[5,256,128]{2,1,0:T(8,128)} %collective-permute-done.1.far_a, f32[5,256,128]{2,1,0:T(8,128)S(1)} %copy-done.8, f32[5,256,128]{2,1,0:T(8,128)} %collective-permute-done.2.far_b), custom_call_target="tpu_custom_call" | custom-call | flops 20000000000 | bytes 4000000 | tf_op jit(solution)/shard_map/merge/pallas_call | solution.py:206
  45.2 0.0 copy-start.4
  45.2 0.8 copy-done.4
  46.0 15.6 %all-to-all-done = f32[32,40,128]{2,1,0:T(8,128)} async-done(((f32[32,40,128]{2,1,0:T(8,128)}), f32[32,40,128]{2,1,0:T(8,128)}, u32[]{:S(2)}, u32[]{:S(2)}) %all-to-all-start) | async-done | bytes 655392 | tf_op jit(solution)/shard_map/all_to_all | solution.py:309
  61.6 0.3 collective-permute-start.3
  61.9 2.9 %collective-permute-start.6 = (f32[5,256,128]{2,1,0:T(8,128)S(1)}, f32[5,256,128]{2,1,0:T(8,128)}, u32[]{:S(2)}, u32[]{:S(2)}) collective-permute-start(f32[5,256,128]{2,1,0:T(8,128)S(1)} %get-tuple-element.42), channel_id=1, source_target_pairs={{0,3},{1,0},{2,1},{3,2},{4,7},{5,4},{6,5},{7,6},{8,11},{9,8},{10,9... | collective-permute-start | bytes 1966088 | tf_op jit(solution)/shard_map/ppermute | solution.py:332
  64.8 1.7 %slice_sum.1 = f32[5,8,128]{2,1,0:T(8,128)} custom-call(f32[32,5,8,128]{3,2,1,0:T(8,128)} %bitcast.5.parts), custom_call_target="tpu_custom_call" | custom-call | flops 1000000 | bytes 1000000 | tf_op jit(solution)/shard_map/slice_sum/pallas_call | solution.py:225
  66.6 0.0 collective-permute-done.4.a2
  66.6 0.0 collective-permute-done.5.b1
  66.6 1.7 %collective-permute-start.9 = (f32[5,8,128]{2,1,0:T(8,128)}, f32[5,8,128]{2,1,0:T(8,128)S(1)}, u32[]{:S(2)}, u32[]{:S(2)}) collective-permute-start(f32[5,8,128]{2,1,0:T(8,128)} %slice_sum.1), channel_id=1, source_target_pairs={{0,3},{1,0},{2,1},{3,2},{4,7},{5,4},{6,5},{7,6},{8,11},{9,8},{10,9... | collective-permute-start | bytes 61448 | tf_op jit(solution)/shard_map/ppermute | solution.py:333
  68.3 0.4 collective-permute-start.8
  68.6 1.2 %collective-permute-start.7 = (f32[5,8,128]{2,1,0:T(8,128)}, f32[5,8,128]{2,1,0:T(8,128)S(1)}, u32[]{:S(2)}, u32[]{:S(2)}) collective-permute-start(f32[5,8,128]{2,1,0:T(8,128)} %slice_sum.1), channel_id=1, source_target_pairs={{0,2},{1,3},{2,0},{3,1},{4,6},{5,7},{6,4},{7,5},{8,10},{9,11},{10,... | collective-permute-start | bytes 61448 | tf_op jit(solution)/shard_map/ppermute | solution.py:333
  69.8 6.9 %collective-permute-done.9 = f32[5,8,128]{2,1,0:T(8,128)S(1)} collective-permute-done((f32[5,8,128]{2,1,0:T(8,128)}, f32[5,8,128]{2,1,0:T(8,128)S(1)}, u32[]{:S(2)}, u32[]{:S(2)}) %collective-permute-start.9) | collective-permute-done | bytes 20512 | tf_op jit(solution)/shard_map/ppermute | solution.py:333
  76.8 0.7 collective-permute-done.8
  77.5 1.4 %collective-permute-done.7 = f32[5,8,128]{2,1,0:T(8,128)S(1)} collective-permute-done((f32[5,8,128]{2,1,0:T(8,128)}, f32[5,8,128]{2,1,0:T(8,128)S(1)}, u32[]{:S(2)}, u32[]{:S(2)}) %collective-permute-start.7) | collective-permute-done | bytes 20512 | tf_op jit(solution)/shard_map/ppermute | solution.py:333
  78.9 0.7 add_add_fusion.own
  79.6 0.0 copy-start.9
  79.6 0.1 collective-permute-start.10
  79.7 1.2 %collective-permute-done.10.other = f32[5,8,128]{2,1,0:T(8,128)S(1)} collective-permute-done((f32[5,8,128]{2,1,0:T(8,128)S(1)}, f32[5,8,128]{2,1,0:T(8,128)S(1)}, u32[]{:S(2)}, u32[]{:S(2)}) %collective-permute-start.10) | collective-permute-done | bytes 20512 | tf_op jit(solution)/shard_map/ppermute | solution.py:335
  80.9 0.0 copy-done.9
  80.9 0.0 copy-start.10
  80.9 0.6 copy-done.10
  81.5 1.7 %route.1 = f32[32,3,8,128]{3,2,1,0:T(8,128)} custom-call(s32[10]{0:T(128)} %owner.1, s32[2]{0:T(128)} %copy-done, f32[5,8,128]{2,1,0:T(8,128)} %copy-done.9, f32[5,8,128]{2,1,0:T(8,128)} %copy-done.10), custom_call_target="tpu_custom_call" | custom-call | flops 100000 | bytes 1000000 | tf_op jit(solution)/shard_map/route/pallas_call | solution.py:250
  83.2 6.8 %all-to-all-start.1 = ((f32[32,24,128]{2,1,0:T(8,128)}), f32[32,24,128]{2,1,0:T(8,128)}, u32[]{:S(2)}, u32[]{:S(2)}) async-start(f32[32,24,128]{2,1,0:T(8,128)} %bitcast.9), calls=%async_computation.1 | async-start | bytes 786432 | tf_op jit(solution)/shard_map/all_to_all | solution.py:309
  90.0 0.0 collective-permute-done.3.a1
  90.0 0.0 collective-permute-done.6.b2
  90.0 2.3 %finish.1 = bf16[512,640]{1,0:T(8,128)(2,1)} custom-call(f32[5,512,128]{2,1,0:T(8,128)S(1)} %get-tuple-element.27.own, f32[5,256,128]{2,1,0:T(8,128)} %collective-permute-done.3.a1, f32[5,256,128]{2,1,0:T(8,128)S(1)} %collective-permute-done.4.a2, f32[5,256,128]{2,1,0:T(8,128)S(1)} %collective-permute-done.5.b1, f32[5,256,128]{2,1,0:T(8,128)} %collective-permute-done.6.b2), custom_call_target="tpu_custom_call" | custom-call | flops 10000000000 | bytes 5000000 | tf_op jit(solution)/shard_map/finish/pallas_call | solution.py:293
  92.3 13.1 %all-to-all-done.1 = f32[32,24,128]{2,1,0:T(8,128)} async-done(((f32[32,24,128]{2,1,0:T(8,128)}), f32[32,24,128]{2,1,0:T(8,128)}, u32[]{:S(2)}, u32[]{:S(2)}) %all-to-all-start.1) | async-done | bytes 393248 | tf_op jit(solution)/shard_map/all_to_all | solution.py:309
  105.4 2.1 %unpack.1 = f32[3,256,256]{2,1,0:T(8,128)} custom-call(f32[32,3,8,128]{3,2,1,0:T(8,128)} %bitcast.7.parts), custom_call_target="tpu_custom_call" | custom-call | flops 1000000 | bytes 1000000 | tf_op jit(solution)/shard_map/unpack/pallas_call | solution.py:275
Async XLA Ops:
  0.7 26.0 %copy-start = (s32[2]{0:T(128)}, s32[2]{0:T(128)S(1)}, u32[]{:S(2)}) copy-start(s32[2]{0:T(128)S(1)} %pad_add_fusion.place) | copy-start | bytes 28
  0.7 0.7 copy-start.1
  1.4 1.5 %copy-start.2 = (bf16[512,1728]{0,1:T(8,128)(2,1)S(1)}, bf16[512,1728]{0,1:T(8,128)(2,1)}, u32[]{:S(2)}) copy-start(bf16[512,1728]{0,1:T(8,128)(2,1)} %param.7) | copy-start | bytes 5308420
  2.8 1.3 %copy-start.3 = (bf16[10,256,256]{2,1,0:T(8,128)(2,1)S(1)}, bf16[10,256,256]{2,1,0:T(8,128)(2,1)}, u32[]{:S(2)}) copy-start(bf16[10,256,256]{2,1,0:T(8,128)(2,1)} %skew.3) | copy-start | bytes 3932164
  16.6 10.0 %collective-permute-start = (f32[5,256,256]{2,1,0:T(8,128)S(1)}, f32[5,256,256]{2,1,0:T(8,128)S(1)}, u32[]{:S(2)}, u32[]{:S(2)}) collective-permute-start(f32[5,256,256]{2,1,0:T(8,128)S(1)} %get-tuple-element.29), channel_id=1, source_target_pairs={{0,4},{4,0},{1,5},{5,1},{2,6},{6,2},{3,7},{7,3},{8,12},{12,8},{9,1... | collective-permute-start | bytes 3932168 | tf_op jit(solution)/shard_map/ppermute | solution.py:317
  21.4 9.0 %copy-start.5 = (f32[5,256,128]{2,1,0:T(8,128)}, f32[5,256,128]{2,1,0:T(8,128)S(1)}, u32[]{:S(2)}) copy-start(f32[5,256,128]{2,1,0:T(8,128)S(1)} %get-tuple-element.30.next_a) | copy-start | bytes 1966084
  21.4 9.0 %copy-start.7 = (f32[5,256,128]{2,1,0:T(8,128)}, f32[5,256,128]{2,1,0:T(8,128)S(1)}, u32[]{:S(2)}) copy-start(f32[5,256,128]{2,1,0:T(8,128)S(1)} %get-tuple-element.32.last_b) | copy-start | bytes 1966084
  21.4 20.2 %collective-permute-start.1 = (f32[5,256,128]{2,1,0:T(8,128)}, f32[5,256,128]{2,1,0:T(8,128)}, u32[]{:S(2)}, u32[]{:S(2)}) collective-permute-start(f32[5,256,128]{2,1,0:T(8,128)} %get-tuple-element.31), channel_id=1, source_target_pairs={{0,1},{1,2},{2,3},{3,0},{4,5},{5,6},{6,7},{7,4},{8,9},{9,10},{10,1... | collective-permute-start | bytes 1966088 | tf_op jit(solution)/shard_map/ppermute | solution.py:321
  23.0 18.6 %collective-permute-start.2 = (f32[5,256,128]{2,1,0:T(8,128)}, f32[5,256,128]{2,1,0:T(8,128)}, u32[]{:S(2)}, u32[]{:S(2)}) collective-permute-start(f32[5,256,128]{2,1,0:T(8,128)} %get-tuple-element.33), channel_id=1, source_target_pairs={{0,3},{1,0},{2,1},{3,2},{4,7},{5,4},{6,5},{7,6},{8,11},{9,8},{10,9... | collective-permute-start | bytes 1966088 | tf_op jit(solution)/shard_map/ppermute | solution.py:322
  24.6 42.0 %collective-permute-start.4 = (f32[5,256,128]{2,1,0:T(8,128)}, f32[5,256,128]{2,1,0:T(8,128)S(1)}, u32[]{:S(2)}, u32[]{:S(2)}) collective-permute-start(f32[5,256,128]{2,1,0:T(8,128)} %get-tuple-element.38), channel_id=1, source_target_pairs={{0,3},{1,0},{2,1},{3,2},{4,7},{5,4},{6,5},{7,6},{8,11},{9,8},{10,9... | collective-permute-start | bytes 1966088 | tf_op jit(solution)/shard_map/ppermute | solution.py:323
  26.4 40.2 %collective-permute-start.5 = (f32[5,256,128]{2,1,0:T(8,128)}, f32[5,256,128]{2,1,0:T(8,128)S(1)}, u32[]{:S(2)}, u32[]{:S(2)}) collective-permute-start(f32[5,256,128]{2,1,0:T(8,128)} %get-tuple-element.39), channel_id=1, source_target_pairs={{0,1},{1,2},{2,3},{3,0},{4,5},{5,6},{6,7},{7,4},{8,9},{9,10},{10,1... | collective-permute-start | bytes 1966088 | tf_op jit(solution)/shard_map/ppermute | solution.py:324
  30.3 31.3 %all-to-all-start = ((f32[32,40,128]{2,1,0:T(8,128)}), f32[32,40,128]{2,1,0:T(8,128)}, u32[]{:S(2)}, u32[]{:S(2)}) async-start(f32[32,40,128]{2,1,0:T(8,128)} %bitcast.4), calls=%async_computation | async-start | bytes 1310720 | tf_op jit(solution)/shard_map/all_to_all | solution.py:309
  41.6 1.1 %copy-start.6 = (f32[5,256,128]{2,1,0:T(8,128)S(1)}, f32[5,256,128]{2,1,0:T(8,128)}, u32[]{:S(2)}) copy-start(f32[5,256,128]{2,1,0:T(8,128)} %copy-done.5) | copy-start | bytes 1966084
  42.7 1.1 %copy-start.8 = (f32[5,256,128]{2,1,0:T(8,128)S(1)}, f32[5,256,128]{2,1,0:T(8,128)}, u32[]{:S(2)}) copy-start(f32[5,256,128]{2,1,0:T(8,128)} %copy-done.7) | copy-start | bytes 1966084
  45.2 0.8 copy-start.4
  61.6 28.4 %collective-permute-start.3 = (f32[5,256,128]{2,1,0:T(8,128)}, f32[5,256,128]{2,1,0:T(8,128)}, u32[]{:S(2)}, u32[]{:S(2)}) collective-permute-start(f32[5,256,128]{2,1,0:T(8,128)} %copy-done.4), channel_id=1, source_target_pairs={{0,1},{1,2},{2,3},{3,0},{4,5},{5,6},{6,7},{7,4},{8,9},{9,10},{10,1... | collective-permute-start | bytes 1966088 | tf_op jit(solution)/shard_map/ppermute | solution.py:331
  61.9 28.1 %collective-permute-start.6 = (f32[5,256,128]{2,1,0:T(8,128)S(1)}, f32[5,256,128]{2,1,0:T(8,128)}, u32[]{:S(2)}, u32[]{:S(2)}) collective-permute-start(f32[5,256,128]{2,1,0:T(8,128)S(1)} %get-tuple-element.42), channel_id=1, source_target_pairs={{0,3},{1,0},{2,1},{3,2},{4,7},{5,4},{6,5},{7,6},{8,11},{9,8},{10,9... | collective-permute-start | bytes 1966088 | tf_op jit(solution)/shard_map/ppermute | solution.py:332
  66.6 10.2 %collective-permute-start.9 = (f32[5,8,128]{2,1,0:T(8,128)}, f32[5,8,128]{2,1,0:T(8,128)S(1)}, u32[]{:S(2)}, u32[]{:S(2)}) collective-permute-start(f32[5,8,128]{2,1,0:T(8,128)} %slice_sum.1), channel_id=1, source_target_pairs={{0,3},{1,0},{2,1},{3,2},{4,7},{5,4},{6,5},{7,6},{8,11},{9,8},{10,9... | collective-permute-start | bytes 61448 | tf_op jit(solution)/shard_map/ppermute | solution.py:333
  68.3 9.2 %collective-permute-start.8 = (f32[5,8,128]{2,1,0:T(8,128)}, f32[5,8,128]{2,1,0:T(8,128)S(1)}, u32[]{:S(2)}, u32[]{:S(2)}) collective-permute-start(f32[5,8,128]{2,1,0:T(8,128)} %slice_sum.1), channel_id=1, source_target_pairs={{0,1},{1,2},{2,3},{3,0},{4,5},{5,6},{6,7},{7,4},{8,9},{9,10},{10,1... | collective-permute-start | bytes 61448 | tf_op jit(solution)/shard_map/ppermute | solution.py:333
  68.6 10.3 %collective-permute-start.7 = (f32[5,8,128]{2,1,0:T(8,128)}, f32[5,8,128]{2,1,0:T(8,128)S(1)}, u32[]{:S(2)}, u32[]{:S(2)}) collective-permute-start(f32[5,8,128]{2,1,0:T(8,128)} %slice_sum.1), channel_id=1, source_target_pairs={{0,2},{1,3},{2,0},{3,1},{4,6},{5,7},{6,4},{7,5},{8,10},{9,11},{10,... | collective-permute-start | bytes 61448 | tf_op jit(solution)/shard_map/ppermute | solution.py:333
  79.6 1.3 %copy-start.9 = (f32[5,8,128]{2,1,0:T(8,128)}, f32[5,8,128]{2,1,0:T(8,128)S(1)}, u32[]{:S(2)}) copy-start(f32[5,8,128]{2,1,0:T(8,128)S(1)} %add_add_fusion.own) | copy-start | bytes 61444
  79.6 1.3 %collective-permute-start.10 = (f32[5,8,128]{2,1,0:T(8,128)S(1)}, f32[5,8,128]{2,1,0:T(8,128)S(1)}, u32[]{:S(2)}, u32[]{:S(2)}) collective-permute-start(f32[5,8,128]{2,1,0:T(8,128)S(1)} %add_add_fusion.own), channel_id=1, source_target_pairs={{0,4},{4,0},{1,5},{5,1},{2,6},{6,2},{3,7},{7,3},{8,12},{12,8},{9,1... | collective-permute-start | bytes 61448 | tf_op jit(solution)/shard_map/ppermute | solution.py:335
  80.9 0.6 copy-start.10
  83.2 22.2 %all-to-all-start.1 = ((f32[32,24,128]{2,1,0:T(8,128)}), f32[32,24,128]{2,1,0:T(8,128)}, u32[]{:S(2)}, u32[]{:S(2)}) async-start(f32[32,24,128]{2,1,0:T(8,128)} %bitcast.9), calls=%async_computation.1 | async-start | bytes 786432 | tf_op jit(solution)/shard_map/all_to_all | solution.py:309

commit v3 on v2

--- a/solution.py
+++ b/solution.py
@@ -10,7 +10,7 @@
 
 SLOTS = 3
 FINISH = 10**10
-MERGE = int(2e10)
+MERGE = 10**10
 X, Z, CORES, Y = 4, 8, 2, 4
 TILE = 128
 BLOCK = 256
@@ -327,11 +327,11 @@
     next_a, last_b = merge_call(next_a, far_a, last_b, far_b)
     parts, next_a, last_b = lax.optimization_barrier((parts, next_a, last_b))
     slices = sum_call(parts)
-    slices, last_a, next_b = lax.optimization_barrier((slices, last_a, next_b))
+    others = [lax.ppermute(slices, "y", turn(Y, s)) for s in (1, 2, 3)]
+    slices = (slices + others[1]) + (others[0] + others[2])
+    slices, next_a, last_b, last_a, next_b = lax.optimization_barrier((slices, next_a, last_b, last_a, next_b))
     next_a = lax.ppermute(next_a, "y", turn(Y, 1))
     last_b = lax.ppermute(last_b, "y", turn(Y, -1))
-    others = [lax.ppermute(slices, "y", turn(Y, s)) for s in (1, 2, 3)]
-    slices = (slices + others[1]) + (others[0] + others[2])
     routed = route_call(block_owner, place, slices, lax.ppermute(slices, "core", turn(CORES, 1)))
     owned = exchange(routed)
     scale = 1.0 / math.sqrt(cotangent.shape[0] * X * Z * CORES)

time: 108 us -> 100 us (0.926)
  waiting for transfers between devices: 38.9 us -> 31.8 us
  starting transfers between devices: 29.9 us -> 28.7 us
    ppermute x3, waiting for transfers between devices: 9.07 us -> 3.89 us  [local(): others = [lax.ppermute(slices, 'y', turn(Y, s)) for s in (1, 2, 3)]]
    all_to_all x2, waiting for transfers between devices: 28.6 us -> 23.9 us  [exchange(): lax.all_to_all(rows, ('x', 'z'), 0, 0, tiled=True).reshape(parts.shape)]
    ppermute x1, waiting for transfers between devices: 0.01 us -> 2.78 us  [local(): next_a = lax.ppermute(next_a, 'y', turn(Y, 1))]
    all_to_all x2, starting transfers between devices: 18 us -> 16.2 us  [exchange(): lax.all_to_all(rows, ('x', 'z'), 0, 0, tiled=True).reshape(parts.shape)]
    unnamed x22 -> x24, local copies, waits for them, and re-layouts: 7.07 us -> 7.9 us
  transfers between devices with their start and end apart: 13 -> 13, of which waited for: 6 -> 7; matrix products, arithmetic and copies ran while one was open for 1% -> 1% of each run, Pallas kernels for 14% -> 15%
where the time goes in v3:
time: 100 us; the launch traced here: 99.5 us
  waiting for transfers between devices  31.8 us (32%)
  Pallas kernels  29.7 us (30%)
  starting transfers between devices  28.7 us (29%)
  local copies, waits for them, and re-layouts  7.9 us (8%)
    all_to_all x2, waiting for transfers between devices, exchange(): lax.all_to_all(rows, ('x', 'z'), 0, 0, tiled=True).reshape(parts.shape)  23.9 us
    all_to_all x2, starting transfers between devices, exchange(): lax.all_to_all(rows, ('x', 'z'), 0, 0, tiled=True).reshape(parts.shape)  16.2 us
    pallas_call x1, Pallas kernels, grad_call(): pl.pallas_call(grad_kernel, out_shape=[turns, turns, part, part, gram, gr...  12.5 us
    unnamed x24, local copies, waits for them, and re-layouts  7.9 us
    pallas_call x1, Pallas kernels, rotate_call(): pl.pallas_call(rotate_kernel, out_shape=[half] * 6 + [jax.ShapeDtypeStruc...  4.49 us
    ppermute x3, waiting for transfers between devices, local(): others = [lax.ppermute(slices, 'y', turn(Y, s)) for s in (1, 2, 3)]  3.89 us
    pallas_call x1, Pallas kernels, adjoint_call(): pl.pallas_call(adjoint_kernel, out_shape=jax.ShapeDtypeStruct((32, 5, 8,...  3.67 us
    ppermute x3, starting transfers between devices, local(): others = [lax.ppermute(slices, 'y', turn(Y, s)) for s in (1, 2, 3)]  3.63 us
  transfers between devices with their start and end apart: 13, of which 7 were waited for; matrix products, arithmetic and copies ran while one was open for 1% of the time, Pallas kernels for 15%

profile of v3, /device:TPU:32, one launch (start us, length us, event | category | flops | bytes accessed | tf_op | source)
XLA Modules:
  0.0 99.5 jit_solution(11633323131448955166)
XLA Ops:
  0.6 0.1 pad_add_fusion.place
  0.7 0.0 copy-start
  0.7 0.0 copy-start.1
  0.7 0.7 copy-done.1
  1.4 0.0 copy-start.2
  1.4 1.5 %copy-done.2 = bf16[512,1728]{0,1:T(8,128)(2,1)S(1)} copy-done((bf16[512,1728]{0,1:T(8,128)(2,1)S(1)}, bf16[512,1728]{0,1:T(8,128)(2,1)}, u32[]{:S(2)}) %copy-start.2) | copy-done | bytes 1769496
  2.8 0.0 copy-start.3
  2.8 1.3 %copy-done.3 = bf16[10,256,256]{2,1,0:T(8,128)(2,1)S(1)} copy-done((bf16[10,256,256]{2,1,0:T(8,128)(2,1)S(1)}, bf16[10,256,256]{2,1,0:T(8,128)(2,1)}, u32[]{:S(2)}) %copy-start.3) | copy-done | bytes 1310744
  4.2 12.5 %grad.1 = (bf16[10,256,256]{2,1,0:T(8,128)(2,1)S(1)}, bf16[10,256,256]{2,1,0:T(8,128)(2,1)S(1)}, bf16[10,512,256]{2,1,0:T(8,128)(2,1)S(1)}, bf16[10,512,256]{2,1...) custom-call(s32[20]{0:T(128)S(1)} %copy-done.1, s32[2]{0:T(128)S(1)} %pad_add_fusion.place, ...), custom_call_target="tpu_custom_call" | custom-call | flops 8000000000 | bytes 14000000 | tf_op jit(solution)/shard_map/grad/pallas_call | solution.py:117
  16.6 0.1 collective-permute-start
  16.7 4.5 %rotate.1 = (f32[5,256,128]{2,1,0:T(8,128)}, f32[5,256,128]{2,1,0:T(8,128)}, f32[5,256,128]{2,1,0:T(8,128)S(1)}, f32[5,256,128]{2,1,0:T(8,128)S(1)}, f32[5,256,1...) custom-call(s32[20]{0:T(128)S(1)} %copy-done.1, s32[2]{0:T(128)S(1)} %pad_add_fusion.place, ...), custom_call_target="tpu_custom_call" | custom-call | flops 2000000000 | bytes 10000000 | tf_op jit(solution)/shard_map/rotate/pallas_call | solution.py:156
  21.2 0.0 copy-start.6
  21.2 0.0 copy-start.8
  21.2 1.6 %collective-permute-start.1 = (f32[5,256,128]{2,1,0:T(8,128)}, f32[5,256,128]{2,1,0:T(8,128)}, u32[]{:S(2)}, u32[]{:S(2)}) collective-permute-start(f32[5,256,128]{2,1,0:T(8,128)} %get-tuple-element.33), channel_id=1, source_target_pairs={{0,1},{1,2},{2,3},{3,0},{4,5},{5,6},{6,7},{7,4},{8,9},{9,10},{10,1... | collective-permute-start | bytes 1966088 | tf_op jit(solution)/shard_map/ppermute | solution.py:321
  22.8 1.7 %collective-permute-start.2 = (f32[5,256,128]{2,1,0:T(8,128)}, f32[5,256,128]{2,1,0:T(8,128)}, u32[]{:S(2)}, u32[]{:S(2)}) collective-permute-start(f32[5,256,128]{2,1,0:T(8,128)} %get-tuple-element.35), channel_id=1, source_target_pairs={{0,3},{1,0},{2,1},{3,2},{4,7},{5,4},{6,5},{7,6},{8,11},{9,8},{10,9... | collective-permute-start | bytes 1966088 | tf_op jit(solution)/shard_map/ppermute | solution.py:322
  24.5 0.0 collective-permute-done.came
  24.5 0.0 copy-done
  24.5 3.7 %adjoint.1 = f32[32,5,8,128]{3,2,1,0:T(8,128)} custom-call(s32[2]{0:T(128)S(1)} %pad_add_fusion.place, f32[5,256,256]{2,1,0:T(8,128)S(1)} %get-tuple-element.30.mine, f32[5,256,256]{2,1,0:T(8,128)S(1)} %collective-permute-done.came, bf16[10,256,256]{2,1,0:T(8,128)(2,1)S(1)} %copy-done.3), custom_call_target="tpu_custom_call" | custom-call | flops 2000000000 | bytes 4000000 | tf_op jit(solution)/shard_map/adjoint/pallas_call | solution.py:189
  28.2 0.0 copy-done.6
  28.2 0.0 copy-done.8
  28.2 11.2 %all-to-all-start = ((f32[32,40,128]{2,1,0:T(8,128)}), f32[32,40,128]{2,1,0:T(8,128)}, u32[]{:S(2)}, u32[]{:S(2)}) async-start(f32[32,40,128]{2,1,0:T(8,128)} %bitcast.4), calls=%async_computation | async-start | bytes 1310720 | tf_op jit(solution)/shard_map/all_to_all | solution.py:309
  39.4 1.8 %collective-permute-start.6 = (f32[5,256,128]{2,1,0:T(8,128)}, f32[5,256,128]{2,1,0:T(8,128)S(1)}, u32[]{:S(2)}, u32[]{:S(2)}) collective-permute-start(f32[5,256,128]{2,1,0:T(8,128)} %get-tuple-element.41), channel_id=1, source_target_pairs={{0,3},{1,0},{2,1},{3,2},{4,7},{5,4},{6,5},{7,6},{8,11},{9,8},{10,9... | collective-permute-start | bytes 1966088 | tf_op jit(solution)/shard_map/ppermute | solution.py:323
  41.3 0.3 collective-permute-start.7
  41.5 0.0 collective-permute-done.1.far_a
  41.5 0.0 collective-permute-done.2.far_b
  41.5 0.0 copy-start.7
  41.5 1.1 %copy-done.7 = f32[5,256,128]{2,1,0:T(8,128)S(1)} copy-done((f32[5,256,128]{2,1,0:T(8,128)S(1)}, f32[5,256,128]{2,1,0:T(8,128)}, u32[]{:S(2)}) %copy-start.7) | copy-done | bytes 655384
  42.6 0.0 copy-start.9
  42.6 1.1 %copy-done.9 = f32[5,256,128]{2,1,0:T(8,128)S(1)} copy-done((f32[5,256,128]{2,1,0:T(8,128)S(1)}, f32[5,256,128]{2,1,0:T(8,128)}, u32[]{:S(2)}) %copy-start.9) | copy-done | bytes 655384
  43.7 1.4 %merge.1 = (f32[5,256,128]{2,1,0:T(8,128)S(1)}, f32[5,256,128]{2,1,0:T(8,128)S(1)}) custom-call(f32[5,256,128]{2,1,0:T(8,128)S(1)} %copy-done.7, f32[5,256,128]{2,1,0:T(8,128)} %collective-permute-done.1.far_a, f32[5,256,128]{2,1,0:T(8,128)S(1)} %copy-done.9, f32[5,256,128]{2,1,0:T(8,128)} %collective-permute-done.2.far_b), custom_call_target="tpu_custom_call" | custom-call | flops 10000000000 | bytes 4000000 | tf_op jit(solution)/shard_map/merge/pallas_call | solution.py:206
  45.1 0.0 copy-start.4
  45.1 0.8 copy-done.4
  46.0 0.0 copy-start.5
  46.0 0.8 copy-done.5
  46.8 13.4 %all-to-all-done = f32[32,40,128]{2,1,0:T(8,128)} async-done(((f32[32,40,128]{2,1,0:T(8,128)}), f32[32,40,128]{2,1,0:T(8,128)}, u32[]{:S(2)}, u32[]{:S(2)}) %all-to-all-start) | async-done | bytes 655392 | tf_op jit(solution)/shard_map/all_to_all | solution.py:309
  60.2 1.7 %slice_sum.1 = f32[5,8,128]{2,1,0:T(8,128)} custom-call(f32[32,5,8,128]{3,2,1,0:T(8,128)} %bitcast.5.parts), custom_call_target="tpu_custom_call" | custom-call | flops 1000000 | bytes 1000000 | tf_op jit(solution)/shard_map/slice_sum/pallas_call | solution.py:225
  61.9 1.4 %collective-permute-start.5 = (f32[5,8,128]{2,1,0:T(8,128)}, f32[5,8,128]{2,1,0:T(8,128)S(1)}, u32[]{:S(2)}, u32[]{:S(2)}) collective-permute-start(f32[5,8,128]{2,1,0:T(8,128)} %slice_sum.1), channel_id=1, source_target_pairs={{0,3},{1,0},{2,1},{3,2},{4,7},{5,4},{6,5},{7,6},{8,11},{9,8},{10,9... | collective-permute-start | bytes 61448 | tf_op jit(solution)/shard_map/ppermute | solution.py:330
  63.3 0.6 collective-permute-start.4
  63.9 1.6 %collective-permute-start.3 = (f32[5,8,128]{2,1,0:T(8,128)}, f32[5,8,128]{2,1,0:T(8,128)S(1)}, u32[]{:S(2)}, u32[]{:S(2)}) collective-permute-start(f32[5,8,128]{2,1,0:T(8,128)} %slice_sum.1), channel_id=1, source_target_pairs={{0,2},{1,3},{2,0},{3,1},{4,6},{5,7},{6,4},{7,5},{8,10},{9,11},{10,... | collective-permute-start | bytes 61448 | tf_op jit(solution)/shard_map/ppermute | solution.py:330
  65.5 0.4 collective-permute-done.5
  65.9 2.6 %collective-permute-done.4 = f32[5,8,128]{2,1,0:T(8,128)S(1)} collective-permute-done((f32[5,8,128]{2,1,0:T(8,128)}, f32[5,8,128]{2,1,0:T(8,128)S(1)}, u32[]{:S(2)}, u32[]{:S(2)}) %collective-permute-start.4) | collective-permute-done | bytes 20512 | tf_op jit(solution)/shard_map/ppermute | solution.py:330
  68.5 0.9 collective-permute-done.3
  69.4 0.7 add_add_fusion.own
  70.2 0.0 copy-start.10
  70.2 0.0 collective-permute-done.6.a2
  70.2 0.0 collective-permute-done.7.b1
  70.2 0.1 collective-permute-start.8
  70.3 3.2 %collective-permute-start.9 = (f32[5,256,128]{2,1,0:T(8,128)}, f32[5,256,128]{2,1,0:T(8,128)}, u32[]{:S(2)}, u32[]{:S(2)}) collective-permute-start(f32[5,256,128]{2,1,0:T(8,128)} %copy-done.4), channel_id=1, source_target_pairs={{0,3},{1,0},{2,1},{3,2},{4,7},{5,4},{6,5},{7,6},{8,11},{9,8},{10,9... | collective-permute-start | bytes 1966088 | tf_op jit(solution)/shard_map/ppermute | solution.py:334
  73.5 0.0 collective-permute-start.10
  73.5 1.2 %collective-permute-done.10.other = f32[5,8,128]{2,1,0:T(8,128)S(1)} collective-permute-done((f32[5,8,128]{2,1,0:T(8,128)S(1)}, f32[5,8,128]{2,1,0:T(8,128)S(1)}, u32[]{:S(2)}, u32[]{:S(2)}) %collective-permute-start.10) | collective-permute-done | bytes 20512 | tf_op jit(solution)/shard_map/ppermute | solution.py:335
  74.7 0.0 copy-done.10
  74.7 0.0 copy-start.11
  74.7 0.6 copy-done.11
  75.3 1.7 %route.1 = f32[32,3,8,128]{3,2,1,0:T(8,128)} custom-call(s32[10]{0:T(128)} %owner.1, s32[2]{0:T(128)} %copy-done, f32[5,8,128]{2,1,0:T(8,128)} %copy-done.10, f32[5,8,128]{2,1,0:T(8,128)} %copy-done.11), custom_call_target="tpu_custom_call" | custom-call | flops 100000 | bytes 1000000 | tf_op jit(solution)/shard_map/route/pallas_call | solution.py:250
  77.0 5.0 %all-to-all-start.1 = ((f32[32,24,128]{2,1,0:T(8,128)}), f32[32,24,128]{2,1,0:T(8,128)}, u32[]{:S(2)}, u32[]{:S(2)}) async-start(f32[32,24,128]{2,1,0:T(8,128)} %bitcast.9), calls=%async_computation.1 | async-start | bytes 786432 | tf_op jit(solution)/shard_map/all_to_all | solution.py:309
  82.0 2.8 %collective-permute-done.8.a1 = f32[5,256,128]{2,1,0:T(8,128)S(1)} collective-permute-done((f32[5,256,128]{2,1,0:T(8,128)}, f32[5,256,128]{2,1,0:T(8,128)S(1)}, u32[]{:S(2)}, u32[]{:S(2)}) %collective-permute-start.8) | collective-permute-done | bytes 655392 | tf_op jit(solution)/shard_map/ppermute | solution.py:333
  84.8 0.0 collective-permute-done.9.b2
  84.8 2.1 %finish.1 = bf16[512,640]{1,0:T(8,128)(2,1)} custom-call(f32[5,512,128]{2,1,0:T(8,128)S(1)} %get-tuple-element.29.own, f32[5,256,128]{2,1,0:T(8,128)S(1)} %collective-permute-done.8.a1, f32[5,256,128]{2,1,0:T(8,128)S(1)} %collective-permute-done.6.a2, f32[5,256,128]{2,1,0:T(8,128)S(1)} %collective-permute-done.7.b1, f32[5,256,128]{2,1,0:T(8,128)} %collective-permute-done.9.b2), custom_call_target="tpu_custom_call" | custom-call | flops 10000000000 | bytes 5000000 | tf_op jit(solution)/shard_map/finish/pallas_call | solution.py:293
  86.9 10.5 %all-to-all-done.1 = f32[32,24,128]{2,1,0:T(8,128)} async-done(((f32[32,24,128]{2,1,0:T(8,128)}), f32[32,24,128]{2,1,0:T(8,128)}, u32[]{:S(2)}, u32[]{:S(2)}) %all-to-all-start.1) | async-done | bytes 393248 | tf_op jit(solution)/shard_map/all_to_all | solution.py:309
  97.4 2.1 %unpack.1 = f32[3,256,256]{2,1,0:T(8,128)} custom-call(f32[32,3,8,128]{3,2,1,0:T(8,128)} %bitcast.7.parts), custom_call_target="tpu_custom_call" | custom-call | flops 1000000 | bytes 1000000 | tf_op jit(solution)/shard_map/unpack/pallas_call | solution.py:275
Async XLA Ops:
  0.7 23.8 %copy-start = (s32[2]{0:T(128)}, s32[2]{0:T(128)S(1)}, u32[]{:S(2)}) copy-start(s32[2]{0:T(128)S(1)} %pad_add_fusion.place) | copy-start | bytes 28
  0.7 0.7 copy-start.1
  1.4 1.5 %copy-start.2 = (bf16[512,1728]{0,1:T(8,128)(2,1)S(1)}, bf16[512,1728]{0,1:T(8,128)(2,1)}, u32[]{:S(2)}) copy-start(bf16[512,1728]{0,1:T(8,128)(2,1)} %param.7) | copy-start | bytes 5308420
  2.8 1.3 %copy-start.3 = (bf16[10,256,256]{2,1,0:T(8,128)(2,1)S(1)}, bf16[10,256,256]{2,1,0:T(8,128)(2,1)}, u32[]{:S(2)}) copy-start(bf16[10,256,256]{2,1,0:T(8,128)(2,1)} %skew.3) | copy-start | bytes 3932164
  16.6 7.9 %collective-permute-start = (f32[5,256,256]{2,1,0:T(8,128)S(1)}, f32[5,256,256]{2,1,0:T(8,128)S(1)}, u32[]{:S(2)}, u32[]{:S(2)}) collective-permute-start(f32[5,256,256]{2,1,0:T(8,128)S(1)} %get-tuple-element.31), channel_id=1, source_target_pairs={{0,4},{4,0},{1,5},{5,1},{2,6},{6,2},{3,7},{7,3},{8,12},{12,8},{9,1... | collective-permute-start | bytes 3932168 | tf_op jit(solution)/shard_map/ppermute | solution.py:317
  21.2 7.0 %copy-start.6 = (f32[5,256,128]{2,1,0:T(8,128)}, f32[5,256,128]{2,1,0:T(8,128)S(1)}, u32[]{:S(2)}) copy-start(f32[5,256,128]{2,1,0:T(8,128)S(1)} %get-tuple-element.32.next_a) | copy-start | bytes 1966084
  21.2 7.0 %copy-start.8 = (f32[5,256,128]{2,1,0:T(8,128)}, f32[5,256,128]{2,1,0:T(8,128)S(1)}, u32[]{:S(2)}) copy-start(f32[5,256,128]{2,1,0:T(8,128)S(1)} %get-tuple-element.34.last_b) | copy-start | bytes 1966084
  21.2 20.3 %collective-permute-start.1 = (f32[5,256,128]{2,1,0:T(8,128)}, f32[5,256,128]{2,1,0:T(8,128)}, u32[]{:S(2)}, u32[]{:S(2)}) collective-permute-start(f32[5,256,128]{2,1,0:T(8,128)} %get-tuple-element.33), channel_id=1, source_target_pairs={{0,1},{1,2},{2,3},{3,0},{4,5},{5,6},{6,7},{7,4},{8,9},{9,10},{10,1... | collective-permute-start | bytes 1966088 | tf_op jit(solution)/shard_map/ppermute | solution.py:321
  22.8 18.7 %collective-permute-start.2 = (f32[5,256,128]{2,1,0:T(8,128)}, f32[5,256,128]{2,1,0:T(8,128)}, u32[]{:S(2)}, u32[]{:S(2)}) collective-permute-start(f32[5,256,128]{2,1,0:T(8,128)} %get-tuple-element.35), channel_id=1, source_target_pairs={{0,3},{1,0},{2,1},{3,2},{4,7},{5,4},{6,5},{7,6},{8,11},{9,8},{10,9... | collective-permute-start | bytes 1966088 | tf_op jit(solution)/shard_map/ppermute | solution.py:322
  28.2 32.0 %all-to-all-start = ((f32[32,40,128]{2,1,0:T(8,128)}), f32[32,40,128]{2,1,0:T(8,128)}, u32[]{:S(2)}, u32[]{:S(2)}) async-start(f32[32,40,128]{2,1,0:T(8,128)} %bitcast.4), calls=%async_computation | async-start | bytes 1310720 | tf_op jit(solution)/shard_map/all_to_all | solution.py:309
  39.4 30.8 %collective-permute-start.6 = (f32[5,256,128]{2,1,0:T(8,128)}, f32[5,256,128]{2,1,0:T(8,128)S(1)}, u32[]{:S(2)}, u32[]{:S(2)}) collective-permute-start(f32[5,256,128]{2,1,0:T(8,128)} %get-tuple-element.41), channel_id=1, source_target_pairs={{0,3},{1,0},{2,1},{3,2},{4,7},{5,4},{6,5},{7,6},{8,11},{9,8},{10,9... | collective-permute-start | bytes 1966088 | tf_op jit(solution)/shard_map/ppermute | solution.py:323
  41.3 28.9 %collective-permute-start.7 = (f32[5,256,128]{2,1,0:T(8,128)S(1)}, f32[5,256,128]{2,1,0:T(8,128)S(1)}, u32[]{:S(2)}, u32[]{:S(2)}) collective-permute-start(f32[5,256,128]{2,1,0:T(8,128)S(1)} %get-tuple-element.42), channel_id=1, source_target_pairs={{0,1},{1,2},{2,3},{3,0},{4,5},{5,6},{6,7},{7,4},{8,9},{9,10},{10,1... | collective-permute-start | bytes 1966088 | tf_op jit(solution)/shard_map/ppermute | solution.py:324
  41.5 1.1 %copy-start.7 = (f32[5,256,128]{2,1,0:T(8,128)S(1)}, f32[5,256,128]{2,1,0:T(8,128)}, u32[]{:S(2)}) copy-start(f32[5,256,128]{2,1,0:T(8,128)} %copy-done.6) | copy-start | bytes 1966084
  42.6 1.1 %copy-start.9 = (f32[5,256,128]{2,1,0:T(8,128)S(1)}, f32[5,256,128]{2,1,0:T(8,128)}, u32[]{:S(2)}) copy-start(f32[5,256,128]{2,1,0:T(8,128)} %copy-done.8) | copy-start | bytes 1966084
  45.1 0.8 copy-start.4
  46.0 0.8 copy-start.5
  61.9 4.0 %collective-permute-start.5 = (f32[5,8,128]{2,1,0:T(8,128)}, f32[5,8,128]{2,1,0:T(8,128)S(1)}, u32[]{:S(2)}, u32[]{:S(2)}) collective-permute-start(f32[5,8,128]{2,1,0:T(8,128)} %slice_sum.1), channel_id=1, source_target_pairs={{0,3},{1,0},{2,1},{3,2},{4,7},{5,4},{6,5},{7,6},{8,11},{9,8},{10,9... | collective-permute-start | bytes 61448 | tf_op jit(solution)/shard_map/ppermute | solution.py:330
  63.3 5.2 %collective-permute-start.4 = (f32[5,8,128]{2,1,0:T(8,128)}, f32[5,8,128]{2,1,0:T(8,128)S(1)}, u32[]{:S(2)}, u32[]{:S(2)}) collective-permute-start(f32[5,8,128]{2,1,0:T(8,128)} %slice_sum.1), channel_id=1, source_target_pairs={{0,1},{1,2},{2,3},{3,0},{4,5},{5,6},{6,7},{7,4},{8,9},{9,10},{10,1... | collective-permute-start | bytes 61448 | tf_op jit(solution)/shard_map/ppermute | solution.py:330
  63.9 5.5 %collective-permute-start.3 = (f32[5,8,128]{2,1,0:T(8,128)}, f32[5,8,128]{2,1,0:T(8,128)S(1)}, u32[]{:S(2)}, u32[]{:S(2)}) collective-permute-start(f32[5,8,128]{2,1,0:T(8,128)} %slice_sum.1), channel_id=1, source_target_pairs={{0,2},{1,3},{2,0},{3,1},{4,6},{5,7},{6,4},{7,5},{8,10},{9,11},{10,... | collective-permute-start | bytes 61448 | tf_op jit(solution)/shard_map/ppermute | solution.py:330
  70.2 4.5 %copy-start.10 = (f32[5,8,128]{2,1,0:T(8,128)}, f32[5,8,128]{2,1,0:T(8,128)S(1)}, u32[]{:S(2)}) copy-start(f32[5,8,128]{2,1,0:T(8,128)S(1)} %add_add_fusion.own) | copy-start | bytes 61444
  70.2 14.6 %collective-permute-start.8 = (f32[5,256,128]{2,1,0:T(8,128)}, f32[5,256,128]{2,1,0:T(8,128)S(1)}, u32[]{:S(2)}, u32[]{:S(2)}) collective-permute-start(f32[5,256,128]{2,1,0:T(8,128)} %copy-done.5), channel_id=1, source_target_pairs={{0,1},{1,2},{2,3},{3,0},{4,5},{5,6},{6,7},{7,4},{8,9},{9,10},{10,1... | collective-permute-start | bytes 1966088 | tf_op jit(solution)/shard_map/ppermute | solution.py:333
  70.3 14.5 %collective-permute-start.9 = (f32[5,256,128]{2,1,0:T(8,128)}, f32[5,256,128]{2,1,0:T(8,128)}, u32[]{:S(2)}, u32[]{:S(2)}) collective-permute-start(f32[5,256,128]{2,1,0:T(8,128)} %copy-done.4), channel_id=1, source_target_pairs={{0,3},{1,0},{2,1},{3,2},{4,7},{5,4},{6,5},{7,6},{8,11},{9,8},{10,9... | collective-permute-start | bytes 1966088 | tf_op jit(solution)/shard_map/ppermute | solution.py:334
  73.5 1.2 %collective-permute-start.10 = (f32[5,8,128]{2,1,0:T(8,128)S(1)}, f32[5,8,128]{2,1,0:T(8,128)S(1)}, u32[]{:S(2)}, u32[]{:S(2)}) collective-permute-start(f32[5,8,128]{2,1,0:T(8,128)S(1)} %add_add_fusion.own), channel_id=1, source_target_pairs={{0,4},{4,0},{1,5},{5,1},{2,6},{6,2},{3,7},{7,3},{8,12},{12,8},{9,1... | collective-permute-start | bytes 61448 | tf_op jit(solution)/shard_map/ppermute | solution.py:335
  74.7 0.6 copy-start.11
  77.0 20.4 %all-to-all-start.1 = ((f32[32,24,128]{2,1,0:T(8,128)}), f32[32,24,128]{2,1,0:T(8,128)}, u32[]{:S(2)}, u32[]{:S(2)}) async-start(f32[32,24,128]{2,1,0:T(8,128)} %bitcast.9), calls=%async_computation.1 | async-start | bytes 786432 | tf_op jit(solution)/shard_map/all_to_all | solution.py:309

commit v4 on v3

--- a/solution.py
+++ b/solution.py
@@ -224,7 +224,11 @@
 def sum_call(parts):
     return pl.pallas_call(
         sum_kernel,
+        grid=(5,),
         out_shape=jax.ShapeDtypeStruct(parts.shape[1:], f32),
+        in_specs=[pl.BlockSpec((32, 1, 8, TILE), lambda j: (0, j, 0, 0))],
+        out_specs=pl.BlockSpec((1, 8, TILE), lambda j: (j, 0, 0)),
+        compiler_params=pltpu.CompilerParams(vmem_limit_bytes=4 * 2**20),
         cost_estimate=pl.CostEstimate(flops=10**6, bytes_accessed=10**6, transcendentals=0),
         name="slice_sum",
     )(parts)
@@ -252,6 +256,7 @@
         out_shape=jax.ShapeDtypeStruct((32, SLOTS, 8, TILE), f32),
         in_specs=[smem(), smem(), vmem(), vmem()],
         out_specs=vmem(),
+        compiler_params=pltpu.CompilerParams(vmem_limit_bytes=4 * 2**20),
         cost_estimate=pl.CostEstimate(flops=10**5, bytes_accessed=10**6, transcendentals=0),
         name="route",
     )(block_owner, place, own, other)
@@ -260,22 +265,24 @@
 def unpack_kernel(scale, parts, out):
     rows = lax.broadcasted_iota(jnp.int32, (TILE, TILE), 0)
     cols = lax.broadcasted_iota(jnp.int32, (TILE, TILE), 1)
-    for s in range(SLOTS):
-        pack = parts[:, s].reshape(2 * TILE, TILE) * scale
-        upper = jnp.where(rows < cols, pack[:TILE], 0.0)
-        lower = jnp.where(rows > cols, pack[:TILE], 0.0)
-        across = pack[TILE:]
-        out[s, :TILE, :TILE] = upper - upper.T
-        out[s, TILE:, TILE:] = lower - lower.T
-        out[s, :TILE, TILE:] = across
-        out[s, TILE:, :TILE] = -across.T
+    pack = parts[...].reshape(2 * TILE, TILE) * scale
+    upper = jnp.where(rows < cols, pack[:TILE], 0.0)
+    lower = jnp.where(rows > cols, pack[:TILE], 0.0)
+    across = pack[TILE:]
+    out[0, :TILE, :TILE] = upper - upper.T
+    out[0, TILE:, TILE:] = lower - lower.T
+    out[0, :TILE, TILE:] = across
+    out[0, TILE:, :TILE] = -across.T
 
 
 def unpack_call(parts, scale):
     return pl.pallas_call(
         lambda parts, out: unpack_kernel(scale, parts, out),
+        grid=(SLOTS,),
         out_shape=jax.ShapeDtypeStruct((SLOTS, BLOCK, BLOCK), f32),
-        in_specs=[vmem()],
+        in_specs=[pl.BlockSpec((32, 1, 8, TILE), lambda s: (0, s, 0, 0))],
+        out_specs=pl.BlockSpec((1, BLOCK, BLOCK), lambda s: (s, 0, 0)),
+        compiler_params=pltpu.CompilerParams(vmem_limit_bytes=4 * 2**20),
         cost_estimate=pl.CostEstimate(flops=10**6, bytes_accessed=10**6, transcendentals=0),
         name="unpack",
     )(parts)

time: 100 us -> 96.4 us (0.964)
  Pallas kernels: 29.7 us -> 28.1 us
    pallas_call x2, Pallas kernels: 3.85 us -> 1.95 us  [the longest x1 1.72 us: unpack_call(): pl.pallas_call(lambda parts, out: unpack_kernel(scale, parts, out), grid=...]
    all_to_all x2, waiting for transfers between devices: 23.9 us -> 22.3 us  [exchange(): lax.all_to_all(rows, ('x', 'z'), 0, 0, tiled=True).reshape(parts.shape)]
    unnamed x24 -> x22, local copies, waits for them, and re-layouts: 7.9 us -> 7.3 us
  transfers between devices with their start and end apart: 13 -> 13, of which waited for: 7 -> 7; matrix products, arithmetic and copies ran while one was open for 1% -> 0% of each run, Pallas kernels for 15% -> 14%
where the time goes in v4:
time: 96.4 us; the launch traced here: 95.9 us
  waiting for transfers between devices  31 us (32%)
  starting transfers between devices  28.7 us (30%)
  Pallas kernels  28.1 us (29%)
  local copies, waits for them, and re-layouts  7.3 us (8%)
    all_to_all x2, waiting for transfers between devices, exchange(): lax.all_to_all(rows, ('x', 'z'), 0, 0, tiled=True).reshape(parts.shape)  22.3 us
    all_to_all x2, starting transfers between devices, exchange(): lax.all_to_all(rows, ('x', 'z'), 0, 0, tiled=True).reshape(parts.shape)  16.2 us
    pallas_call x1, Pallas kernels, grad_call(): pl.pallas_call(grad_kernel, out_shape=[turns, turns, part, part, gram, gr...  12.5 us
    unnamed x22, local copies, waits for them, and re-layouts  7.3 us
    pallas_call x1, Pallas kernels, rotate_call(): pl.pallas_call(rotate_kernel, out_shape=[half] * 6 + [jax.ShapeDtypeStruc...  4.5 us
    ppermute x1, waiting for transfers between devices, local(): next_a = lax.ppermute(next_a, 'y', turn(Y, 1))  3.77 us
    pallas_call x1, Pallas kernels, adjoint_call(): pl.pallas_call(adjoint_kernel, out_shape=jax.ShapeDtypeStruct((32, 5, 8,...  3.73 us
    ppermute x3, waiting for transfers between devices, local(): others = [lax.ppermute(slices, 'y', turn(Y, s)) for s in (1, 2, 3)]  3.7 us
  transfers between devices with their start and end apart: 13, of which 7 were waited for; matrix products, arithmetic and copies ran while one was open for 0% of the time, Pallas kernels for 14%

profile of v4, /device:TPU:32, one launch (start us, length us, event | category | flops | bytes accessed | tf_op | source)
XLA Modules:
  0.0 95.9 jit_solution(634298400446551432)
XLA Ops:
  0.6 0.1 pad_add_fusion.place
  0.7 0.0 copy-start
  0.7 0.7 copy-done
  1.4 0.0 copy-start.2
  1.4 1.5 %copy-done.2 = bf16[512,1728]{0,1:T(8,128)(2,1)S(1)} copy-done((bf16[512,1728]{0,1:T(8,128)(2,1)S(1)}, bf16[512,1728]{0,1:T(8,128)(2,1)}, u32[]{:S(2)}) %copy-start.2) | copy-done | bytes 1769496
  2.8 0.0 copy-start.3
  2.8 1.3 %copy-done.3 = bf16[10,256,256]{2,1,0:T(8,128)(2,1)S(1)} copy-done((bf16[10,256,256]{2,1,0:T(8,128)(2,1)S(1)}, bf16[10,256,256]{2,1,0:T(8,128)(2,1)}, u32[]{:S(2)}) %copy-start.3) | copy-done | bytes 1310744
  4.2 12.5 %grad.1 = (bf16[10,256,256]{2,1,0:T(8,128)(2,1)S(1)}, bf16[10,256,256]{2,1,0:T(8,128)(2,1)S(1)}, bf16[10,512,256]{2,1,0:T(8,128)(2,1)S(1)}, bf16[10,512,256]{2,1...) custom-call(s32[20]{0:T(128)S(1)} %copy-done, s32[2]{0:T(128)S(1)} %pad_add_fusion.place, ...), custom_call_target="tpu_custom_call" | custom-call | flops 8000000000 | bytes 14000000 | tf_op jit(solution)/shard_map/grad/pallas_call | solution.py:117
  16.7 0.1 collective-permute-start
  16.8 4.5 %rotate.1 = (f32[5,256,128]{2,1,0:T(8,128)}, f32[5,256,128]{2,1,0:T(8,128)}, f32[5,256,128]{2,1,0:T(8,128)S(1)}, f32[5,256,128]{2,1,0:T(8,128)S(1)}, f32[5,256,1...) custom-call(s32[20]{0:T(128)S(1)} %copy-done, s32[2]{0:T(128)S(1)} %pad_add_fusion.place, ...), custom_call_target="tpu_custom_call" | custom-call | flops 2000000000 | bytes 10000000 | tf_op jit(solution)/shard_map/rotate/pallas_call | solution.py:156
  21.3 0.0 copy-start.4
  21.3 0.0 copy-start.7
  21.3 0.0 copy-start.9
  21.3 1.6 %collective-permute-start.1 = (f32[5,256,128]{2,1,0:T(8,128)}, f32[5,256,128]{2,1,0:T(8,128)}, u32[]{:S(2)}, u32[]{:S(2)}) collective-permute-start(f32[5,256,128]{2,1,0:T(8,128)} %get-tuple-element.33), channel_id=1, source_target_pairs={{0,1},{1,2},{2,3},{3,0},{4,5},{5,6},{6,7},{7,4},{8,9},{9,10},{10,1... | collective-permute-start | bytes 1966088 | tf_op jit(solution)/shard_map/ppermute | solution.py:328
  22.9 1.7 %collective-permute-start.2 = (f32[5,256,128]{2,1,0:T(8,128)}, f32[5,256,128]{2,1,0:T(8,128)}, u32[]{:S(2)}, u32[]{:S(2)}) collective-permute-start(f32[5,256,128]{2,1,0:T(8,128)} %get-tuple-element.35), channel_id=1, source_target_pairs={{0,3},{1,0},{2,1},{3,2},{4,7},{5,4},{6,5},{7,6},{8,11},{9,8},{10,9... | collective-permute-start | bytes 1966088 | tf_op jit(solution)/shard_map/ppermute | solution.py:329
  24.6 0.0 collective-permute-done.came
  24.6 3.7 %adjoint.1 = f32[32,5,8,128]{3,2,1,0:T(8,128)} custom-call(s32[2]{0:T(128)S(1)} %pad_add_fusion.place, f32[5,256,256]{2,1,0:T(8,128)S(1)} %get-tuple-element.30.mine, f32[5,256,256]{2,1,0:T(8,128)S(1)} %collective-permute-done.came, bf16[10,256,256]{2,1,0:T(8,128)(2,1)S(1)} %copy-done.3), custom_call_target="tpu_custom_call" | custom-call | flops 2000000000 | bytes 4000000 | tf_op jit(solution)/shard_map/adjoint/pallas_call | solution.py:189
  28.4 0.0 copy-done.4
  28.4 0.0 copy-done.7
  28.4 0.0 copy-done.9
  28.4 11.2 %all-to-all-start = ((f32[32,40,128]{2,1,0:T(8,128)}), f32[32,40,128]{2,1,0:T(8,128)S(1)}, u32[]{:S(2)}, u32[]{:S(2)}) async-start(f32[32,40,128]{2,1,0:T(8,128)} %bitcast.4), calls=%async_computation | async-start | bytes 1310720 | tf_op jit(solution)/shard_map/all_to_all | solution.py:316
  39.6 1.8 %collective-permute-start.6 = (f32[5,256,128]{2,1,0:T(8,128)}, f32[5,256,128]{2,1,0:T(8,128)S(1)}, u32[]{:S(2)}, u32[]{:S(2)}) collective-permute-start(f32[5,256,128]{2,1,0:T(8,128)} %get-tuple-element.41), channel_id=1, source_target_pairs={{0,3},{1,0},{2,1},{3,2},{4,7},{5,4},{6,5},{7,6},{8,11},{9,8},{10,9... | collective-permute-start | bytes 1966088 | tf_op jit(solution)/shard_map/ppermute | solution.py:330
  41.4 0.3 collective-permute-start.7
  41.7 0.0 collective-permute-done.1.far_a
  41.7 0.0 collective-permute-done.2.far_b
  41.7 0.0 copy-start.8
  41.7 1.1 %copy-done.8 = f32[5,256,128]{2,1,0:T(8,128)S(1)} copy-done((f32[5,256,128]{2,1,0:T(8,128)S(1)}, f32[5,256,128]{2,1,0:T(8,128)}, u32[]{:S(2)}) %copy-start.8) | copy-done | bytes 655384
  42.8 0.0 copy-start.10
  42.8 1.1 %copy-done.10 = f32[5,256,128]{2,1,0:T(8,128)S(1)} copy-done((f32[5,256,128]{2,1,0:T(8,128)S(1)}, f32[5,256,128]{2,1,0:T(8,128)}, u32[]{:S(2)}) %copy-start.10) | copy-done | bytes 655384
  43.9 0.0 copy-start.1
  43.9 1.5 %merge.1 = (f32[5,256,128]{2,1,0:T(8,128)S(1)}, f32[5,256,128]{2,1,0:T(8,128)S(1)}) custom-call(f32[5,256,128]{2,1,0:T(8,128)S(1)} %copy-done.8, f32[5,256,128]{2,1,0:T(8,128)} %collective-permute-done.1.far_a, f32[5,256,128]{2,1,0:T(8,128)S(1)} %copy-done.10, f32[5,256,128]{2,1,0:T(8,128)} %collective-permute-done.2.far_b), custom_call_target="tpu_custom_call" | custom-call | flops 10000000000 | bytes 4000000 | tf_op jit(solution)/shard_map/merge/pallas_call | solution.py:206
  45.4 0.0 copy-start.5
  45.4 0.8 copy-done.5
  46.2 0.0 copy-start.6
  46.2 0.8 copy-done.6
  47.1 13.2 %all-to-all-done = f32[32,40,128]{2,1,0:T(8,128)S(1)} async-done(((f32[32,40,128]{2,1,0:T(8,128)}), f32[32,40,128]{2,1,0:T(8,128)S(1)}, u32[]{:S(2)}, u32[]{:S(2)}) %all-to-all-start) | async-done | bytes 655392 | tf_op jit(solution)/shard_map/all_to_all | solution.py:316
  60.3 0.2 slice_sum.1
  60.5 1.5 %collective-permute-start.5 = (f32[5,8,128]{2,1,0:T(8,128)S(1)}, f32[5,8,128]{2,1,0:T(8,128)S(1)}, u32[]{:S(2)}, u32[]{:S(2)}) collective-permute-start(f32[5,8,128]{2,1,0:T(8,128)S(1)} %slice_sum.1), channel_id=1, source_target_pairs={{0,3},{1,0},{2,1},{3,2},{4,7},{5,4},{6,5},{7,6},{8,11},{9,8},{10,9... | collective-permute-start | bytes 61448 | tf_op jit(solution)/shard_map/ppermute | solution.py:337
  62.0 0.6 collective-permute-start.4
  62.6 1.6 %collective-permute-start.3 = (f32[5,8,128]{2,1,0:T(8,128)S(1)}, f32[5,8,128]{2,1,0:T(8,128)S(1)}, u32[]{:S(2)}, u32[]{:S(2)}) collective-permute-start(f32[5,8,128]{2,1,0:T(8,128)S(1)} %slice_sum.1), channel_id=1, source_target_pairs={{0,2},{1,3},{2,0},{3,1},{4,6},{5,7},{6,4},{7,5},{8,10},{9,11},{10,... | collective-permute-start | bytes 61448 | tf_op jit(solution)/shard_map/ppermute | solution.py:337
  64.2 0.2 collective-permute-done.5
  64.4 2.6 %collective-permute-done.4 = f32[5,8,128]{2,1,0:T(8,128)S(1)} collective-permute-done((f32[5,8,128]{2,1,0:T(8,128)S(1)}, f32[5,8,128]{2,1,0:T(8,128)S(1)}, u32[]{:S(2)}, u32[]{:S(2)}) %collective-permute-start.4) | collective-permute-done | bytes 20512 | tf_op jit(solution)/shard_map/ppermute | solution.py:337
  67.0 0.9 collective-permute-done.3
  67.9 0.0 collective-permute-done.6.a2
  67.9 0.0 collective-permute-done.7.b1
  67.9 0.1 collective-permute-start.8
  68.0 3.2 %collective-permute-start.9 = (f32[5,256,128]{2,1,0:T(8,128)}, f32[5,256,128]{2,1,0:T(8,128)}, u32[]{:S(2)}, u32[]{:S(2)}) collective-permute-start(f32[5,256,128]{2,1,0:T(8,128)} %copy-done.5), channel_id=1, source_target_pairs={{0,3},{1,0},{2,1},{3,2},{4,7},{5,4},{6,5},{7,6},{8,11},{9,8},{10,9... | collective-permute-start | bytes 1966088 | tf_op jit(solution)/shard_map/ppermute | solution.py:341
  71.3 0.0 collective-permute-start.10
  71.3 1.2 %collective-permute-done.10.other = f32[5,8,128]{2,1,0:T(8,128)S(1)} collective-permute-done((f32[5,8,128]{2,1,0:T(8,128)S(1)}, f32[5,8,128]{2,1,0:T(8,128)S(1)}, u32[]{:S(2)}, u32[]{:S(2)}) %collective-permute-start.10) | collective-permute-done | bytes 20512 | tf_op jit(solution)/shard_map/ppermute | solution.py:342
  72.5 0.0 copy-done.1
  72.5 1.5 %route.1 = f32[32,3,8,128]{3,2,1,0:T(8,128)} custom-call(s32[10]{0:T(128)S(1)} %copy-done.1, s32[2]{0:T(128)S(1)} %pad_add_fusion.place, f32[5,8,128]{2,1,0:T(8,128)S(1)} %add_add_fusion.own, f32[5,8,128]{2,1,0:T(8,128)S(1)} %collective-permute-done.10.other), custom_call_target="tpu_custom_call" | custom-call | flops 100000 | bytes 1000000 | tf_op jit(solution)/shard_map/route/pallas_call | solution.py:254
  73.9 5.0 %all-to-all-start.1 = ((f32[32,24,128]{2,1,0:T(8,128)}), f32[32,24,128]{2,1,0:T(8,128)S(1)}, u32[]{:S(2)}, u32[]{:S(2)}) async-start(f32[32,24,128]{2,1,0:T(8,128)} %bitcast.6), calls=%async_computation.1 | async-start | bytes 786432 | tf_op jit(solution)/shard_map/all_to_all | solution.py:316
  78.9 3.8 %collective-permute-done.8.a1 = f32[5,256,128]{2,1,0:T(8,128)} collective-permute-done((f32[5,256,128]{2,1,0:T(8,128)}, f32[5,256,128]{2,1,0:T(8,128)}, u32[]{:S(2)}, u32[]{:S(2)}) %collective-permute-start.8) | collective-permute-done | bytes 655392 | tf_op jit(solution)/shard_map/ppermute | solution.py:340
  82.7 0.0 collective-permute-done.9.b2
  82.7 2.4 %finish.1 = bf16[512,640]{1,0:T(8,128)(2,1)} custom-call(f32[5,512,128]{2,1,0:T(8,128)S(1)} %get-tuple-element.29.own, f32[5,256,128]{2,1,0:T(8,128)} %collective-permute-done.8.a1, f32[5,256,128]{2,1,0:T(8,128)S(1)} %collective-permute-done.6.a2, f32[5,256,128]{2,1,0:T(8,128)S(1)} %collective-permute-done.7.b1, f32[5,256,128]{2,1,0:T(8,128)} %collective-permute-done.9.b2), custom_call_target="tpu_custom_call" | custom-call | flops 10000000000 | bytes 5000000 | tf_op jit(solution)/shard_map/finish/pallas_call | solution.py:300
  85.1 9.1 %all-to-all-done.1 = f32[32,24,128]{2,1,0:T(8,128)S(1)} async-done(((f32[32,24,128]{2,1,0:T(8,128)}), f32[32,24,128]{2,1,0:T(8,128)S(1)}, u32[]{:S(2)}, u32[]{:S(2)}) %all-to-all-start.1) | async-done | bytes 393248 | tf_op jit(solution)/shard_map/all_to_all | solution.py:316
  94.2 1.7 %unpack.1 = f32[3,256,256]{2,1,0:T(8,128)} custom-call(f32[32,3,8,128]{3,2,1,0:T(8,128)S(1)} %bitcast.9), custom_call_target="tpu_custom_call" | custom-call | flops 1000000 | bytes 1000000 | tf_op jit(solution)/shard_map/unpack/pallas_call | solution.py:279
  (1 shorter events, 0.0 us)
Async XLA Ops:
  0.7 0.7 copy-start
  1.4 1.5 %copy-start.2 = (bf16[512,1728]{0,1:T(8,128)(2,1)S(1)}, bf16[512,1728]{0,1:T(8,128)(2,1)}, u32[]{:S(2)}) copy-start(bf16[512,1728]{0,1:T(8,128)(2,1)} %param.7) | copy-start | bytes 5308420
  2.8 1.3 %copy-start.3 = (bf16[10,256,256]{2,1,0:T(8,128)(2,1)S(1)}, bf16[10,256,256]{2,1,0:T(8,128)(2,1)}, u32[]{:S(2)}) copy-start(bf16[10,256,256]{2,1,0:T(8,128)(2,1)} %skew.3) | copy-start | bytes 3932164
  16.7 8.0 %collective-permute-start = (f32[5,256,256]{2,1,0:T(8,128)S(1)}, f32[5,256,256]{2,1,0:T(8,128)S(1)}, u32[]{:S(2)}, u32[]{:S(2)}) collective-permute-start(f32[5,256,256]{2,1,0:T(8,128)S(1)} %get-tuple-element.31), channel_id=1, source_target_pairs={{0,4},{4,0},{1,5},{5,1},{2,6},{6,2},{3,7},{7,3},{8,12},{12,8},{9,1... | collective-permute-start | bytes 3932168 | tf_op jit(solution)/shard_map/ppermute | solution.py:324
  21.3 7.1 %copy-start.4 = (f32[5,256,128]{2,1,0:T(8,128)}, f32[5,256,128]{2,1,0:T(8,128)S(1)}, u32[]{:S(2)}) copy-start(f32[5,256,128]{2,1,0:T(8,128)S(1)} %get-tuple-element.42) | copy-start | bytes 1966084
  21.3 7.1 %copy-start.7 = (f32[5,256,128]{2,1,0:T(8,128)}, f32[5,256,128]{2,1,0:T(8,128)S(1)}, u32[]{:S(2)}) copy-start(f32[5,256,128]{2,1,0:T(8,128)S(1)} %get-tuple-element.32.next_a) | copy-start | bytes 1966084
  21.3 7.1 %copy-start.9 = (f32[5,256,128]{2,1,0:T(8,128)}, f32[5,256,128]{2,1,0:T(8,128)S(1)}, u32[]{:S(2)}) copy-start(f32[5,256,128]{2,1,0:T(8,128)S(1)} %get-tuple-element.34.last_b) | copy-start | bytes 1966084
  21.3 20.4 %collective-permute-start.1 = (f32[5,256,128]{2,1,0:T(8,128)}, f32[5,256,128]{2,1,0:T(8,128)}, u32[]{:S(2)}, u32[]{:S(2)}) collective-permute-start(f32[5,256,128]{2,1,0:T(8,128)} %get-tuple-element.33), channel_id=1, source_target_pairs={{0,1},{1,2},{2,3},{3,0},{4,5},{5,6},{6,7},{7,4},{8,9},{9,10},{10,1... | collective-permute-start | bytes 1966088 | tf_op jit(solution)/shard_map/ppermute | solution.py:328
  22.9 18.8 %collective-permute-start.2 = (f32[5,256,128]{2,1,0:T(8,128)}, f32[5,256,128]{2,1,0:T(8,128)}, u32[]{:S(2)}, u32[]{:S(2)}) collective-permute-start(f32[5,256,128]{2,1,0:T(8,128)} %get-tuple-element.35), channel_id=1, source_target_pairs={{0,3},{1,0},{2,1},{3,2},{4,7},{5,4},{6,5},{7,6},{8,11},{9,8},{10,9... | collective-permute-start | bytes 1966088 | tf_op jit(solution)/shard_map/ppermute | solution.py:329
  28.4 31.9 %all-to-all-start = ((f32[32,40,128]{2,1,0:T(8,128)}), f32[32,40,128]{2,1,0:T(8,128)S(1)}, u32[]{:S(2)}, u32[]{:S(2)}) async-start(f32[32,40,128]{2,1,0:T(8,128)} %bitcast.4), calls=%async_computation | async-start | bytes 1310720 | tf_op jit(solution)/shard_map/all_to_all | solution.py:316
  39.6 28.4 %collective-permute-start.6 = (f32[5,256,128]{2,1,0:T(8,128)}, f32[5,256,128]{2,1,0:T(8,128)S(1)}, u32[]{:S(2)}, u32[]{:S(2)}) collective-permute-start(f32[5,256,128]{2,1,0:T(8,128)} %get-tuple-element.41), channel_id=1, source_target_pairs={{0,3},{1,0},{2,1},{3,2},{4,7},{5,4},{6,5},{7,6},{8,11},{9,8},{10,9... | collective-permute-start | bytes 1966088 | tf_op jit(solution)/shard_map/ppermute | solution.py:330
  41.4 26.5 %collective-permute-start.7 = (f32[5,256,128]{2,1,0:T(8,128)}, f32[5,256,128]{2,1,0:T(8,128)S(1)}, u32[]{:S(2)}, u32[]{:S(2)}) collective-permute-start(f32[5,256,128]{2,1,0:T(8,128)} %copy-done.4), channel_id=1, source_target_pairs={{0,1},{1,2},{2,3},{3,0},{4,5},{5,6},{6,7},{7,4},{8,9},{9,10},{10,1... | collective-permute-start | bytes 1966088 | tf_op jit(solution)/shard_map/ppermute | solution.py:331
  41.7 1.1 %copy-start.8 = (f32[5,256,128]{2,1,0:T(8,128)S(1)}, f32[5,256,128]{2,1,0:T(8,128)}, u32[]{:S(2)}) copy-start(f32[5,256,128]{2,1,0:T(8,128)} %copy-done.7) | copy-start | bytes 1966084
  42.8 1.1 %copy-start.10 = (f32[5,256,128]{2,1,0:T(8,128)S(1)}, f32[5,256,128]{2,1,0:T(8,128)}, u32[]{:S(2)}) copy-start(f32[5,256,128]{2,1,0:T(8,128)} %copy-done.9) | copy-start | bytes 1966084
  43.9 28.6 %copy-start.1 = (s32[10]{0:T(128)S(1)}, s32[10]{0:T(128)}, u32[]{:S(2)}) copy-start(s32[10]{0:T(128)} %owner.1) | copy-start | bytes 124
  45.4 0.8 copy-start.5
  46.2 0.8 copy-start.6
  60.5 3.9 %collective-permute-start.5 = (f32[5,8,128]{2,1,0:T(8,128)S(1)}, f32[5,8,128]{2,1,0:T(8,128)S(1)}, u32[]{:S(2)}, u32[]{:S(2)}) collective-permute-start(f32[5,8,128]{2,1,0:T(8,128)S(1)} %slice_sum.1), channel_id=1, source_target_pairs={{0,3},{1,0},{2,1},{3,2},{4,7},{5,4},{6,5},{7,6},{8,11},{9,8},{10,9... | collective-permute-start | bytes 61448 | tf_op jit(solution)/shard_map/ppermute | solution.py:337
  62.0 5.0 %collective-permute-start.4 = (f32[5,8,128]{2,1,0:T(8,128)S(1)}, f32[5,8,128]{2,1,0:T(8,128)S(1)}, u32[]{:S(2)}, u32[]{:S(2)}) collective-permute-start(f32[5,8,128]{2,1,0:T(8,128)S(1)} %slice_sum.1), channel_id=1, source_target_pairs={{0,1},{1,2},{2,3},{3,0},{4,5},{5,6},{6,7},{7,4},{8,9},{9,10},{10,1... | collective-permute-start | bytes 61448 | tf_op jit(solution)/shard_map/ppermute | solution.py:337
  62.6 5.3 %collective-permute-start.3 = (f32[5,8,128]{2,1,0:T(8,128)S(1)}, f32[5,8,128]{2,1,0:T(8,128)S(1)}, u32[]{:S(2)}, u32[]{:S(2)}) collective-permute-start(f32[5,8,128]{2,1,0:T(8,128)S(1)} %slice_sum.1), channel_id=1, source_target_pairs={{0,2},{1,3},{2,0},{3,1},{4,6},{5,7},{6,4},{7,5},{8,10},{9,11},{10,... | collective-permute-start | bytes 61448 | tf_op jit(solution)/shard_map/ppermute | solution.py:337
  67.9 14.7 %collective-permute-start.8 = (f32[5,256,128]{2,1,0:T(8,128)}, f32[5,256,128]{2,1,0:T(8,128)}, u32[]{:S(2)}, u32[]{:S(2)}) collective-permute-start(f32[5,256,128]{2,1,0:T(8,128)} %copy-done.6), channel_id=1, source_target_pairs={{0,1},{1,2},{2,3},{3,0},{4,5},{5,6},{6,7},{7,4},{8,9},{9,10},{10,1... | collective-permute-start | bytes 1966088 | tf_op jit(solution)/shard_map/ppermute | solution.py:340
  68.0 14.6 %collective-permute-start.9 = (f32[5,256,128]{2,1,0:T(8,128)}, f32[5,256,128]{2,1,0:T(8,128)}, u32[]{:S(2)}, u32[]{:S(2)}) collective-permute-start(f32[5,256,128]{2,1,0:T(8,128)} %copy-done.5), channel_id=1, source_target_pairs={{0,3},{1,0},{2,1},{3,2},{4,7},{5,4},{6,5},{7,6},{8,11},{9,8},{10,9... | collective-permute-start | bytes 1966088 | tf_op jit(solution)/shard_map/ppermute | solution.py:341
  71.3 1.2 %collective-permute-start.10 = (f32[5,8,128]{2,1,0:T(8,128)S(1)}, f32[5,8,128]{2,1,0:T(8,128)S(1)}, u32[]{:S(2)}, u32[]{:S(2)}) collective-permute-start(f32[5,8,128]{2,1,0:T(8,128)S(1)} %add_add_fusion.own), channel_id=1, source_target_pairs={{0,4},{4,0},{1,5},{5,1},{2,6},{6,2},{3,7},{7,3},{8,12},{12,8},{9,1... | collective-permute-start | bytes 61448 | tf_op jit(solution)/shard_map/ppermute | solution.py:342
  73.9 20.3 %all-to-all-start.1 = ((f32[32,24,128]{2,1,0:T(8,128)}), f32[32,24,128]{2,1,0:T(8,128)S(1)}, u32[]{:S(2)}, u32[]{:S(2)}) async-start(f32[32,24,128]{2,1,0:T(8,128)} %bitcast.6), calls=%async_computation.1 | async-start | bytes 786432 | tf_op jit(solution)/shard_map/all_to_all | solution.py:316

commit v5 on v4

--- a/solution.py
+++ b/solution.py
@@ -36,6 +36,11 @@
 
 def product(a, b):
     return dot(stack(a, 1), stack(b, 0))
+
+
+def square_of(a):
+    mixed = dot(a[0], a[1])
+    return dot(a[0], a[0]) + (mixed + mixed.T)
 
 
 def turned_skew(ref, b):
@@ -78,16 +83,17 @@
         group = range(b0, b0 + 5)
         turned = [turned_skew(skews, b) for b in group]
         pairs = [split(a) for a in turned]
-        squares = [product(a, a) for a in pairs]
+        squares = [square_of(a) for a in pairs]
         cubes = [product(split(a), p) for a, p in zip(squares, pairs)]
         for b, a, square, cube in zip(group, turned, squares, cubes):
             turn_high[b], turn_low[b] = split(identity + 2.0 * a + 2.0 * square + cube)
     get_cot.wait()
     cot[...] = cots[...].T
-    for t in range(20):
-        fetch(t).wait()
-    for b in range(10):
-        high[b], low[b] = split(dot(cot[...], tiles[b]))
+    for b0 in range(0, 10, 5):
+        for t in range(2 * b0, 2 * b0 + 10):
+            fetch(t).wait()
+        for b in range(b0, b0 + 5):
+            high[b], low[b] = split(dot(cot[...], tiles[b]))
     for t in range(20):
         fetch_inputs(t).wait()
     for out, first in ((mine, 5 * core), (other, 5 * (1 - core))):
@@ -175,10 +181,9 @@
     odd = [a - a.T for a in grams]
     even = [2.0 * (a + a.T) for a in grams]
     first = [product(split(a), t) for a, t in zip(odd, turned)]
-    second = [product(split(e + a), t) for e, a, t in zip(even, first, turned)]
-    third = [product(t, split(a)) for a, t in zip(first, turned)]
+    second = [product(split(e + a + 0.5 * a.T), t) for e, a, t in zip(even, first, turned)]
     for j in group:
-        total = odd[j] + second[j] + 0.5 * third[j]
+        total = odd[j] + second[j]
         grads = total - total.T
         out[:, j] = jnp.concatenate(
             [jnp.where(rows < cols, grads[:TILE, :TILE], grads[TILE:, TILE:]), grads[:TILE, TILE:]], axis=0

time: 96.4 us -> 95.5 us (level)
  no operation moved by 1% of the time
where the time goes in v5:
time: 95.5 us; the launch traced here: 95.1 us
  waiting for transfers between devices  31 us (32%)
  starting transfers between devices  28.7 us (30%)
  Pallas kernels  27.2 us (28%)
  local copies, waits for them, and re-layouts  7.3 us (8%)
    all_to_all x2, waiting for transfers between devices, exchange(): lax.all_to_all(rows, ('x', 'z'), 0, 0, tiled=True).reshape(parts.shape)  22.4 us
    all_to_all x2, starting transfers between devices, exchange(): lax.all_to_all(rows, ('x', 'z'), 0, 0, tiled=True).reshape(parts.shape)  16.2 us
    pallas_call x1, Pallas kernels, grad_call(): pl.pallas_call(grad_kernel, out_shape=[turns, turns, part, part, gram, gr...  12.1 us
    unnamed x22, local copies, waits for them, and re-layouts  7.3 us
    pallas_call x1, Pallas kernels, rotate_call(): pl.pallas_call(rotate_kernel, out_shape=[half] * 6 + [jax.ShapeDtypeStruc...  4.5 us
    ppermute x1, waiting for transfers between devices, local(): next_a = lax.ppermute(next_a, 'y', turn(Y, 1))  3.75 us
    ppermute x3, starting transfers between devices, local(): others = [lax.ppermute(slices, 'y', turn(Y, s)) for s in (1, 2, 3)]  3.69 us
    ppermute x3, waiting for transfers between devices, local(): others = [lax.ppermute(slices, 'y', turn(Y, s)) for s in (1, 2, 3)]  3.69 us
  transfers between devices with their start and end apart: 13, of which 7 were waited for; matrix products, arithmetic and copies ran while one was open for 0% of the time, Pallas kernels for 14%

profile of v5, /device:TPU:32, one launch (start us, length us, event | category | flops | bytes accessed | tf_op | source)
XLA Modules:
  0.0 95.1 jit_solution(13689354655882312933)
XLA Ops:
  0.6 0.1 pad_add_fusion.place
  0.7 0.0 copy-start
  0.7 0.7 copy-done
  1.4 0.0 copy-start.2
  1.4 1.5 %copy-done.2 = bf16[512,1728]{0,1:T(8,128)(2,1)S(1)} copy-done((bf16[512,1728]{0,1:T(8,128)(2,1)S(1)}, bf16[512,1728]{0,1:T(8,128)(2,1)}, u32[]{:S(2)}) %copy-start.2) | copy-done | bytes 1769496
  2.8 0.0 copy-start.3
  2.8 1.3 %copy-done.3 = bf16[10,256,256]{2,1,0:T(8,128)(2,1)S(1)} copy-done((bf16[10,256,256]{2,1,0:T(8,128)(2,1)S(1)}, bf16[10,256,256]{2,1,0:T(8,128)(2,1)}, u32[]{:S(2)}) %copy-start.3) | copy-done | bytes 1310744
  4.2 12.1 %grad.1 = (bf16[10,256,256]{2,1,0:T(8,128)(2,1)S(1)}, bf16[10,256,256]{2,1,0:T(8,128)(2,1)S(1)}, bf16[10,512,256]{2,1,0:T(8,128)(2,1)S(1)}, bf16[10,512,256]{2,1...) custom-call(s32[20]{0:T(128)S(1)} %copy-done, s32[2]{0:T(128)S(1)} %pad_add_fusion.place, ...), custom_call_target="tpu_custom_call" | custom-call | flops 8000000000 | bytes 14000000 | tf_op jit(solution)/shard_map/grad/pallas_call | solution.py:123
  16.3 0.1 collective-permute-start
  16.4 4.5 %rotate.1 = (f32[5,256,128]{2,1,0:T(8,128)}, f32[5,256,128]{2,1,0:T(8,128)}, f32[5,256,128]{2,1,0:T(8,128)S(1)}, f32[5,256,128]{2,1,0:T(8,128)S(1)}, f32[5,256,1...) custom-call(s32[20]{0:T(128)S(1)} %copy-done, s32[2]{0:T(128)S(1)} %pad_add_fusion.place, ...), custom_call_target="tpu_custom_call" | custom-call | flops 2000000000 | bytes 10000000 | tf_op jit(solution)/shard_map/rotate/pallas_call | solution.py:162
  20.9 0.0 copy-start.4
  20.9 0.0 copy-start.7
  20.9 0.0 copy-start.9
  20.9 1.6 %collective-permute-start.1 = (f32[5,256,128]{2,1,0:T(8,128)}, f32[5,256,128]{2,1,0:T(8,128)}, u32[]{:S(2)}, u32[]{:S(2)}) collective-permute-start(f32[5,256,128]{2,1,0:T(8,128)} %get-tuple-element.33), channel_id=1, source_target_pairs={{0,1},{1,2},{2,3},{3,0},{4,5},{5,6},{6,7},{7,4},{8,9},{9,10},{10,1... | collective-permute-start | bytes 1966088 | tf_op jit(solution)/shard_map/ppermute | solution.py:333
  22.5 1.7 %collective-permute-start.2 = (f32[5,256,128]{2,1,0:T(8,128)}, f32[5,256,128]{2,1,0:T(8,128)}, u32[]{:S(2)}, u32[]{:S(2)}) collective-permute-start(f32[5,256,128]{2,1,0:T(8,128)} %get-tuple-element.35), channel_id=1, source_target_pairs={{0,3},{1,0},{2,1},{3,2},{4,7},{5,4},{6,5},{7,6},{8,11},{9,8},{10,9... | collective-permute-start | bytes 1966088 | tf_op jit(solution)/shard_map/ppermute | solution.py:334
  24.2 0.0 collective-permute-done.came
  24.2 3.3 %adjoint.1 = f32[32,5,8,128]{3,2,1,0:T(8,128)} custom-call(s32[2]{0:T(128)S(1)} %pad_add_fusion.place, f32[5,256,256]{2,1,0:T(8,128)S(1)} %get-tuple-element.30.mine, f32[5,256,256]{2,1,0:T(8,128)S(1)} %collective-permute-done.came, bf16[10,256,256]{2,1,0:T(8,128)(2,1)S(1)} %copy-done.3), custom_call_target="tpu_custom_call" | custom-call | flops 2000000000 | bytes 4000000 | tf_op jit(solution)/shard_map/adjoint/pallas_call | solution.py:194
  27.5 0.0 copy-done.4
  27.5 0.0 copy-done.7
  27.5 0.0 copy-done.9
  27.5 11.2 %all-to-all-start = ((f32[32,40,128]{2,1,0:T(8,128)}), f32[32,40,128]{2,1,0:T(8,128)S(1)}, u32[]{:S(2)}, u32[]{:S(2)}) async-start(f32[32,40,128]{2,1,0:T(8,128)} %bitcast.4), calls=%async_computation | async-start | bytes 1310720 | tf_op jit(solution)/shard_map/all_to_all | solution.py:321
  38.7 1.8 %collective-permute-start.6 = (f32[5,256,128]{2,1,0:T(8,128)}, f32[5,256,128]{2,1,0:T(8,128)S(1)}, u32[]{:S(2)}, u32[]{:S(2)}) collective-permute-start(f32[5,256,128]{2,1,0:T(8,128)} %get-tuple-element.41), channel_id=1, source_target_pairs={{0,3},{1,0},{2,1},{3,2},{4,7},{5,4},{6,5},{7,6},{8,11},{9,8},{10,9... | collective-permute-start | bytes 1966088 | tf_op jit(solution)/shard_map/ppermute | solution.py:335
  40.6 0.3 collective-permute-start.7
  40.8 0.0 collective-permute-done.1.far_a
  40.8 0.0 collective-permute-done.2.far_b
  40.8 0.0 copy-start.8
  40.8 1.1 %copy-done.8 = f32[5,256,128]{2,1,0:T(8,128)S(1)} copy-done((f32[5,256,128]{2,1,0:T(8,128)S(1)}, f32[5,256,128]{2,1,0:T(8,128)}, u32[]{:S(2)}) %copy-start.8) | copy-done | bytes 655384
  41.9 0.0 copy-start.10
  41.9 1.1 %copy-done.10 = f32[5,256,128]{2,1,0:T(8,128)S(1)} copy-done((f32[5,256,128]{2,1,0:T(8,128)S(1)}, f32[5,256,128]{2,1,0:T(8,128)}, u32[]{:S(2)}) %copy-start.10) | copy-done | bytes 655384
  43.0 0.0 copy-start.1
  43.0 1.5 %merge.1 = (f32[5,256,128]{2,1,0:T(8,128)S(1)}, f32[5,256,128]{2,1,0:T(8,128)S(1)}) custom-call(f32[5,256,128]{2,1,0:T(8,128)S(1)} %copy-done.8, f32[5,256,128]{2,1,0:T(8,128)} %collective-permute-done.1.far_a, f32[5,256,128]{2,1,0:T(8,128)S(1)} %copy-done.10, f32[5,256,128]{2,1,0:T(8,128)} %collective-permute-done.2.far_b), custom_call_target="tpu_custom_call" | custom-call | flops 10000000000 | bytes 4000000 | tf_op jit(solution)/shard_map/merge/pallas_call | solution.py:211
  44.5 0.0 copy-start.5
  44.6 0.8 copy-done.5
  45.4 0.0 copy-start.6
  45.4 0.8 copy-done.6
  46.2 13.2 %all-to-all-done = f32[32,40,128]{2,1,0:T(8,128)S(1)} async-done(((f32[32,40,128]{2,1,0:T(8,128)}), f32[32,40,128]{2,1,0:T(8,128)S(1)}, u32[]{:S(2)}, u32[]{:S(2)}) %all-to-all-start) | async-done | bytes 655392 | tf_op jit(solution)/shard_map/all_to_all | solution.py:321
  59.4 0.2 slice_sum.1
  59.7 1.5 %collective-permute-start.5 = (f32[5,8,128]{2,1,0:T(8,128)S(1)}, f32[5,8,128]{2,1,0:T(8,128)S(1)}, u32[]{:S(2)}, u32[]{:S(2)}) collective-permute-start(f32[5,8,128]{2,1,0:T(8,128)S(1)} %slice_sum.1), channel_id=1, source_target_pairs={{0,3},{1,0},{2,1},{3,2},{4,7},{5,4},{6,5},{7,6},{8,11},{9,8},{10,9... | collective-permute-start | bytes 61448 | tf_op jit(solution)/shard_map/ppermute | solution.py:342
  61.2 0.6 collective-permute-start.4
  61.8 1.6 %collective-permute-start.3 = (f32[5,8,128]{2,1,0:T(8,128)S(1)}, f32[5,8,128]{2,1,0:T(8,128)S(1)}, u32[]{:S(2)}, u32[]{:S(2)}) collective-permute-start(f32[5,8,128]{2,1,0:T(8,128)S(1)} %slice_sum.1), channel_id=1, source_target_pairs={{0,2},{1,3},{2,0},{3,1},{4,6},{5,7},{6,4},{7,5},{8,10},{9,11},{10,... | collective-permute-start | bytes 61448 | tf_op jit(solution)/shard_map/ppermute | solution.py:342
  63.4 0.2 collective-permute-done.5
  63.5 2.6 %collective-permute-done.4 = f32[5,8,128]{2,1,0:T(8,128)S(1)} collective-permute-done((f32[5,8,128]{2,1,0:T(8,128)S(1)}, f32[5,8,128]{2,1,0:T(8,128)S(1)}, u32[]{:S(2)}, u32[]{:S(2)}) %collective-permute-start.4) | collective-permute-done | bytes 20512 | tf_op jit(solution)/shard_map/ppermute | solution.py:342
  66.1 0.9 collective-permute-done.3
  67.1 0.0 collective-permute-done.6.a2
  67.1 0.0 collective-permute-done.7.b1
  67.1 0.1 collective-permute-start.8
  67.2 3.2 %collective-permute-start.9 = (f32[5,256,128]{2,1,0:T(8,128)}, f32[5,256,128]{2,1,0:T(8,128)}, u32[]{:S(2)}, u32[]{:S(2)}) collective-permute-start(f32[5,256,128]{2,1,0:T(8,128)} %copy-done.5), channel_id=1, source_target_pairs={{0,3},{1,0},{2,1},{3,2},{4,7},{5,4},{6,5},{7,6},{8,11},{9,8},{10,9... | collective-permute-start | bytes 1966088 | tf_op jit(solution)/shard_map/ppermute | solution.py:346
  70.4 0.0 collective-permute-start.10
  70.4 1.2 %collective-permute-done.10.other = f32[5,8,128]{2,1,0:T(8,128)S(1)} collective-permute-done((f32[5,8,128]{2,1,0:T(8,128)S(1)}, f32[5,8,128]{2,1,0:T(8,128)S(1)}, u32[]{:S(2)}, u32[]{:S(2)}) %collective-permute-start.10) | collective-permute-done | bytes 20512 | tf_op jit(solution)/shard_map/ppermute | solution.py:347
  71.6 0.0 copy-done.1
  71.6 1.5 %route.1 = f32[32,3,8,128]{3,2,1,0:T(8,128)} custom-call(s32[10]{0:T(128)S(1)} %copy-done.1, s32[2]{0:T(128)S(1)} %pad_add_fusion.place, f32[5,8,128]{2,1,0:T(8,128)S(1)} %add_add_fusion.own, f32[5,8,128]{2,1,0:T(8,128)S(1)} %collective-permute-done.10.other), custom_call_target="tpu_custom_call" | custom-call | flops 100000 | bytes 1000000 | tf_op jit(solution)/shard_map/route/pallas_call | solution.py:259
  73.0 5.0 %all-to-all-start.1 = ((f32[32,24,128]{2,1,0:T(8,128)}), f32[32,24,128]{2,1,0:T(8,128)S(1)}, u32[]{:S(2)}, u32[]{:S(2)}) async-start(f32[32,24,128]{2,1,0:T(8,128)} %bitcast.6), calls=%async_computation.1 | async-start | bytes 786432 | tf_op jit(solution)/shard_map/all_to_all | solution.py:321
  78.0 3.8 %collective-permute-done.8.a1 = f32[5,256,128]{2,1,0:T(8,128)} collective-permute-done((f32[5,256,128]{2,1,0:T(8,128)}, f32[5,256,128]{2,1,0:T(8,128)}, u32[]{:S(2)}, u32[]{:S(2)}) %collective-permute-start.8) | collective-permute-done | bytes 655392 | tf_op jit(solution)/shard_map/ppermute | solution.py:345
  81.8 0.0 collective-permute-done.9.b2
  81.8 2.4 %finish.1 = bf16[512,640]{1,0:T(8,128)(2,1)} custom-call(f32[5,512,128]{2,1,0:T(8,128)S(1)} %get-tuple-element.29.own, f32[5,256,128]{2,1,0:T(8,128)} %collective-permute-done.8.a1, f32[5,256,128]{2,1,0:T(8,128)S(1)} %collective-permute-done.6.a2, f32[5,256,128]{2,1,0:T(8,128)S(1)} %collective-permute-done.7.b1, f32[5,256,128]{2,1,0:T(8,128)} %collective-permute-done.9.b2), custom_call_target="tpu_custom_call" | custom-call | flops 10000000000 | bytes 5000000 | tf_op jit(solution)/shard_map/finish/pallas_call | solution.py:305
  84.2 9.2 %all-to-all-done.1 = f32[32,24,128]{2,1,0:T(8,128)S(1)} async-done(((f32[32,24,128]{2,1,0:T(8,128)}), f32[32,24,128]{2,1,0:T(8,128)S(1)}, u32[]{:S(2)}, u32[]{:S(2)}) %all-to-all-start.1) | async-done | bytes 393248 | tf_op jit(solution)/shard_map/all_to_all | solution.py:321
  93.4 1.7 %unpack.1 = f32[3,256,256]{2,1,0:T(8,128)} custom-call(f32[32,3,8,128]{3,2,1,0:T(8,128)S(1)} %bitcast.9), custom_call_target="tpu_custom_call" | custom-call | flops 1000000 | bytes 1000000 | tf_op jit(solution)/shard_map/unpack/pallas_call | solution.py:284
  (1 shorter events, 0.0 us)
Async XLA Ops:
  0.7 0.7 copy-start
  1.4 1.5 %copy-start.2 = (bf16[512,1728]{0,1:T(8,128)(2,1)S(1)}, bf16[512,1728]{0,1:T(8,128)(2,1)}, u32[]{:S(2)}) copy-start(bf16[512,1728]{0,1:T(8,128)(2,1)} %param.7) | copy-start | bytes 5308420
  2.8 1.3 %copy-start.3 = (bf16[10,256,256]{2,1,0:T(8,128)(2,1)S(1)}, bf16[10,256,256]{2,1,0:T(8,128)(2,1)}, u32[]{:S(2)}) copy-start(bf16[10,256,256]{2,1,0:T(8,128)(2,1)} %skew.3) | copy-start | bytes 3932164
  16.3 8.0 %collective-permute-start = (f32[5,256,256]{2,1,0:T(8,128)S(1)}, f32[5,256,256]{2,1,0:T(8,128)S(1)}, u32[]{:S(2)}, u32[]{:S(2)}) collective-permute-start(f32[5,256,256]{2,1,0:T(8,128)S(1)} %get-tuple-element.31), channel_id=1, source_target_pairs={{0,4},{4,0},{1,5},{5,1},{2,6},{6,2},{3,7},{7,3},{8,12},{12,8},{9,1... | collective-permute-start | bytes 3932168 | tf_op jit(solution)/shard_map/ppermute | solution.py:329
  20.9 6.6 %copy-start.4 = (f32[5,256,128]{2,1,0:T(8,128)}, f32[5,256,128]{2,1,0:T(8,128)S(1)}, u32[]{:S(2)}) copy-start(f32[5,256,128]{2,1,0:T(8,128)S(1)} %get-tuple-element.42) | copy-start | bytes 1966084
  20.9 6.6 %copy-start.7 = (f32[5,256,128]{2,1,0:T(8,128)}, f32[5,256,128]{2,1,0:T(8,128)S(1)}, u32[]{:S(2)}) copy-start(f32[5,256,128]{2,1,0:T(8,128)S(1)} %get-tuple-element.32.next_a) | copy-start | bytes 1966084
  20.9 6.6 %copy-start.9 = (f32[5,256,128]{2,1,0:T(8,128)}, f32[5,256,128]{2,1,0:T(8,128)S(1)}, u32[]{:S(2)}) copy-start(f32[5,256,128]{2,1,0:T(8,128)S(1)} %get-tuple-element.34.last_b) | copy-start | bytes 1966084
  20.9 20.0 %collective-permute-start.1 = (f32[5,256,128]{2,1,0:T(8,128)}, f32[5,256,128]{2,1,0:T(8,128)}, u32[]{:S(2)}, u32[]{:S(2)}) collective-permute-start(f32[5,256,128]{2,1,0:T(8,128)} %get-tuple-element.33), channel_id=1, source_target_pairs={{0,1},{1,2},{2,3},{3,0},{4,5},{5,6},{6,7},{7,4},{8,9},{9,10},{10,1... | collective-permute-start | bytes 1966088 | tf_op jit(solution)/shard_map/ppermute | solution.py:333
  22.5 18.3 %collective-permute-start.2 = (f32[5,256,128]{2,1,0:T(8,128)}, f32[5,256,128]{2,1,0:T(8,128)}, u32[]{:S(2)}, u32[]{:S(2)}) collective-permute-start(f32[5,256,128]{2,1,0:T(8,128)} %get-tuple-element.35), channel_id=1, source_target_pairs={{0,3},{1,0},{2,1},{3,2},{4,7},{5,4},{6,5},{7,6},{8,11},{9,8},{10,9... | collective-permute-start | bytes 1966088 | tf_op jit(solution)/shard_map/ppermute | solution.py:334
  27.5 31.9 %all-to-all-start = ((f32[32,40,128]{2,1,0:T(8,128)}), f32[32,40,128]{2,1,0:T(8,128)S(1)}, u32[]{:S(2)}, u32[]{:S(2)}) async-start(f32[32,40,128]{2,1,0:T(8,128)} %bitcast.4), calls=%async_computation | async-start | bytes 1310720 | tf_op jit(solution)/shard_map/all_to_all | solution.py:321
  38.7 28.3 %collective-permute-start.6 = (f32[5,256,128]{2,1,0:T(8,128)}, f32[5,256,128]{2,1,0:T(8,128)S(1)}, u32[]{:S(2)}, u32[]{:S(2)}) collective-permute-start(f32[5,256,128]{2,1,0:T(8,128)} %get-tuple-element.41), channel_id=1, source_target_pairs={{0,3},{1,0},{2,1},{3,2},{4,7},{5,4},{6,5},{7,6},{8,11},{9,8},{10,9... | collective-permute-start | bytes 1966088 | tf_op jit(solution)/shard_map/ppermute | solution.py:335
  40.6 26.5 %collective-permute-start.7 = (f32[5,256,128]{2,1,0:T(8,128)}, f32[5,256,128]{2,1,0:T(8,128)S(1)}, u32[]{:S(2)}, u32[]{:S(2)}) collective-permute-start(f32[5,256,128]{2,1,0:T(8,128)} %copy-done.4), channel_id=1, source_target_pairs={{0,1},{1,2},{2,3},{3,0},{4,5},{5,6},{6,7},{7,4},{8,9},{9,10},{10,1... | collective-permute-start | bytes 1966088 | tf_op jit(solution)/shard_map/ppermute | solution.py:336
  40.8 1.1 %copy-start.8 = (f32[5,256,128]{2,1,0:T(8,128)S(1)}, f32[5,256,128]{2,1,0:T(8,128)}, u32[]{:S(2)}) copy-start(f32[5,256,128]{2,1,0:T(8,128)} %copy-done.7) | copy-start | bytes 1966084
  41.9 1.1 %copy-start.10 = (f32[5,256,128]{2,1,0:T(8,128)S(1)}, f32[5,256,128]{2,1,0:T(8,128)}, u32[]{:S(2)}) copy-start(f32[5,256,128]{2,1,0:T(8,128)} %copy-done.9) | copy-start | bytes 1966084
  43.0 28.6 %copy-start.1 = (s32[10]{0:T(128)S(1)}, s32[10]{0:T(128)}, u32[]{:S(2)}) copy-start(s32[10]{0:T(128)} %owner.1) | copy-start | bytes 124
  44.5 0.8 copy-start.5
  45.4 0.8 copy-start.6
  59.7 3.9 %collective-permute-start.5 = (f32[5,8,128]{2,1,0:T(8,128)S(1)}, f32[5,8,128]{2,1,0:T(8,128)S(1)}, u32[]{:S(2)}, u32[]{:S(2)}) collective-permute-start(f32[5,8,128]{2,1,0:T(8,128)S(1)} %slice_sum.1), channel_id=1, source_target_pairs={{0,3},{1,0},{2,1},{3,2},{4,7},{5,4},{6,5},{7,6},{8,11},{9,8},{10,9... | collective-permute-start | bytes 61448 | tf_op jit(solution)/shard_map/ppermute | solution.py:342
  61.2 5.0 %collective-permute-start.4 = (f32[5,8,128]{2,1,0:T(8,128)S(1)}, f32[5,8,128]{2,1,0:T(8,128)S(1)}, u32[]{:S(2)}, u32[]{:S(2)}) collective-permute-start(f32[5,8,128]{2,1,0:T(8,128)S(1)} %slice_sum.1), channel_id=1, source_target_pairs={{0,1},{1,2},{2,3},{3,0},{4,5},{5,6},{6,7},{7,4},{8,9},{9,10},{10,1... | collective-permute-start | bytes 61448 | tf_op jit(solution)/shard_map/ppermute | solution.py:342
  61.8 5.3 %collective-permute-start.3 = (f32[5,8,128]{2,1,0:T(8,128)S(1)}, f32[5,8,128]{2,1,0:T(8,128)S(1)}, u32[]{:S(2)}, u32[]{:S(2)}) collective-permute-start(f32[5,8,128]{2,1,0:T(8,128)S(1)} %slice_sum.1), channel_id=1, source_target_pairs={{0,2},{1,3},{2,0},{3,1},{4,6},{5,7},{6,4},{7,5},{8,10},{9,11},{10,... | collective-permute-start | bytes 61448 | tf_op jit(solution)/shard_map/ppermute | solution.py:342
  67.1 14.7 %collective-permute-start.8 = (f32[5,256,128]{2,1,0:T(8,128)}, f32[5,256,128]{2,1,0:T(8,128)}, u32[]{:S(2)}, u32[]{:S(2)}) collective-permute-start(f32[5,256,128]{2,1,0:T(8,128)} %copy-done.6), channel_id=1, source_target_pairs={{0,1},{1,2},{2,3},{3,0},{4,5},{5,6},{6,7},{7,4},{8,9},{9,10},{10,1... | collective-permute-start | bytes 1966088 | tf_op jit(solution)/shard_map/ppermute | solution.py:345
  67.2 14.6 %collective-permute-start.9 = (f32[5,256,128]{2,1,0:T(8,128)}, f32[5,256,128]{2,1,0:T(8,128)}, u32[]{:S(2)}, u32[]{:S(2)}) collective-permute-start(f32[5,256,128]{2,1,0:T(8,128)} %copy-done.5), channel_id=1, source_target_pairs={{0,3},{1,0},{2,1},{3,2},{4,7},{5,4},{6,5},{7,6},{8,11},{9,8},{10,9... | collective-permute-start | bytes 1966088 | tf_op jit(solution)/shard_map/ppermute | solution.py:346
  70.4 1.2 %collective-permute-start.10 = (f32[5,8,128]{2,1,0:T(8,128)S(1)}, f32[5,8,128]{2,1,0:T(8,128)S(1)}, u32[]{:S(2)}, u32[]{:S(2)}) collective-permute-start(f32[5,8,128]{2,1,0:T(8,128)S(1)} %add_add_fusion.own), channel_id=1, source_target_pairs={{0,4},{4,0},{1,5},{5,1},{2,6},{6,2},{3,7},{7,3},{8,12},{12,8},{9,1... | collective-permute-start | bytes 61448 | tf_op jit(solution)/shard_map/ppermute | solution.py:347
  73.0 20.3 %all-to-all-start.1 = ((f32[32,24,128]{2,1,0:T(8,128)}), f32[32,24,128]{2,1,0:T(8,128)S(1)}, u32[]{:S(2)}, u32[]{:S(2)}) async-start(f32[32,24,128]{2,1,0:T(8,128)} %bitcast.6), calls=%async_computation.1 | async-start | bytes 786432 | tf_op jit(solution)/shard_map/all_to_all | solution.py:321

commit v6 on v5

--- a/solution.py
+++ b/solution.py
@@ -89,10 +89,10 @@
             turn_high[b], turn_low[b] = split(identity + 2.0 * a + 2.0 * square + cube)
     get_cot.wait()
     cot[...] = cots[...].T
-    for b0 in range(0, 10, 5):
-        for t in range(2 * b0, 2 * b0 + 10):
+    for b0 in range(0, 10, 2):
+        for t in range(2 * b0, 2 * b0 + 4):
             fetch(t).wait()
-        for b in range(b0, b0 + 5):
+        for b in range(b0, b0 + 2):
             high[b], low[b] = split(dot(cot[...], tiles[b]))
     for t in range(20):
         fetch_inputs(t).wait()

time: 95.5 us -> 95.1 us (level)
  no operation moved by 1% of the time
where the time goes in v6:
time: 95.1 us; the launch traced here: 94.7 us
  waiting for transfers between devices  31 us (33%)
  starting transfers between devices  28.7 us (30%)
  Pallas kernels  26.8 us (28%)
  local copies, waits for them, and re-layouts  7.3 us (8%)
    all_to_all x2, waiting for transfers between devices, exchange(): lax.all_to_all(rows, ('x', 'z'), 0, 0, tiled=True).reshape(parts.shape)  22.4 us
    all_to_all x2, starting transfers between devices, exchange(): lax.all_to_all(rows, ('x', 'z'), 0, 0, tiled=True).reshape(parts.shape)  16.2 us
    pallas_call x1, Pallas kernels, grad_call(): pl.pallas_call(grad_kernel, out_shape=[turns, turns, part, part, gram, gr...  11.7 us
    unnamed x22, local copies, waits for them, and re-layouts  7.3 us
    pallas_call x1, Pallas kernels, rotate_call(): pl.pallas_call(rotate_kernel, out_shape=[half] * 6 + [jax.ShapeDtypeStruc...  4.5 us
    ppermute x1, waiting for transfers between devices, local(): next_a = lax.ppermute(next_a, 'y', turn(Y, 1))  3.75 us
    ppermute x3, starting transfers between devices, local(): others = [lax.ppermute(slices, 'y', turn(Y, s)) for s in (1, 2, 3)]  3.69 us
    ppermute x3, waiting for transfers between devices, local(): others = [lax.ppermute(slices, 'y', turn(Y, s)) for s in (1, 2, 3)]  3.69 us
  transfers between devices with their start and end apart: 13, of which 7 were waited for; matrix products, arithmetic and copies ran while one was open for 0% of the time, Pallas kernels for 14%

profile of v6, /device:TPU:32, one launch (start us, length us, event | category | flops | bytes accessed | tf_op | source)
XLA Modules:
  0.0 94.7 jit_solution(9761662135775530414)
XLA Ops:
  0.6 0.1 pad_add_fusion.place
  0.7 0.0 copy-start
  0.7 0.7 copy-done
  1.4 0.0 copy-start.2
  1.4 1.5 %copy-done.2 = bf16[512,1728]{0,1:T(8,128)(2,1)S(1)} copy-done((bf16[512,1728]{0,1:T(8,128)(2,1)S(1)}, bf16[512,1728]{0,1:T(8,128)(2,1)}, u32[]{:S(2)}) %copy-start.2) | copy-done | bytes 1769496
  2.8 0.0 copy-start.3
  2.8 1.3 %copy-done.3 = bf16[10,256,256]{2,1,0:T(8,128)(2,1)S(1)} copy-done((bf16[10,256,256]{2,1,0:T(8,128)(2,1)S(1)}, bf16[10,256,256]{2,1,0:T(8,128)(2,1)}, u32[]{:S(2)}) %copy-start.3) | copy-done | bytes 1310744
  4.2 11.7 %grad.1 = (bf16[10,256,256]{2,1,0:T(8,128)(2,1)S(1)}, bf16[10,256,256]{2,1,0:T(8,128)(2,1)S(1)}, bf16[10,512,256]{2,1,0:T(8,128)(2,1)S(1)}, bf16[10,512,256]{2,1...) custom-call(s32[20]{0:T(128)S(1)} %copy-done, s32[2]{0:T(128)S(1)} %pad_add_fusion.place, ...), custom_call_target="tpu_custom_call" | custom-call | flops 8000000000 | bytes 14000000 | tf_op jit(solution)/shard_map/grad/pallas_call | solution.py:123
  15.9 0.1 collective-permute-start
  16.0 4.5 %rotate.1 = (f32[5,256,128]{2,1,0:T(8,128)}, f32[5,256,128]{2,1,0:T(8,128)}, f32[5,256,128]{2,1,0:T(8,128)S(1)}, f32[5,256,128]{2,1,0:T(8,128)S(1)}, f32[5,256,1...) custom-call(s32[20]{0:T(128)S(1)} %copy-done, s32[2]{0:T(128)S(1)} %pad_add_fusion.place, ...), custom_call_target="tpu_custom_call" | custom-call | flops 2000000000 | bytes 10000000 | tf_op jit(solution)/shard_map/rotate/pallas_call | solution.py:162
  20.5 0.0 copy-start.4
  20.5 0.0 copy-start.7
  20.5 0.0 copy-start.9
  20.5 1.6 %collective-permute-start.1 = (f32[5,256,128]{2,1,0:T(8,128)}, f32[5,256,128]{2,1,0:T(8,128)}, u32[]{:S(2)}, u32[]{:S(2)}) collective-permute-start(f32[5,256,128]{2,1,0:T(8,128)} %get-tuple-element.33), channel_id=1, source_target_pairs={{0,1},{1,2},{2,3},{3,0},{4,5},{5,6},{6,7},{7,4},{8,9},{9,10},{10,1... | collective-permute-start | bytes 1966088 | tf_op jit(solution)/shard_map/ppermute | solution.py:333
  22.1 1.7 %collective-permute-start.2 = (f32[5,256,128]{2,1,0:T(8,128)}, f32[5,256,128]{2,1,0:T(8,128)}, u32[]{:S(2)}, u32[]{:S(2)}) collective-permute-start(f32[5,256,128]{2,1,0:T(8,128)} %get-tuple-element.35), channel_id=1, source_target_pairs={{0,3},{1,0},{2,1},{3,2},{4,7},{5,4},{6,5},{7,6},{8,11},{9,8},{10,9... | collective-permute-start | bytes 1966088 | tf_op jit(solution)/shard_map/ppermute | solution.py:334
  23.8 0.0 collective-permute-done.came
  23.8 3.3 %adjoint.1 = f32[32,5,8,128]{3,2,1,0:T(8,128)} custom-call(s32[2]{0:T(128)S(1)} %pad_add_fusion.place, f32[5,256,256]{2,1,0:T(8,128)S(1)} %get-tuple-element.30.mine, f32[5,256,256]{2,1,0:T(8,128)S(1)} %collective-permute-done.came, bf16[10,256,256]{2,1,0:T(8,128)(2,1)S(1)} %copy-done.3), custom_call_target="tpu_custom_call" | custom-call | flops 2000000000 | bytes 4000000 | tf_op jit(solution)/shard_map/adjoint/pallas_call | solution.py:194
  27.1 0.0 copy-done.4
  27.1 0.0 copy-done.7
  27.1 0.0 copy-done.9
  27.1 11.2 %all-to-all-start = ((f32[32,40,128]{2,1,0:T(8,128)}), f32[32,40,128]{2,1,0:T(8,128)S(1)}, u32[]{:S(2)}, u32[]{:S(2)}) async-start(f32[32,40,128]{2,1,0:T(8,128)} %bitcast.4), calls=%async_computation | async-start | bytes 1310720 | tf_op jit(solution)/shard_map/all_to_all | solution.py:321
  38.3 1.8 %collective-permute-start.6 = (f32[5,256,128]{2,1,0:T(8,128)}, f32[5,256,128]{2,1,0:T(8,128)S(1)}, u32[]{:S(2)}, u32[]{:S(2)}) collective-permute-start(f32[5,256,128]{2,1,0:T(8,128)} %get-tuple-element.41), channel_id=1, source_target_pairs={{0,3},{1,0},{2,1},{3,2},{4,7},{5,4},{6,5},{7,6},{8,11},{9,8},{10,9... | collective-permute-start | bytes 1966088 | tf_op jit(solution)/shard_map/ppermute | solution.py:335
  40.1 0.3 collective-permute-start.7
  40.4 0.0 collective-permute-done.1.far_a
  40.4 0.0 collective-permute-done.2.far_b
  40.4 0.0 copy-start.8
  40.4 1.1 %copy-done.8 = f32[5,256,128]{2,1,0:T(8,128)S(1)} copy-done((f32[5,256,128]{2,1,0:T(8,128)S(1)}, f32[5,256,128]{2,1,0:T(8,128)}, u32[]{:S(2)}) %copy-start.8) | copy-done | bytes 655384
  41.5 0.0 copy-start.10
  41.5 1.1 %copy-done.10 = f32[5,256,128]{2,1,0:T(8,128)S(1)} copy-done((f32[5,256,128]{2,1,0:T(8,128)S(1)}, f32[5,256,128]{2,1,0:T(8,128)}, u32[]{:S(2)}) %copy-start.10) | copy-done | bytes 655384
  42.6 0.0 copy-start.1
  42.6 1.5 %merge.1 = (f32[5,256,128]{2,1,0:T(8,128)S(1)}, f32[5,256,128]{2,1,0:T(8,128)S(1)}) custom-call(f32[5,256,128]{2,1,0:T(8,128)S(1)} %copy-done.8, f32[5,256,128]{2,1,0:T(8,128)} %collective-permute-done.1.far_a, f32[5,256,128]{2,1,0:T(8,128)S(1)} %copy-done.10, f32[5,256,128]{2,1,0:T(8,128)} %collective-permute-done.2.far_b), custom_call_target="tpu_custom_call" | custom-call | flops 10000000000 | bytes 4000000 | tf_op jit(solution)/shard_map/merge/pallas_call | solution.py:211
  44.1 0.0 copy-start.5
  44.1 0.8 copy-done.5
  45.0 0.0 copy-start.6
  45.0 0.8 copy-done.6
  45.8 13.2 %all-to-all-done = f32[32,40,128]{2,1,0:T(8,128)S(1)} async-done(((f32[32,40,128]{2,1,0:T(8,128)}), f32[32,40,128]{2,1,0:T(8,128)S(1)}, u32[]{:S(2)}, u32[]{:S(2)}) %all-to-all-start) | async-done | bytes 655392 | tf_op jit(solution)/shard_map/all_to_all | solution.py:321
  59.0 0.2 slice_sum.1
  59.3 1.5 %collective-permute-start.5 = (f32[5,8,128]{2,1,0:T(8,128)S(1)}, f32[5,8,128]{2,1,0:T(8,128)S(1)}, u32[]{:S(2)}, u32[]{:S(2)}) collective-permute-start(f32[5,8,128]{2,1,0:T(8,128)S(1)} %slice_sum.1), channel_id=1, source_target_pairs={{0,3},{1,0},{2,1},{3,2},{4,7},{5,4},{6,5},{7,6},{8,11},{9,8},{10,9... | collective-permute-start | bytes 61448 | tf_op jit(solution)/shard_map/ppermute | solution.py:342
  60.7 0.6 collective-permute-start.4
  61.4 1.6 %collective-permute-start.3 = (f32[5,8,128]{2,1,0:T(8,128)S(1)}, f32[5,8,128]{2,1,0:T(8,128)S(1)}, u32[]{:S(2)}, u32[]{:S(2)}) collective-permute-start(f32[5,8,128]{2,1,0:T(8,128)S(1)} %slice_sum.1), channel_id=1, source_target_pairs={{0,2},{1,3},{2,0},{3,1},{4,6},{5,7},{6,4},{7,5},{8,10},{9,11},{10,... | collective-permute-start | bytes 61448 | tf_op jit(solution)/shard_map/ppermute | solution.py:342
  62.9 0.2 collective-permute-done.5
  63.1 2.6 %collective-permute-done.4 = f32[5,8,128]{2,1,0:T(8,128)S(1)} collective-permute-done((f32[5,8,128]{2,1,0:T(8,128)S(1)}, f32[5,8,128]{2,1,0:T(8,128)S(1)}, u32[]{:S(2)}, u32[]{:S(2)}) %collective-permute-start.4) | collective-permute-done | bytes 20512 | tf_op jit(solution)/shard_map/ppermute | solution.py:342
  65.7 0.9 collective-permute-done.3
  66.7 0.0 collective-permute-done.6.a2
  66.7 0.0 collective-permute-done.7.b1
  66.7 0.1 collective-permute-start.8
  66.8 3.2 %collective-permute-start.9 = (f32[5,256,128]{2,1,0:T(8,128)}, f32[5,256,128]{2,1,0:T(8,128)}, u32[]{:S(2)}, u32[]{:S(2)}) collective-permute-start(f32[5,256,128]{2,1,0:T(8,128)} %copy-done.5), channel_id=1, source_target_pairs={{0,3},{1,0},{2,1},{3,2},{4,7},{5,4},{6,5},{7,6},{8,11},{9,8},{10,9... | collective-permute-start | bytes 1966088 | tf_op jit(solution)/shard_map/ppermute | solution.py:346
  70.0 0.0 collective-permute-start.10
  70.0 1.2 %collective-permute-done.10.other = f32[5,8,128]{2,1,0:T(8,128)S(1)} collective-permute-done((f32[5,8,128]{2,1,0:T(8,128)S(1)}, f32[5,8,128]{2,1,0:T(8,128)S(1)}, u32[]{:S(2)}, u32[]{:S(2)}) %collective-permute-start.10) | collective-permute-done | bytes 20512 | tf_op jit(solution)/shard_map/ppermute | solution.py:347
  71.2 0.0 copy-done.1
  71.2 1.5 %route.1 = f32[32,3,8,128]{3,2,1,0:T(8,128)} custom-call(s32[10]{0:T(128)S(1)} %copy-done.1, s32[2]{0:T(128)S(1)} %pad_add_fusion.place, f32[5,8,128]{2,1,0:T(8,128)S(1)} %add_add_fusion.own, f32[5,8,128]{2,1,0:T(8,128)S(1)} %collective-permute-done.10.other), custom_call_target="tpu_custom_call" | custom-call | flops 100000 | bytes 1000000 | tf_op jit(solution)/shard_map/route/pallas_call | solution.py:259
  72.6 5.0 %all-to-all-start.1 = ((f32[32,24,128]{2,1,0:T(8,128)}), f32[32,24,128]{2,1,0:T(8,128)S(1)}, u32[]{:S(2)}, u32[]{:S(2)}) async-start(f32[32,24,128]{2,1,0:T(8,128)} %bitcast.6), calls=%async_computation.1 | async-start | bytes 786432 | tf_op jit(solution)/shard_map/all_to_all | solution.py:321
  77.6 3.7 %collective-permute-done.8.a1 = f32[5,256,128]{2,1,0:T(8,128)} collective-permute-done((f32[5,256,128]{2,1,0:T(8,128)}, f32[5,256,128]{2,1,0:T(8,128)}, u32[]{:S(2)}, u32[]{:S(2)}) %collective-permute-start.8) | collective-permute-done | bytes 655392 | tf_op jit(solution)/shard_map/ppermute | solution.py:345
  81.4 0.0 collective-permute-done.9.b2
  81.4 2.4 %finish.1 = bf16[512,640]{1,0:T(8,128)(2,1)} custom-call(f32[5,512,128]{2,1,0:T(8,128)S(1)} %get-tuple-element.29.own, f32[5,256,128]{2,1,0:T(8,128)} %collective-permute-done.8.a1, f32[5,256,128]{2,1,0:T(8,128)S(1)} %collective-permute-done.6.a2, f32[5,256,128]{2,1,0:T(8,128)S(1)} %collective-permute-done.7.b1, f32[5,256,128]{2,1,0:T(8,128)} %collective-permute-done.9.b2), custom_call_target="tpu_custom_call" | custom-call | flops 10000000000 | bytes 5000000 | tf_op jit(solution)/shard_map/finish/pallas_call | solution.py:305
  83.8 9.2 %all-to-all-done.1 = f32[32,24,128]{2,1,0:T(8,128)S(1)} async-done(((f32[32,24,128]{2,1,0:T(8,128)}), f32[32,24,128]{2,1,0:T(8,128)S(1)}, u32[]{:S(2)}, u32[]{:S(2)}) %all-to-all-start.1) | async-done | bytes 393248 | tf_op jit(solution)/shard_map/all_to_all | solution.py:321
  92.9 1.7 %unpack.1 = f32[3,256,256]{2,1,0:T(8,128)} custom-call(f32[32,3,8,128]{3,2,1,0:T(8,128)S(1)} %bitcast.9), custom_call_target="tpu_custom_call" | custom-call | flops 1000000 | bytes 1000000 | tf_op jit(solution)/shard_map/unpack/pallas_call | solution.py:284
  (1 shorter events, 0.0 us)
Async XLA Ops:
  0.7 0.7 copy-start
  1.4 1.5 %copy-start.2 = (bf16[512,1728]{0,1:T(8,128)(2,1)S(1)}, bf16[512,1728]{0,1:T(8,128)(2,1)}, u32[]{:S(2)}) copy-start(bf16[512,1728]{0,1:T(8,128)(2,1)} %param.7) | copy-start | bytes 5308420
  2.8 1.3 %copy-start.3 = (bf16[10,256,256]{2,1,0:T(8,128)(2,1)S(1)}, bf16[10,256,256]{2,1,0:T(8,128)(2,1)}, u32[]{:S(2)}) copy-start(bf16[10,256,256]{2,1,0:T(8,128)(2,1)} %skew.3) | copy-start | bytes 3932164
  15.9 8.0 %collective-permute-start = (f32[5,256,256]{2,1,0:T(8,128)S(1)}, f32[5,256,256]{2,1,0:T(8,128)S(1)}, u32[]{:S(2)}, u32[]{:S(2)}) collective-permute-start(f32[5,256,256]{2,1,0:T(8,128)S(1)} %get-tuple-element.31), channel_id=1, source_target_pairs={{0,4},{4,0},{1,5},{5,1},{2,6},{6,2},{3,7},{7,3},{8,12},{12,8},{9,1... | collective-permute-start | bytes 3932168 | tf_op jit(solution)/shard_map/ppermute | solution.py:329
  20.5 6.6 %copy-start.4 = (f32[5,256,128]{2,1,0:T(8,128)}, f32[5,256,128]{2,1,0:T(8,128)S(1)}, u32[]{:S(2)}) copy-start(f32[5,256,128]{2,1,0:T(8,128)S(1)} %get-tuple-element.42) | copy-start | bytes 1966084
  20.5 6.6 %copy-start.7 = (f32[5,256,128]{2,1,0:T(8,128)}, f32[5,256,128]{2,1,0:T(8,128)S(1)}, u32[]{:S(2)}) copy-start(f32[5,256,128]{2,1,0:T(8,128)S(1)} %get-tuple-element.32.next_a) | copy-start | bytes 1966084
  20.5 6.6 %copy-start.9 = (f32[5,256,128]{2,1,0:T(8,128)}, f32[5,256,128]{2,1,0:T(8,128)S(1)}, u32[]{:S(2)}) copy-start(f32[5,256,128]{2,1,0:T(8,128)S(1)} %get-tuple-element.34.last_b) | copy-start | bytes 1966084
  20.5 20.0 %collective-permute-start.1 = (f32[5,256,128]{2,1,0:T(8,128)}, f32[5,256,128]{2,1,0:T(8,128)}, u32[]{:S(2)}, u32[]{:S(2)}) collective-permute-start(f32[5,256,128]{2,1,0:T(8,128)} %get-tuple-element.33), channel_id=1, source_target_pairs={{0,1},{1,2},{2,3},{3,0},{4,5},{5,6},{6,7},{7,4},{8,9},{9,10},{10,1... | collective-permute-start | bytes 1966088 | tf_op jit(solution)/shard_map/ppermute | solution.py:333
  22.1 18.3 %collective-permute-start.2 = (f32[5,256,128]{2,1,0:T(8,128)}, f32[5,256,128]{2,1,0:T(8,128)}, u32[]{:S(2)}, u32[]{:S(2)}) collective-permute-start(f32[5,256,128]{2,1,0:T(8,128)} %get-tuple-element.35), channel_id=1, source_target_pairs={{0,3},{1,0},{2,1},{3,2},{4,7},{5,4},{6,5},{7,6},{8,11},{9,8},{10,9... | collective-permute-start | bytes 1966088 | tf_op jit(solution)/shard_map/ppermute | solution.py:334
  27.1 31.9 %all-to-all-start = ((f32[32,40,128]{2,1,0:T(8,128)}), f32[32,40,128]{2,1,0:T(8,128)S(1)}, u32[]{:S(2)}, u32[]{:S(2)}) async-start(f32[32,40,128]{2,1,0:T(8,128)} %bitcast.4), calls=%async_computation | async-start | bytes 1310720 | tf_op jit(solution)/shard_map/all_to_all | solution.py:321
  38.3 28.3 %collective-permute-start.6 = (f32[5,256,128]{2,1,0:T(8,128)}, f32[5,256,128]{2,1,0:T(8,128)S(1)}, u32[]{:S(2)}, u32[]{:S(2)}) collective-permute-start(f32[5,256,128]{2,1,0:T(8,128)} %get-tuple-element.41), channel_id=1, source_target_pairs={{0,3},{1,0},{2,1},{3,2},{4,7},{5,4},{6,5},{7,6},{8,11},{9,8},{10,9... | collective-permute-start | bytes 1966088 | tf_op jit(solution)/shard_map/ppermute | solution.py:335
  40.1 26.5 %collective-permute-start.7 = (f32[5,256,128]{2,1,0:T(8,128)}, f32[5,256,128]{2,1,0:T(8,128)S(1)}, u32[]{:S(2)}, u32[]{:S(2)}) collective-permute-start(f32[5,256,128]{2,1,0:T(8,128)} %copy-done.4), channel_id=1, source_target_pairs={{0,1},{1,2},{2,3},{3,0},{4,5},{5,6},{6,7},{7,4},{8,9},{9,10},{10,1... | collective-permute-start | bytes 1966088 | tf_op jit(solution)/shard_map/ppermute | solution.py:336
  40.4 1.1 %copy-start.8 = (f32[5,256,128]{2,1,0:T(8,128)S(1)}, f32[5,256,128]{2,1,0:T(8,128)}, u32[]{:S(2)}) copy-start(f32[5,256,128]{2,1,0:T(8,128)} %copy-done.7) | copy-start | bytes 1966084
  41.5 1.1 %copy-start.10 = (f32[5,256,128]{2,1,0:T(8,128)S(1)}, f32[5,256,128]{2,1,0:T(8,128)}, u32[]{:S(2)}) copy-start(f32[5,256,128]{2,1,0:T(8,128)} %copy-done.9) | copy-start | bytes 1966084
  42.6 28.6 %copy-start.1 = (s32[10]{0:T(128)S(1)}, s32[10]{0:T(128)}, u32[]{:S(2)}) copy-start(s32[10]{0:T(128)} %owner.1) | copy-start | bytes 124
  44.1 0.8 copy-start.5
  45.0 0.8 copy-start.6
  59.3 3.9 %collective-permute-start.5 = (f32[5,8,128]{2,1,0:T(8,128)S(1)}, f32[5,8,128]{2,1,0:T(8,128)S(1)}, u32[]{:S(2)}, u32[]{:S(2)}) collective-permute-start(f32[5,8,128]{2,1,0:T(8,128)S(1)} %slice_sum.1), channel_id=1, source_target_pairs={{0,3},{1,0},{2,1},{3,2},{4,7},{5,4},{6,5},{7,6},{8,11},{9,8},{10,9... | collective-permute-start | bytes 61448 | tf_op jit(solution)/shard_map/ppermute | solution.py:342
  60.7 5.0 %collective-permute-start.4 = (f32[5,8,128]{2,1,0:T(8,128)S(1)}, f32[5,8,128]{2,1,0:T(8,128)S(1)}, u32[]{:S(2)}, u32[]{:S(2)}) collective-permute-start(f32[5,8,128]{2,1,0:T(8,128)S(1)} %slice_sum.1), channel_id=1, source_target_pairs={{0,1},{1,2},{2,3},{3,0},{4,5},{5,6},{6,7},{7,4},{8,9},{9,10},{10,1... | collective-permute-start | bytes 61448 | tf_op jit(solution)/shard_map/ppermute | solution.py:342
  61.4 5.3 %collective-permute-start.3 = (f32[5,8,128]{2,1,0:T(8,128)S(1)}, f32[5,8,128]{2,1,0:T(8,128)S(1)}, u32[]{:S(2)}, u32[]{:S(2)}) collective-permute-start(f32[5,8,128]{2,1,0:T(8,128)S(1)} %slice_sum.1), channel_id=1, source_target_pairs={{0,2},{1,3},{2,0},{3,1},{4,6},{5,7},{6,4},{7,5},{8,10},{9,11},{10,... | collective-permute-start | bytes 61448 | tf_op jit(solution)/shard_map/ppermute | solution.py:342
  66.7 14.7 %collective-permute-start.8 = (f32[5,256,128]{2,1,0:T(8,128)}, f32[5,256,128]{2,1,0:T(8,128)}, u32[]{:S(2)}, u32[]{:S(2)}) collective-permute-start(f32[5,256,128]{2,1,0:T(8,128)} %copy-done.6), channel_id=1, source_target_pairs={{0,1},{1,2},{2,3},{3,0},{4,5},{5,6},{6,7},{7,4},{8,9},{9,10},{10,1... | collective-permute-start | bytes 1966088 | tf_op jit(solution)/shard_map/ppermute | solution.py:345
  66.8 14.6 %collective-permute-start.9 = (f32[5,256,128]{2,1,0:T(8,128)}, f32[5,256,128]{2,1,0:T(8,128)}, u32[]{:S(2)}, u32[]{:S(2)}) collective-permute-start(f32[5,256,128]{2,1,0:T(8,128)} %copy-done.5), channel_id=1, source_target_pairs={{0,3},{1,0},{2,1},{3,2},{4,7},{5,4},{6,5},{7,6},{8,11},{9,8},{10,9... | collective-permute-start | bytes 1966088 | tf_op jit(solution)/shard_map/ppermute | solution.py:346
  70.0 1.2 %collective-permute-start.10 = (f32[5,8,128]{2,1,0:T(8,128)S(1)}, f32[5,8,128]{2,1,0:T(8,128)S(1)}, u32[]{:S(2)}, u32[]{:S(2)}) collective-permute-start(f32[5,8,128]{2,1,0:T(8,128)S(1)} %add_add_fusion.own), channel_id=1, source_target_pairs={{0,4},{4,0},{1,5},{5,1},{2,6},{6,2},{3,7},{7,3},{8,12},{12,8},{9,1... | collective-permute-start | bytes 61448 | tf_op jit(solution)/shard_map/ppermute | solution.py:347
  72.6 20.3 %all-to-all-start.1 = ((f32[32,24,128]{2,1,0:T(8,128)}), f32[32,24,128]{2,1,0:T(8,128)S(1)}, u32[]{:S(2)}, u32[]{:S(2)}) async-start(f32[32,24,128]{2,1,0:T(8,128)} %bitcast.6), calls=%async_computation.1 | async-start | bytes 786432 | tf_op jit(solution)/shard_map/all_to_all | solution.py:321
